TPU v7x, 256 devices: a whole 4x4x8 slice. The times are simulated.
256 devices in a mesh: sect: 2 (over x_hi), gx: 16 (over x_lo, y, core), gy: 8 (over z).
Axes of the slice: x: 4 (x_hi: 2, x_lo: 2; x = x_hi * 2 + x_lo), y: 4, z: 8, core: 2. Of those that a mesh axis runs over, the one named last changes fastest.
Arguments:
- air_profile_matrix: float32 [1024, 256, 256], P('gx', 'gy'), may hold values from -6 to 6
- spreading_numbers: float32 [256], replicated, may hold values from 0.025 to 0.2
- eastward_advection_number: float32 [256], replicated, may hold values from -0.2 to 0.2
- northward_advection_number: float32 [256], replicated, may hold values from -0.2 to 0.2
- landmass_warmth: float32 [1024, 256], P('gx', 'gy'), may hold values from -6 to 6
- physics_increments: int32 [1024, 64], P(None, 'gy'), may hold values from 1 to 4
- underlying_water_index: int32 [1024, 256], P('gx', 'gy'), may hold values from 0 to 511
- water_indicator: int32 [512, 128], P('gx', 'gy'), may hold values 0 or 1
- waterbody_profiles: float32 [2, 80, 512, 128], P(None, None, 'gx', 'gy'), may hold values from -6 to 6
- waterbody_drivers: float32 [2, 512, 128], P(None, 'gx', 'gy'), may hold values from -6 to 6
- inverted_blending_matrix: float32 [80, 80], replicated, may hold values from 0 to 0.55, as said below
- entry_layer_matrix: bfloat16 [256, 512], replicated, may hold values from -0.375 to 0.375
- entry_layer_offset: float32 [512], replicated, may hold values from -3 to 3
- exit_layer_matrix: bfloat16 [512, 256], replicated, may hold values from -0.25 to 0.25
Outputs:
- coupled: float32 [2, 2, 512, 128], P('sect', None, 'gx', 'gy')
Inputs may be any that keep to these rules, and one draw needn't show every extreme that they name: `underlying_water_index`: a local row-major index into the same device's ocean block. `inverted_blending_matrix`: nonnegative entries; the diagonal is 0.5 or more.
All inputs are finite; a program needn't handle non-finite values. No bound on the sum of `water_indicator` on one device may be relied on, other than what follows from the above.
Results may differ from a plain program's by a relative error of at most 0.0019.
The roundings to bfloat16 on the way count: a program that leaves them out, or rounds other values in their place, can miss the bound.
Values sent between devices are 32-bit elements; how exact they have to be, the bound alone decides.
No kernel may reach another device: no remote copies, remote signals or barrier semaphores. Data moves between devices by JAX's collectives and lax.ppermute only.
A program may use at most 64 MiB of HBM per device.

v0:
```python
import math

import jax
import jax.numpy as jnp
from jax import lax
from jax.sharding import PartitionSpec as P

BS = 4
DSTEPS = 2
OSTEPS = 12


THERMAL_FACTOR = 0.8
WETNESS_FACTOR = 0.6
OCEAN_STEP = 0.1


def shifted(block, axis, distance):
    devices = range(lax.axis_size(axis))
    route = [(i - distance, i) for i in devices if i - distance in devices]
    return lax.ppermute(block, axis, route)


def padded_2(block, sides, width):
    for axis, dim in sides:
        count = lax.axis_size(axis)
        forward = [(i, i + 1) for i in range(count - 1)]
        forward.append((count - 1, 0))
        backward = [(target, source) for source, target in forward]
        low = lax.ppermute(
            lax.slice_in_dim(block, block.shape[dim] - width, None, axis=dim), axis, forward
        )
        high = lax.ppermute(lax.slice_in_dim(block, 0, width, axis=dim), axis, backward)
        block = jnp.concatenate([low, block, high], axis=dim)
    return block


def advance(padded, spreading_numbers, eastward_advection_number, northward_advection_number):
    centre = padded[1:-1, 1:-1]
    plus_x = padded[2:, 1:-1]
    minus_x = padded[:-2, 1:-1]
    plus_y = padded[1:-1, 2:]
    minus_y = padded[1:-1, :-2]
    spread = plus_x + minus_x + plus_y + minus_y - 4.0 * centre
    return (
        centre
        + spreading_numbers * spread
        - 0.5 * eastward_advection_number * (plus_x - minus_x)
        - 0.5 * northward_advection_number * (plus_y - minus_y)
    )


def subcycle(states, counts, entry_layer_matrix, entry_layer_offset, exit_layer_matrix):
    total = states.shape[0]
    tile = math.gcd(total, 256)

    def one_tile(index, result):
        start = (index * tile).astype(jnp.int32)
        block = lax.dynamic_slice_in_dim(result, start, tile, 0)
        needed = lax.dynamic_slice_in_dim(counts, start, tile, 0)

        def one_round(round_index, current):
            hidden = jax.nn.gelu(
                jnp.dot(
                    current.astype(jnp.bfloat16),
                    entry_layer_matrix,
                    preferred_element_type=jnp.float32,
                )
                + entry_layer_offset
            ).astype(jnp.bfloat16)
            stepped = current + jnp.dot(
                hidden, exit_layer_matrix, preferred_element_type=jnp.float32
            )
            return jnp.where((needed > round_index)[:, None], stepped, current)

        block = lax.fori_loop(jnp.int32(0), jnp.max(needed), one_round, block)
        return lax.dynamic_update_slice_in_dim(result, block, start, 0)

    return lax.fori_loop(jnp.int32(0), jnp.int32(total // tile), one_tile, states)


def mix_ocean(initial, forcing, sea_cells, inverted_blending_matrix):

    def one_step(step_index, current):
        forced = current.at[:, 0].add(OCEAN_STEP * forcing)
        mixed_cols = jnp.einsum(
            "lk,fkc->flc", inverted_blending_matrix, forced, precision=lax.Precision.HIGHEST
        )
        return jnp.where(sea_cells, mixed_cols, current)

    return lax.fori_loop(0, OSTEPS, one_step, initial)


def shards(
    air_profile_matrix,
    spreading_numbers,
    eastward_advection_number,
    northward_advection_number,
    landmass_warmth,
    physics_increments,
    underlying_water_index,
    water_indicator,
    waterbody_profiles,
    waterbody_drivers,
    inverted_blending_matrix,
    entry_layer_matrix,
    entry_layer_offset,
    exit_layer_matrix,
):
    rows_x, rows_y, channels = air_profile_matrix.shape
    ocean_x, ocean_y = water_indicator.shape
    ocean_cols = ocean_x * ocean_y
    levels_ocean = waterbody_profiles.shape[1]
    is_ocean = lax.axis_index("sect") == 1
    sea_cells = water_indicator.reshape(-1) == 1

    def run_ocean(operand):
        ocean_end = mix_ocean(
            waterbody_profiles.reshape(2, levels_ocean, ocean_cols),
            waterbody_drivers.reshape(2, ocean_cols),
            sea_cells[None, None, :],
            inverted_blending_matrix,
        )
        return ocean_end[:, 0]

    def skip_ocean(operand):
        return jnp.zeros((2, ocean_cols), jnp.float32)

    boundary_entries = lax.cond(is_ocean, run_ocean, skip_ocean, 0)
    arriving_entries = shifted(boundary_entries[0], "sect", -1)
    atm_field = air_profile_matrix
    for step_index in range(DSTEPS):
        padded = padded_2(atm_field, (("gx", 0), ("gy", 1)), 1)
        atm_field = advance(
            padded, spreading_numbers, eastward_advection_number, northward_advection_number
        )
    half_channel = channels // 2
    block_cols = physics_increments.shape[1]
    column_steps = jnp.broadcast_to(
        physics_increments[:, :, None], (physics_increments.shape[0], block_cols, BS)
    ).reshape(physics_increments.shape[0], block_cols * BS)
    own_start = lax.axis_index("gx") * rows_x
    own_steps = lax.dynamic_slice_in_dim(column_steps, own_start, rows_x, 0)

    def surface_channels(final):
        return jnp.stack([final[:, 0], final[:, half_channel]])

    def run_local(operand):
        return surface_channels(
            subcycle(
                atm_field.reshape(rows_x * rows_y, channels),
                own_steps.reshape(rows_x * rows_y),
                entry_layer_matrix,
                entry_layer_offset,
                exit_layer_matrix,
            )
        )

    def none_local(operand):
        return jnp.zeros((2, rows_x * rows_y), jnp.float32)

    picked = lax.cond(is_ocean, none_local, run_local, 0).reshape(2, rows_x, rows_y)
    bottom_layer = picked[0].reshape(-1)
    wetness_share = picked[1].reshape(-1)
    target_position_table = underlying_water_index.reshape(-1)
    ocean_slots = jnp.arange(ocean_cols, dtype=jnp.int32)
    selector = (target_position_table[:, None] == ocean_slots[None, :]).astype(jnp.float32)
    ocean_table = jnp.stack([arriving_entries, sea_cells.astype(jnp.float32)])
    looked_up = jnp.einsum("kc,rc->kr", ocean_table, selector, precision=lax.Precision.HIGHEST)
    oceanic_top_warmth = looked_up[0]
    oceanic_profile = looked_up[1] > 0.5
    interface_warmth = jnp.where(oceanic_profile, oceanic_top_warmth, landmass_warmth.reshape(-1))
    thermal_transfer = THERMAL_FACTOR * (interface_warmth - bottom_layer)
    evaporation_transfer = WETNESS_FACTOR * (jnp.tanh(interface_warmth) - wetness_share)
    contributions = jnp.stack(
        [thermal_transfer, evaporation_transfer, jnp.ones_like(thermal_transfer)]
    )
    gathered_sums = jnp.einsum(
        "kr,rc->kc", contributions, selector, precision=lax.Precision.HIGHEST
    )
    fluxes = gathered_sums[:2] / jnp.maximum(gathered_sums[2], 1.0)
    coupled = jnp.where(is_ocean, boundary_entries, fluxes)
    return coupled.reshape(1, 2, ocean_x, ocean_y)


def solution(mesh):
    in_specs = (
        P("gx", "gy", None),
        P(),
        P(),
        P(),
        P("gx", "gy"),
        P(None, "gy"),
        P("gx", "gy"),
        P("gx", "gy"),
        P(None, None, "gx", "gy"),
        P(None, "gx", "gy"),
        P(),
        P(),
        P(),
        P(),
    )
    out_specs = P("sect", None, "gx", "gy")
    return jax.shard_map(shards, mesh=mesh, in_specs=in_specs, out_specs=out_specs, check_vma=False)
```

profile of v0, /device:TPU:0, one launch (start us, length us, event | category | flops | bytes accessed | tf_op | source)
XLA Modules:
  0.0 129.6 jit_solution(2877881409601353477)
XLA Ops:
  0.0 0.8 fusion.42
  0.8 3.9 %collective-permute-start.1 = (f32[1,32,256]{2,1,0:T(8,128)S(1)}, f32[1,32,256]{2,1,0:T(8,128)S(1)}, u32[]{:S(2)}, u32[]{:S(2)}) collective-permute-start(f32[1,32,256]{2,1,0:T(8,128)S(1)} %get-tuple-element.401), channel_id=1, source_target_pairs={{8,0},{16,8},{24,16},{32,24},{40,32},{48,40},{56,48},{64,56},{72,6... | collective-permute-start | bytes 98312 | tf_op jit(solution)/shard_map/ppermute | solution.py:33
  4.6 0.8 copy.36
  5.5 1.4 %collective-permute-start = (f32[512]{0:T(512)S(1)}, f32[512]{0:T(512)S(1)}, u32[]{:S(2)}, u32[]{:S(2)}) collective-permute-start(f32[512]{0:T(512)S(1)} %bitcast.41), channel_id=1, source_target_pairs={{128,0},{129,1},{130,2},{131,3},{132,4},{133,5},{134,6},{135,7},{1... | collective-permute-start | bytes 6152 | tf_op jit(solution)/shard_map/ppermute | solution.py:21
  7.2 1.4 %copy-done.1 = f32[66,32,256]{2,1,0:T(8,128)} copy-done((f32[66,32,256]{2,1,0:T(8,128)}, f32[66,32,256]{2,1,0:T(8,128)S(1)}, u32[]{:S(2)}) %copy-start.1) | copy-done | bytes 2162712
  8.7 4.2 %collective-permute-start.3 = (f32[66,1,256]{2,1,0:T(1,128)S(1)}, f32[66,1,256]{2,1,0:T(1,128)S(1)}, u32[]{:S(2)}, u32[]{:S(2)}) collective-permute-start(f32[66,1,256]{2,1,0:T(1,128)S(1)} %get-tuple-element.395), channel_id=1, source_target_pairs={{1,0},{2,1},{3,2},{4,3},{5,4},{6,5},{7,6},{0,7},{9,8},{10,9},{11,1... | collective-permute-start | bytes 202760 | tf_op jit(solution)/shard_map/ppermute | solution.py:33
  13.4 1.4 %collective-permute-done.3 = f32[66,1,256]{2,1,0:T(1,128)S(1)} collective-permute-done((f32[66,1,256]{2,1,0:T(1,128)S(1)}, f32[66,1,256]{2,1,0:T(1,128)S(1)}, u32[]{:S(2)}, u32[]{:S(2)}) %collective-permute-start.3) | collective-permute-done | bytes 67616 | tf_op jit(solution)/shard_map/ppermute | solution.py:33
  14.8 3.6 %collective-permute-done.4 = f32[66,1,256]{2,1,0:T(1,128)S(1)} collective-permute-done((f32[66,1,256]{2,1,0:T(1,128)S(1)}, f32[66,1,256]{2,1,0:T(1,128)S(1)}, u32[]{:S(2)}, u32[]{:S(2)}) %collective-permute-start.4) | collective-permute-done | bytes 67616 | tf_op jit(solution)/shard_map/ppermute | solution.py:30
  18.4 5.3 %multiply_subtract_fusion.1 = f32[64,32,256]{2,1,0:T(8,128)S(1)} fusion(f32[64,32,256]{2,1,0:T(8,128)} %param.26, f32[66,32,256]{2,1,0:T(8,128)} %copy-done.1, f32[66,1,256]{2,1,0:T(1,128)S(1)} %collective-permute-done.4, f32[66,1,256]{2,1,0:T(1,128)S(1)} %collective-permute-done.3, f32[1,32,256]{2,1,0:T(8,128)S(1)} %collective-permute-done.1, ...), kind=kLoop, calls=%fused_computation.46 | loop fusion | flops 8912896 | bytes 6560768 | tf_op jit(solution)/shard_map/sub | solution.py:46
  23.7 2.2 %collective-permute-start.5 = (f32[1,32,256]{2,1,0:T(8,128)S(1)}, f32[1,32,256]{2,1,0:T(8,128)S(1)}, u32[]{:S(2)}, u32[]{:S(2)}) collective-permute-start(f32[1,32,256]{2,1,0:T(8,128)S(1)} %get-tuple-element.400), channel_id=1, source_target_pairs={{8,0},{16,8},{24,16},{32,24},{40,32},{48,40},{56,48},{64,56},{72,6... | collective-permute-start | bytes 98312 | tf_op jit(solution)/shard_map/ppermute | solution.py:33
  25.9 7.1 %collective-permute-done = f32[512]{0:T(512)S(1)} collective-permute-done((f32[512]{0:T(512)S(1)}, f32[512]{0:T(512)S(1)}, u32[]{:S(2)}, u32[]{:S(2)}) %collective-permute-start) | collective-permute-done | bytes 2080 | tf_op jit(solution)/shard_map/ppermute | solution.py:21
  33.0 2.2 %fusion.23 = f32[2,2048]{1,0:T(2,128)S(1)} fusion(s32[2048]{0:T(1024)S(1)} %eq.39, f32[1,512]{1,0:T(1,128)S(1)} %reshape.110, f32[1,512]{1,0:T(1,128)S(1)} %bitcast.42), kind=kOutput, calls=%fused_computation.37 | convolution fusion | flops 26215424 | bytes 28672 | tf_op jit(solution)/shard_map/kc,rc->kr/dot_general | solution.py:169
  35.3 5.9 %collective-permute-start.7 = (f32[66,1,256]{2,1,0:T(1,128)S(1)}, f32[66,1,256]{2,1,0:T(1,128)S(1)}, u32[]{:S(2)}, u32[]{:S(2)}) collective-permute-start(f32[66,1,256]{2,1,0:T(1,128)S(1)} %get-tuple-element.394), channel_id=1, source_target_pairs={{1,0},{2,1},{3,2},{4,3},{5,4},{6,5},{7,6},{0,7},{9,8},{10,9},{11,1... | collective-permute-start | bytes 202760 | tf_op jit(solution)/shard_map/ppermute | solution.py:33
  41.2 2.6 %pad_maximum_fusion.3 = (f32[65,32,256]{2,1,0:T(8,128)}, f32[65,32,256]{2,1,0:T(8,128)}) fusion(f32[64,32,256]{2,1,0:T(8,128)S(1)} %multiply_subtract_fusion.1, f32[1,32,256]{2,1,0:T(8,128)S(1)} %collective-permute-done.6, f32[1,32,256]{2,1,0:T(8,128)S(1)} %collective-permute-done.5), kind=kLoop, calls=%fused_computation.41 | loop fusion | flops 1064960 | bytes 6422528 | tf_op jit(solution)/shard_map/concatenate | solution.py:34
  43.8 2.9 %collective-permute-done.8 = f32[66,1,256]{2,1,0:T(1,128)S(1)} collective-permute-done((f32[66,1,256]{2,1,0:T(1,128)S(1)}, f32[66,1,256]{2,1,0:T(1,128)S(1)}, u32[]{:S(2)}, u32[]{:S(2)}) %collective-permute-start.8) | collective-permute-done | bytes 67616 | tf_op jit(solution)/shard_map/ppermute | solution.py:30
  46.7 2.9 %maximum_maximum_fusion = (f32[66,33,256]{2,1,0:T(8,128)}, f32[66,33,256]{2,1,0:T(8,128)}) fusion(f32[1,32,256]{2,1,0:T(8,128)S(1)} %collective-permute-done.5, f32[64,32,256]{2,1,0:T(8,128)S(1)} %multiply_subtract_fusion.1, f32[1,32,256]{2,1,0:T(8,128)S(1)} %collective-permute-done.6, f32[66,1,256]{2,1,0:T(1,128)S(1)} %collective-permute-done.8, ...), kind=kLoop, calls=%fused_computation.39 | loop fusion | flops 3345408 | bytes 6758400 | tf_op jit(solution)/shard_map/concatenate | solution.py:34
  49.6 1.6 %mul.120 = f32[64,32,256]{2,1,0:T(8,128)} broadcast(f32[256]{0:T(256)S(1)} %get-tuple-element.404), dimensions={2} | broadcast | bytes 2098176 | tf_op jit(solution)/shard_map/mul | solution.py:48
  51.2 1.6 %mul.123 = f32[64,32,256]{2,1,0:T(8,128)} broadcast(f32[256]{0:T(256)S(1)} %get-tuple-element.403), dimensions={2} | broadcast | bytes 2098176 | tf_op jit(solution)/shard_map/mul | solution.py:49
  52.8 1.6 %mul.116 = f32[64,32,256]{2,1,0:T(8,128)} broadcast(f32[256]{0:T(256)S(1)} %copy-done.5), dimensions={2} | broadcast | bytes 2098176 | tf_op jit(solution)/shard_map/mul | solution.py:47
  54.4 1.6 %broadcast.93 = f32[64,32,256]{2,1,0:T(8,128)} broadcast(f32[]{:T(128)} %constant.119.clone.1), dimensions={} | broadcast | bytes 2097156 | tf_op jit(solution)/shard_map/broadcast.17
  56.0 71.3 %conditional.3 = (f32[2,2048]{1,0:T(2,128)S(1)}) conditional(s32[]{:T(128)} %convert_element_type.24, (f32[65,32,256]{2,1,0:T(8,128)}, f32[65,32,256]{2,1,0:T(8,128)}, f32[66,33,256]{2,1,0:T(8,128)}, f32[66,33,256]{2,1,0:T(8,128)}, f32[64,32,256]{2,1,0:T(8,128)S(1)}, /*index=5*/f32[64,32,256]{2,1,0:T(8,128)}, f32[64,32,256]{2,1,0:T(8,128)}, ...), branch_computations={%region_4.10_spmd, %region_10.11_spmd} | conditional | flops 142545408 | bytes 24139748 | solution.py:162
  56.5 9.7 %multiply_subtract_fusion = f32[64,32,256]{2,1,0:T(8,128)} fusion(f32[64,32,256]{2,1,0:T(8,128)} %get-tuple-element.312, f32[64,32,256]{2,1,0:T(8,128)} %get-tuple-element.311, f32[64,32,256]{2,1,0:T(8,128)S(1)} %get-tuple-element.304, f32[64,32,256]{2,1,0:T(8,128)} %get-tuple-element.305, f32[64,32,256]{2,1,0:T(8,128)} %get-tuple-element.310, ...), kind=kLoop, calls=%fused_computation.30 | loop fusion | flops 6815744 | bytes 20971520 | tf_op jit(solution)/shard_map/sub | solution.py:46
  66.2 58.9 %while.39 = (s32[]{:T(128)}, f32[2048,256]{1,0:T(8,128)}, s32[2048]{0:T(1024)S(1)}, bf16[256,512]{1,0:T(8,128)(2,1)S(1)}, f32[512]{0:T(512)S(1)}, /*index=5*/bf1...) while((s32[]{:T(128)}, f32[2048,256]{1,0:T(8,128)}, ...), condition=%wide.region_9.9_spmd, body=%wide.region_5.8_spmd.sunk | while | flops 135725568 | bytes 2627404 | solution.py:79
  66.9 1.0 constant_dynamic-slice_fusion.3
  67.9 5.0 %while.40 = (s32[]{:T(128)}, f32[256,256]{1,0:T(8,128)S(1)}, s32[]{:T(128)}, s32[256]{0:T(256)S(1)}, bf16[256,512]{1,0:T(8,128)(2,1)S(1)}, /*index=5*/f32[512]{0:T(512)S(1)}, bf16[512,256]{1,0:T(8,128)(2,1)S(1)}, s32[]{:T(128)}) while((s32[]{:T(128)}, f32[256,256]{1,0:T(8,128)S(1)}, s32[]{:T(128)}, s32[256]{0:T(256)S(1)}, ...), condition=%wide.region_8.7_spmd, body=%wide.region_7.6_spmd.sunk | while | flops 135725312 | bytes 1576537 | solution.py:76
  72.8 0.7 constant_dynamic-update-slice_fusion.5
  74.2 1.0 constant_dynamic-slice_fusion.3
  75.2 4.9 %while.40 = (s32[]{:T(128)}, f32[256,256]{1,0:T(8,128)S(1)}, s32[]{:T(128)}, s32[256]{0:T(256)S(1)}, bf16[256,512]{1,0:T(8,128)(2,1)S(1)}, /*index=5*/f32[512]{0:T(512)S(1)}, bf16[512,256]{1,0:T(8,128)(2,1)S(1)}, s32[]{:T(128)}) while((s32[]{:T(128)}, f32[256,256]{1,0:T(8,128)S(1)}, s32[]{:T(128)}, s32[256]{0:T(256)S(1)}, ...), condition=%wide.region_8.7_spmd, body=%wide.region_7.6_spmd.sunk | while | flops 135725312 | bytes 1576537 | solution.py:76
  81.6 1.0 constant_dynamic-slice_fusion.3
  82.6 4.9 %while.40 = (s32[]{:T(128)}, f32[256,256]{1,0:T(8,128)S(1)}, s32[]{:T(128)}, s32[256]{0:T(256)S(1)}, bf16[256,512]{1,0:T(8,128)(2,1)S(1)}, /*index=5*/f32[512]{0:T(512)S(1)}, bf16[512,256]{1,0:T(8,128)(2,1)S(1)}, s32[]{:T(128)}) while((s32[]{:T(128)}, f32[256,256]{1,0:T(8,128)S(1)}, s32[]{:T(128)}, s32[256]{0:T(256)S(1)}, ...), condition=%wide.region_8.7_spmd, body=%wide.region_7.6_spmd.sunk | while | flops 135725312 | bytes 1576537 | solution.py:76
  87.5 0.7 constant_dynamic-update-slice_fusion.5
  89.0 1.0 constant_dynamic-slice_fusion.3
  89.9 4.9 %while.40 = (s32[]{:T(128)}, f32[256,256]{1,0:T(8,128)S(1)}, s32[]{:T(128)}, s32[256]{0:T(256)S(1)}, bf16[256,512]{1,0:T(8,128)(2,1)S(1)}, /*index=5*/f32[512]{0:T(512)S(1)}, bf16[512,256]{1,0:T(8,128)(2,1)S(1)}, s32[]{:T(128)}) while((s32[]{:T(128)}, f32[256,256]{1,0:T(8,128)S(1)}, s32[]{:T(128)}, s32[256]{0:T(256)S(1)}, ...), condition=%wide.region_8.7_spmd, body=%wide.region_7.6_spmd.sunk | while | flops 135725312 | bytes 1576537 | solution.py:76
  94.9 0.7 constant_dynamic-update-slice_fusion.5
  96.3 1.0 constant_dynamic-slice_fusion.3
  97.3 5.0 %while.40 = (s32[]{:T(128)}, f32[256,256]{1,0:T(8,128)S(1)}, s32[]{:T(128)}, s32[256]{0:T(256)S(1)}, bf16[256,512]{1,0:T(8,128)(2,1)S(1)}, /*index=5*/f32[512]{0:T(512)S(1)}, bf16[512,256]{1,0:T(8,128)(2,1)S(1)}, s32[]{:T(128)}) while((s32[]{:T(128)}, f32[256,256]{1,0:T(8,128)S(1)}, s32[]{:T(128)}, s32[256]{0:T(256)S(1)}, ...), condition=%wide.region_8.7_spmd, body=%wide.region_7.6_spmd.sunk | while | flops 135725312 | bytes 1576537 | solution.py:76
  102.3 0.7 constant_dynamic-update-slice_fusion.5
  103.7 1.0 constant_dynamic-slice_fusion.3
  104.7 4.9 %while.40 = (s32[]{:T(128)}, f32[256,256]{1,0:T(8,128)S(1)}, s32[]{:T(128)}, s32[256]{0:T(256)S(1)}, bf16[256,512]{1,0:T(8,128)(2,1)S(1)}, /*index=5*/f32[512]{0:T(512)S(1)}, bf16[512,256]{1,0:T(8,128)(2,1)S(1)}, s32[]{:T(128)}) while((s32[]{:T(128)}, f32[256,256]{1,0:T(8,128)S(1)}, s32[]{:T(128)}, s32[256]{0:T(256)S(1)}, ...), condition=%wide.region_8.7_spmd, body=%wide.region_7.6_spmd.sunk | while | flops 135725312 | bytes 1576537 | solution.py:76
  109.6 0.7 constant_dynamic-update-slice_fusion.5
  111.1 1.0 constant_dynamic-slice_fusion.3
  112.1 5.0 %while.40 = (s32[]{:T(128)}, f32[256,256]{1,0:T(8,128)S(1)}, s32[]{:T(128)}, s32[256]{0:T(256)S(1)}, bf16[256,512]{1,0:T(8,128)(2,1)S(1)}, /*index=5*/f32[512]{0:T(512)S(1)}, bf16[512,256]{1,0:T(8,128)(2,1)S(1)}, s32[]{:T(128)}) while((s32[]{:T(128)}, f32[256,256]{1,0:T(8,128)S(1)}, s32[]{:T(128)}, s32[256]{0:T(256)S(1)}, ...), condition=%wide.region_8.7_spmd, body=%wide.region_7.6_spmd.sunk | while | flops 135725312 | bytes 1576537 | solution.py:76
  117.0 0.7 constant_dynamic-update-slice_fusion.5
  118.5 1.0 constant_dynamic-slice_fusion.3
  119.4 5.0 %while.40 = (s32[]{:T(128)}, f32[256,256]{1,0:T(8,128)S(1)}, s32[]{:T(128)}, s32[256]{0:T(256)S(1)}, bf16[256,512]{1,0:T(8,128)(2,1)S(1)}, /*index=5*/f32[512]{0:T(512)S(1)}, bf16[512,256]{1,0:T(8,128)(2,1)S(1)}, s32[]{:T(128)}) while((s32[]{:T(128)}, f32[256,256]{1,0:T(8,128)S(1)}, s32[]{:T(128)}, s32[256]{0:T(256)S(1)}, ...), condition=%wide.region_8.7_spmd, body=%wide.region_7.6_spmd.sunk | while | flops 135725312 | bytes 1576537 | solution.py:76
  124.4 0.7 constant_dynamic-update-slice_fusion.5
  125.1 2.1 %slice_reduce_fusion.1 = (f32[2048]{0:T(1024)S(1)}, f32[2048]{0:T(1024)S(1)}) fusion(f32[2048,256]{1,0:T(8,128)} %get-tuple-element.318), kind=kLoop, calls=%fused_computation.32 | loop fusion | bytes 32768 | tf_op jit(solution)/shard_map/cond/branch_0_fun/slice | solution.py:146
  127.4 1.5 %fusion.22 = f32[3,512]{1,0:T(4,128)S(1)} fusion(s32[2048]{0:T(1024)S(1)} %eq.39, f32[1,2048]{1,0:T(1,128)S(1)} %fusion.31, f32[1,2048]{1,0:T(1,128)S(1)} %get-tuple-element.387, f32[3]{0:T(128)S(1)} %pad.6.clone), kind=kOutput, calls=%fused_computation.36 | convolution fusion | flops 38809600 | bytes 30732 | tf_op jit(solution)/shard_map/kr,rc->kc/dot_general | solution.py:178
  (164 shorter events, 24.0 us)
Async XLA Ops:
  0.8 6.1 %collective-permute-start.2 = (f32[1,32,256]{2,1,0:T(8,128)S(1)}, f32[1,32,256]{2,1,0:T(8,128)S(1)}, u32[]{:S(2)}, u32[]{:S(2)}) collective-permute-start(f32[1,32,256]{2,1,0:T(8,128)S(1)} %get-tuple-element.402), channel_id=1, source_target_pairs={{0,8},{8,16},{16,24},{24,32},{32,40},{40,48},{48,56},{56,64},{64,7... | collective-permute-start | bytes 98312 | tf_op jit(solution)/shard_map/ppermute | solution.py:30
  0.8 6.4 %collective-permute-start.1 = (f32[1,32,256]{2,1,0:T(8,128)S(1)}, f32[1,32,256]{2,1,0:T(8,128)S(1)}, u32[]{:S(2)}, u32[]{:S(2)}) collective-permute-start(f32[1,32,256]{2,1,0:T(8,128)S(1)} %get-tuple-element.401), channel_id=1, source_target_pairs={{8,0},{16,8},{24,16},{32,24},{40,32},{48,40},{56,48},{64,56},{72,6... | collective-permute-start | bytes 98312 | tf_op jit(solution)/shard_map/ppermute | solution.py:33
  5.4 1.6 %copy-start = (f32[64,32,256]{2,1,0:T(8,128)S(1)}, f32[64,32,256]{2,1,0:T(8,128)}, u32[]{:S(2)}) copy-start(f32[64,32,256]{2,1,0:T(8,128)} %param.26) | copy-start | bytes 6291460
  5.5 27.5 %collective-permute-start = (f32[512]{0:T(512)S(1)}, f32[512]{0:T(512)S(1)}, u32[]{:S(2)}, u32[]{:S(2)}) collective-permute-start(f32[512]{0:T(512)S(1)} %bitcast.41), channel_id=1, source_target_pairs={{128,0},{129,1},{130,2},{131,3},{132,4},{133,5},{134,6},{135,7},{1... | collective-permute-start | bytes 6152 | tf_op jit(solution)/shard_map/ppermute | solution.py:21
  7.0 5.9 %copy-start.6 = (f32[256]{0:T(256)S(1)}, f32[256]{0:T(256)}, u32[]{:S(2)}) copy-start(f32[256]{0:T(256)} %param.29) | copy-start | bytes 3076
  7.0 5.9 %copy-start.7 = (f32[256]{0:T(256)S(1)}, f32[256]{0:T(256)}, u32[]{:S(2)}) copy-start(f32[256]{0:T(256)} %param.28) | copy-start | bytes 3076
  7.0 5.9 %copy-start.3 = (s32[64,32]{0,1:T(8,128)S(1)}, s32[64,32]{0,1:T(8,128)}, u32[]{:S(2)}) copy-start(s32[64,32]{0,1:T(8,128)} %param.32) | copy-start | bytes 24580
  7.0 6.1 %copy-start.4 = (f32[64,32]{0,1:T(8,128)S(1)}, f32[64,32]{0,1:T(8,128)}, u32[]{:S(2)}) copy-start(f32[64,32]{0,1:T(8,128)} %param.30) | copy-start | bytes 24580
  7.0 11.4 %copy-start.5 = (f32[256]{0:T(256)S(1)}, f32[256]{0:T(256)}, u32[]{:S(2)}) copy-start(f32[256]{0:T(256)} %param.27) | copy-start | bytes 3076
  7.2 1.4 %copy-start.1 = (f32[66,32,256]{2,1,0:T(8,128)}, f32[66,32,256]{2,1,0:T(8,128)S(1)}, u32[]{:S(2)}) copy-start(f32[66,32,256]{2,1,0:T(8,128)S(1)} %constant_dynamic-update-slice_fusion.1) | copy-start | bytes 6488068
  8.7 6.1 %collective-permute-start.3 = (f32[66,1,256]{2,1,0:T(1,128)S(1)}, f32[66,1,256]{2,1,0:T(1,128)S(1)}, u32[]{:S(2)}, u32[]{:S(2)}) collective-permute-start(f32[66,1,256]{2,1,0:T(1,128)S(1)} %get-tuple-element.395), channel_id=1, source_target_pairs={{1,0},{2,1},{3,2},{4,3},{5,4},{6,5},{7,6},{0,7},{9,8},{10,9},{11,1... | collective-permute-start | bytes 202760 | tf_op jit(solution)/shard_map/ppermute | solution.py:33
  12.9 5.5 %collective-permute-start.4 = (f32[66,1,256]{2,1,0:T(1,128)S(1)}, f32[66,1,256]{2,1,0:T(1,128)S(1)}, u32[]{:S(2)}, u32[]{:S(2)}) collective-permute-start(f32[66,1,256]{2,1,0:T(1,128)S(1)} %get-tuple-element.396), channel_id=1, source_target_pairs={{0,1},{1,2},{2,3},{3,4},{4,5},{5,6},{6,7},{7,0},{8,9},{9,10},{10,1... | collective-permute-start | bytes 202760 | tf_op jit(solution)/shard_map/ppermute | solution.py:30
  23.7 11.5 %collective-permute-start.5 = (f32[1,32,256]{2,1,0:T(8,128)S(1)}, f32[1,32,256]{2,1,0:T(8,128)S(1)}, u32[]{:S(2)}, u32[]{:S(2)}) collective-permute-start(f32[1,32,256]{2,1,0:T(8,128)S(1)} %get-tuple-element.400), channel_id=1, source_target_pairs={{8,0},{16,8},{24,16},{32,24},{40,32},{48,40},{56,48},{64,56},{72,6... | collective-permute-start | bytes 98312 | tf_op jit(solution)/shard_map/ppermute | solution.py:33
  25.9 9.3 %collective-permute-start.6 = (f32[1,32,256]{2,1,0:T(8,128)S(1)}, f32[1,32,256]{2,1,0:T(8,128)S(1)}, u32[]{:S(2)}, u32[]{:S(2)}) collective-permute-start(f32[1,32,256]{2,1,0:T(8,128)S(1)} %get-tuple-element.399), channel_id=1, source_target_pairs={{0,8},{8,16},{16,24},{24,32},{32,40},{40,48},{48,56},{56,64},{64,7... | collective-permute-start | bytes 98312 | tf_op jit(solution)/shard_map/ppermute | solution.py:30
  35.3 8.5 %collective-permute-start.7 = (f32[66,1,256]{2,1,0:T(1,128)S(1)}, f32[66,1,256]{2,1,0:T(1,128)S(1)}, u32[]{:S(2)}, u32[]{:S(2)}) collective-permute-start(f32[66,1,256]{2,1,0:T(1,128)S(1)} %get-tuple-element.394), channel_id=1, source_target_pairs={{1,0},{2,1},{3,2},{4,3},{5,4},{6,5},{7,6},{0,7},{9,8},{10,9},{11,1... | collective-permute-start | bytes 202760 | tf_op jit(solution)/shard_map/ppermute | solution.py:33
  41.2 5.5 %collective-permute-start.8 = (f32[66,1,256]{2,1,0:T(1,128)S(1)}, f32[66,1,256]{2,1,0:T(1,128)S(1)}, u32[]{:S(2)}, u32[]{:S(2)}) collective-permute-start(f32[66,1,256]{2,1,0:T(1,128)S(1)} %get-tuple-element.393), channel_id=1, source_target_pairs={{0,1},{1,2},{2,3},{3,4},{4,5},{5,6},{6,7},{7,0},{8,9},{9,10},{10,1... | collective-permute-start | bytes 202760 | tf_op jit(solution)/shard_map/ppermute | solution.py:30
  52.8 3.2 %copy-start.2 = (s32[1024,8]{0,1:T(8,128)S(1)}, s32[1024,8]{0,1:T(8,128)}, u32[]{:S(2)}) copy-start(s32[1024,8]{0,1:T(8,128)} %param.31) | copy-start | bytes 98308
  52.8 3.2 %copy-start.8 = (bf16[256,512]{1,0:T(8,128)(2,1)S(1)}, bf16[256,512]{1,0:T(8,128)(2,1)}, u32[]{:S(2)}) copy-start(bf16[256,512]{1,0:T(8,128)(2,1)} %param.37) | copy-start | bytes 786436
  52.8 3.2 %copy-start.9 = (bf16[512,256]{1,0:T(8,128)(2,1)S(1)}, bf16[512,256]{1,0:T(8,128)(2,1)}, u32[]{:S(2)}) copy-start(bf16[512,256]{1,0:T(8,128)(2,1)} %param.39) | copy-start | bytes 786436
  52.8 3.2 %copy-start.10 = (f32[512]{0:T(512)S(1)}, f32[512]{0:T(512)}, u32[]{:S(2)}) copy-start(f32[512]{0:T(512)} %param.38) | copy-start | bytes 6148
where the time goes:
time: 131 us; the launch traced here: 130 us
  local copies, waits for them, and re-layouts  27.5 us (21%)
  other arithmetic  26.5 us (20%)
  loops' own time  24.5 us (19%)
  matrix products  18.3 us (14%)
  starting transfers between devices  17.6 us (13%)
  waiting for transfers between devices  15 us (11%)
    another operation x8, loops' own time, one_tile(): block = lax.fori_loop(jnp.int32(0), jnp.max(needed), one_round, block)  24.2 us
    ppermute x4, starting transfers between devices, padded_2(): lax.ppermute(lax.slice_in_dim(block, 0, width, axis=dim), axis, backward)  16.1 us
    sub x2, other arithmetic, advance(): centre + spreading_numbers * spread  15 us
    dot_general x32, matrix products, one_round(): jnp.dot(hidden, exit_layer_matrix, preferred_element_type=jnp.float32)  14.6 us
    dynamic_slice x8, local copies, waits for them, and re-layouts, one_tile(): block = lax.dynamic_slice_in_dim(result, start, tile, 0)  7.73 us
    ppermute x1, waiting for transfers between devices, shifted(): return lax.ppermute(block, axis, route)  7.13 us
    ppermute x4, waiting for transfers between devices, padded_2(): lax.ppermute(lax.slice_in_dim(block, block.shape[dim] - width, None, axis...  6.52 us
    dynamic_update_slice x8, local copies, waits for them, and re-layouts, one_tile(): return lax.dynamic_update_slice_in_dim(result, block, start, 0)  5.82 us
  transfers between devices with their start and end apart: 9, of which 4 were waited for; matrix products, arithmetic and copies ran while one was open for 9% of the time, Pallas kernels for 0%

commit v1 on v0

v1 whole, which is shorter than its diff:
```python
import functools

import jax
import jax.numpy as jnp
from jax import lax
from jax.experimental import pallas as pl
from jax.experimental.pallas import tpu as pltpu
from jax.sharding import PartitionSpec as P

BS = 4
PAIRS = 6
THERMAL_FACTOR = 0.8
WETNESS_FACTOR = 0.6
OCEAN_STEP = 0.1
TANH_SCALE = 0.7978845608028654
TANH_CUBE = 0.044715

GROUPS = 3
TILES = 5
LANES = 128
NT = (((1,), (1,)), ((), ()))
F32 = jnp.float32
BF16 = jnp.bfloat16
AXES = ("sect", "gx", "gy")


def iota(shape, dim):
    return lax.broadcasted_iota(jnp.int32, shape, dim)


def coefficients(spread, east, north):
    return (
        1.0 - 4.0 * spread,
        spread - 0.5 * east,
        spread + 0.5 * east,
        spread - 0.5 * north,
        spread + 0.5 * north,
    )


def combine(coefs, centre, plus_x, minus_x, plus_y, minus_y):
    c0, cxp, cxm, cyp, cym = coefs
    return c0 * centre + cxp * plus_x + cxm * minus_x + cyp * plus_y + cym * minus_y


def advance(block, coefs):
    centre = block[1:-1]
    size = centre.shape[1]
    plus_y = pltpu.roll(centre, size - 1, 1)
    minus_y = pltpu.roll(centre, 1, 1)
    return combine(coefs, centre, block[2:], block[:-2], plus_y, minus_y)


def hidden_of(state, w1, bias):
    half = jnp.dot(state.astype(BF16), w1, preferred_element_type=F32) + bias
    inner = half * (half * half * (8.0 * TANH_SCALE * TANH_CUBE) + 2.0 * TANH_SCALE)
    return (half * jnp.tanh(inner) + half).astype(BF16)


def physics(state, counts, w1, bias, w2, w2_last):
    for index in range(3):
        delta = jnp.dot(hidden_of(state, w1, bias), w2, preferred_element_type=F32)
        if index:
            needed = counts > float(index)
            delta = jnp.where(jnp.concatenate([needed, needed], 1), delta, 0.0)
        state = state + delta
    delta = jnp.dot(hidden_of(state, w1, bias), w2_last, preferred_element_type=F32)
    lane = iota((1, LANES), 1)
    kept = jnp.where(lane == 0, state[:, :LANES], pltpu.roll(state[:, LANES:], 1, 1))
    return kept + jnp.where(counts > 3.0, delta, 0.0)


def weights(w1_ref, b_ref, w2_ref):
    w1 = w1_ref[...] * jnp.asarray(0.5, BF16)
    bias = b_ref[...] * 0.5
    w2 = w2_ref[...]
    lane = iota((1, LANES), 1)
    low = w2[:, :LANES].astype(F32)
    high = pltpu.roll(w2[:, LANES:].astype(F32), 1, 1)
    last = jnp.where(lane == 0, low, jnp.where(lane == 1, high, 0.0)).astype(BF16)
    return w1, bias, w2, last


def expand_counts(row):
    square = (LANES, LANES)
    diagonal = jnp.where(iota(square, 0) == iota(square, 1), row, 0.0).astype(BF16)
    return jnp.dot(diagonal, jnp.ones(square, BF16), preferred_element_type=F32)


def split(row):
    high = row.astype(BF16).astype(F32)
    return high, row - high


def one_hots(cells, row):
    n = cells.shape[1]
    first = iota((32, n), 0) == jnp.right_shift(cells, 4)
    second = (iota((16, n), 0) == jnp.bitwise_and(cells, 15)) & (cells >= 0)
    return first, second.astype(F32).astype(BF16)


def scatter(values, first, second):
    rows = []
    for value in values:
        for part in split(value):
            rows.append(jnp.where(first, part, 0.0))
    stacked = jnp.concatenate(rows, 0).astype(BF16)
    return lax.dot_general(stacked, second, NT, preferred_element_type=F32)


def scatter_columns(kept, cells):
    n = kept.shape[0]
    rows = [jnp.transpose(kept[i : i + LANES])[:2] for i in range(0, n, LANES)]
    flat = jnp.concatenate(rows, 1)
    first, second = one_hots(cells, None)
    return scatter([flat[0:1], flat[1:2]], first, second)


def own_counts(inc_ref, size):
    gx = lax.axis_index("gx")
    start = pl.multiple_of((gx // 2) * LANES, LANES)
    block = inc_ref[:, pl.ds(start, LANES)].astype(F32)
    block = jnp.where(gx % 2 == 1, pltpu.roll(block, 64, 1), block)
    spread = (iota((size, 8), 0) // BS == iota((size, 8), 1)).astype(F32)
    return jnp.dot(spread.astype(BF16), block.astype(BF16), preferred_element_type=F32)


def coded_columns(idx_ref, inc_ref):
    counts = own_counts(inc_ref, idx_ref.shape[0])
    cells = idx_ref[...].astype(F32)
    cells = jnp.concatenate([cells, jnp.zeros_like(cells)], 1)
    return cells * 8.0 + counts


def decode(code):
    whole = code.astype(jnp.int32)
    return jnp.right_shift(whole, 3), jnp.bitwise_and(whole, 7).astype(F32)


def interior_kernel(
    range_ref, air_ref, spread_ref, east_ref, north_ref, idx_ref, inc_ref, w1_ref, b_ref, w2_ref,
    acc_ref, turned, cell_rows, count_rows,
):
    lo = range_ref[0]
    hi = range_ref[1]
    acc_ref[...] = jnp.zeros_like(acc_ref)

    @pl.when(hi > lo)
    def _():
        code = coded_columns(idx_ref, inc_ref)
        code = jnp.concatenate([code, jnp.zeros((96, LANES), F32)], 0)
        turned[...] = jnp.transpose(code)
        groups = GROUPS * TILES
        parts = [turned[pl.ds(2 + j, groups, stride=4), :][:, :32] for j in range(4)]
        cells, counts = decode(jnp.concatenate(parts, 1))
        y = jnp.bitwise_and(iota((1, LANES), 1), 31)
        cells = jnp.where((y >= 2) & (y < 30), cells, -1)
        cell_rows[pl.ds(0, groups), :] = cells
        count_rows[pl.ds(0, groups), :] = counts

        coefs = coefficients(spread_ref[...], east_ref[...], north_ref[...])
        w1, bias, w2, w2_last = weights(w1_ref, b_ref, w2_ref)

        @pl.loop(lo, hi)
        def _(tile):
            block = air_ref[pl.ds(tile * (4 * GROUPS), 4 * GROUPS + 4)]
            state = advance(advance(block, coefs), coefs).reshape(GROUPS * LANES, 256)
            rows = [cell_rows[pl.ds(tile * GROUPS + g, 1), :] for g in range(GROUPS)]
            needs = [expand_counts(count_rows[pl.ds(tile * GROUPS + g, 1), :]) for g in range(GROUPS)]
            kept = physics(state, jnp.concatenate(needs, 0), w1, bias, w2, w2_last)
            acc_ref[...] += scatter_columns(kept, jnp.concatenate(rows, 1))


def interior(bounds, air, small, big):
    vmem = pl.BlockSpec(memory_space=pltpu.VMEM)
    return pl.pallas_call(
        interior_kernel,
        out_shape=jax.ShapeDtypeStruct((LANES, 16), F32),
        in_specs=[pl.BlockSpec(memory_space=pltpu.SMEM)] + [vmem] * 9,
        out_specs=vmem,
        scratch_shapes=[
            pltpu.VMEM((LANES, LANES), F32),
            pltpu.VMEM((16, LANES), jnp.int32),
            pltpu.VMEM((16, LANES), F32),
        ],
        compiler_params=pltpu.CompilerParams(vmem_limit_bytes=32 << 20),
        cost_estimate=pl.CostEstimate(flops=1 << 30, bytes_accessed=2 << 20, transcendentals=1 << 20),
    )(bounds, air, *small, *big)


def slab_kernel(air_ref, low_ref, high_ref, low4_ref, high4_ref, low_blk, high_blk, sem):
    copies = []
    for side, block in ((0, low_blk), (1, high_blk)):
        for half in range(2):
            source = air_ref.at[:, pl.ds(24 * side, 8), pl.ds(half * LANES, LANES)]
            copy = pltpu.make_async_copy(source, block.at[half], sem.at[side, half])
            copy.start()
            copies.append(copy)
    for side, block, send, keep in ((0, low_blk, low_ref, low4_ref), (1, high_blk, high_ref, high4_ref)):
        for half in range(2):
            copies[2 * side + half].wait()
            flat = block.at[half].reshape(64 * 8, LANES)
            lanes = pl.ds(half * LANES, LANES)
            for k in range(4):
                row = flat[pl.ds(4 * side + k, 64, stride=8), :]
                keep[k, :, lanes] = row
                sent = k - 2 * side
                if 0 <= sent < 2:
                    send[pl.ds(sent * 64, 64), lanes] = row


def y_slabs(air):
    vmem = pl.BlockSpec(memory_space=pltpu.VMEM)
    return pl.pallas_call(
        slab_kernel,
        out_shape=[jax.ShapeDtypeStruct((LANES, 256), F32)] * 2
        + [jax.ShapeDtypeStruct((4, 64, 256), F32)] * 2,
        in_specs=[pl.BlockSpec(memory_space=pl.ANY)],
        out_specs=[vmem] * 4,
        scratch_shapes=[
            pltpu.VMEM((2, 64, 8, LANES), F32),
            pltpu.VMEM((2, 64, 8, LANES), F32),
            pltpu.SemaphoreType.DMA((2, 2)),
        ],
    )(air)


def shift_down(block, edge):
    row = iota(block.shape, 1)
    return jnp.where(row == 0, edge, pltpu.roll(block, 1, 1))


def shift_up(block, edge):
    row = iota(block.shape, 1)
    size = block.shape[1]
    return jnp.where(row == size - 1, edge, pltpu.roll(block, size - 1, 1))


def edge_states(air_ref, low4_ref, high4_ref, ylow, yhigh, xlow_ref, xhigh_ref, coefs):
    xlow = xlow_ref[...]
    xhigh = xhigh_ref[...]
    before = xlow[:64].reshape(2, 32, 256)
    after = xhigh[:64].reshape(2, 32, 256)
    first_low = advance(jnp.concatenate([before, air_ref[0:4]], 0), coefs)
    first_high = advance(jnp.concatenate([air_ref[60:64], after], 0), coefs)
    state_x = jnp.concatenate([advance(first_low, coefs), advance(first_high, coefs)], 0)

    def column(halo, corners, inner, at, side):
        far, near = (0, 1) if side else (1, 0)
        lo_y = corners[0:1] if at == 0 else halo[near, at - 1 : at]
        hi_y = corners[1:2] if at == 31 else halo[near, at + 1 : at + 2]
        centre = halo[near, at : at + 1]
        outer = halo[far, at : at + 1]
        plus_x, minus_x = (inner, outer) if side else (outer, inner)
        return combine(coefs, centre, plus_x, minus_x, hi_y, lo_y)

    states = []
    for low in (True, False):
        if low:
            block = jnp.concatenate([ylow, low4_ref[...]], 0)
            left = [xlow[64:65]] + [before[1, y : y + 1] for y in (0, 1, 2)]
            right = [xhigh[64:65]] + [after[0, y : y + 1] for y in (0, 1, 2)]
            targets = (0, 1)
        else:
            block = jnp.concatenate([high4_ref[...], yhigh], 0)
            left = [before[1, y : y + 1] for y in (29, 30, 31)] + [xlow[65:66]]
            right = [after[0, y : y + 1] for y in (29, 30, 31)] + [xhigh[65:66]]
            targets = (30, 31)
        centre = block[1:-1]
        once = combine(
            coefs,
            centre,
            shift_up(centre, jnp.stack(right, 0)),
            shift_down(centre, jnp.stack(left, 0)),
            block[2:],
            block[:-2],
        )
        left, right = [], []
        for y in targets:
            left.append(column(before, xlow[64:66], air_ref[0, y : y + 1, :], y, True))
            right.append(column(after, xhigh[64:66], air_ref[63, y : y + 1, :], y, False))
        centre = once[1:-1]
        twice = combine(
            coefs,
            centre,
            shift_up(centre, jnp.stack(right, 0)),
            shift_down(centre, jnp.stack(left, 0)),
            once[2:],
            once[:-2],
        )
        states.append(twice.reshape(LANES, 256))
    return jnp.concatenate(states, 0), state_x.reshape(LANES, 256)


def ocean_surface(water, driver, ocean_ref, mixing_ref, row_scratch):
    levels = mixing_ref.shape[0]
    matrix = mixing_ref[...]
    wide = jnp.concatenate([matrix, jnp.zeros((levels, LANES - levels), F32)], 1)
    tall = jnp.concatenate([wide, jnp.zeros((LANES - levels, LANES), F32)], 0)
    turned = jnp.transpose(tall)
    column = (iota((LANES, 1), 0) == 0).astype(F32)
    total = jnp.zeros((1, 1), F32)

    def pair(_, carry):
        column, total = carry
        row = jnp.sum(column * tall, axis=0, keepdims=True)
        total = total + row[:, 0:1]
        column = jnp.sum(turned * row, axis=1, keepdims=True)
        return column, total + column[0:1]

    column, total = lax.fori_loop(0, PAIRS, pair, (column, total))
    row = jnp.transpose(jnp.broadcast_to(column, (LANES, LANES)))[0:1, :levels]
    fields = []
    for field in range(2):
        block = ocean_ref[field]
        mixed = jnp.sum(block * row, axis=2)
        top = block[:, :, 0]
        mixed = jnp.transpose(mixed) + (OCEAN_STEP * total) * driver[field]
        fields.append(jnp.where(water == 1, mixed, jnp.transpose(top)))
    return fields


def land_sums(land, cells):
    lands = jnp.concatenate([land[y : y + 1] for y in range(32)], 1)
    places = jnp.concatenate([cells[y : y + 1] for y in range(32)], 1)
    first, second = one_hots(places, None)
    sums = scatter([lands, jnp.tanh(lands)], first, second)
    count = lax.dot_general(
        first.astype(F32).astype(BF16), second, NT, preferred_element_type=F32
    )
    return sums, count


def side_kernel(
    ocean_ref, water_ref, driver_ref, mixing_ref, land_ref, idx_ref, out_ref, row_scratch
):
    fields = ocean_surface(water_ref[...], driver_ref[...], ocean_ref, mixing_ref, row_scratch)
    sums, count = land_sums(land_ref[...], idx_ref[...])
    land = jnp.transpose(sums[0:32] + sums[32:64])
    warm = jnp.transpose(sums[64:96] + sums[96:128])
    count = jnp.transpose(count)
    sea = water_ref[...] == 1
    top = fields[0]
    out_ref[0] = fields[0]
    out_ref[1] = fields[1]
    out_ref[2] = jnp.where(sea, count * top, land)
    out_ref[3] = jnp.where(sea, count * jnp.tanh(top), warm)
    out_ref[4] = jnp.maximum(count, 1.0)


def side(ocean, water, driver, mixing, land, idx):
    vmem = pl.BlockSpec(memory_space=pltpu.VMEM)
    return pl.pallas_call(
        side_kernel,
        out_shape=jax.ShapeDtypeStruct((5, 16, 32), F32),
        in_specs=[vmem] * 6,
        out_specs=vmem,
        scratch_shapes=[pltpu.VMEM((8, LANES), F32)],
        compiler_params=pltpu.CompilerParams(vmem_limit_bytes=32 << 20),
        cost_estimate=pl.CostEstimate(flops=1 << 22, bytes_accessed=2 << 20, transcendentals=0),
    )(ocean, water, driver, mixing, land, idx)


def edge_kernel(
    air_ref, low4_ref, high4_ref, ylow_ref, yhigh_ref, xlow_ref, xhigh_ref, spread_ref, east_ref,
    north_ref, idx_ref, inc_ref, w1_ref, b_ref, w2_ref, side_ref, acc0_ref, acc1_ref, acc2_ref, out_ref,
):
    coefs = coefficients(spread_ref[...], east_ref[...], north_ref[...])
    w1, bias, w2, w2_last = weights(w1_ref, b_ref, w2_ref)
    ylow = ylow_ref[...].reshape(2, 64, 256)
    yhigh = yhigh_ref[...].reshape(2, 64, 256)
    by_y, by_x = edge_states(
        air_ref, low4_ref, high4_ref, ylow, yhigh, xlow_ref, xhigh_ref, coefs
    )
    code = coded_columns(idx_ref, inc_ref)
    rows_y = [
        jnp.concatenate([code[0:1, :64], code[1:2, :64]], 1),
        jnp.concatenate([code[30:31, :64], code[31:32, :64]], 1),
    ]
    code = jnp.concatenate([code, jnp.zeros((96, LANES), F32)], 0)
    turned = jnp.transpose(code)[:, :32]
    row_x = jnp.concatenate([turned[i : i + 1] for i in (0, 1, 62, 63)], 1)
    cells, counts = decode(jnp.concatenate(rows_y + [row_x], 1))
    place = iota(cells.shape, 1)
    y = jnp.bitwise_and(place, 31)
    cells = jnp.where((place < 2 * LANES) | ((y >= 2) & (y < 30)), cells, -1)
    needs = [expand_counts(counts[:, i : i + LANES]) for i in range(0, 3 * LANES, LANES)]
    state = jnp.concatenate([by_y, by_x], 0)
    kept = physics(state, jnp.concatenate(needs, 0), w1, bias, w2, w2_last)
    acc = scatter_columns(kept, cells) + acc0_ref[...] + acc1_ref[...] + acc2_ref[...]
    heat = jnp.transpose(acc[0:32] + acc[32:64])
    vapour = jnp.transpose(acc[64:96] + acc[96:128])
    below = side_ref[4]
    ocean = lax.axis_index("sect") == 1
    flux = THERMAL_FACTOR * (side_ref[2] - heat) / below
    out_ref[0] = jnp.where(ocean, side_ref[0], flux)
    flux = WETNESS_FACTOR * (side_ref[3] - vapour) / below
    out_ref[1] = jnp.where(ocean, side_ref[1], flux)


def edges(air, halos, small, big, others):
    vmem = pl.BlockSpec(memory_space=pltpu.VMEM)
    return pl.pallas_call(
        edge_kernel,
        out_shape=jax.ShapeDtypeStruct((2, 16, 32), F32),
        in_specs=[vmem] * 19,
        out_specs=vmem,
        compiler_params=pltpu.CompilerParams(vmem_limit_bytes=32 << 20),
        cost_estimate=pl.CostEstimate(flops=1 << 28, bytes_accessed=2 << 20, transcendentals=1 << 20),
    )(air, *halos, *small, *big, *others)


def neighbours(dx, dy):
    sections, nx, ny = (lax.axis_size(axis) for axis in AXES)

    def place(s, x, y):
        return (s * nx + x % nx) * ny + y % ny

    return [
        (place(s, x + dx, y + dy), place(s, x, y))
        for s in range(sections)
        for x in range(nx)
        for y in range(ny)
    ]


def tied(first, second):
    return lax.optimization_barrier((first, second))


def shards(
    air_profile_matrix,
    spreading_numbers,
    eastward_advection_number,
    northward_advection_number,
    landmass_warmth,
    physics_increments,
    underlying_water_index,
    water_indicator,
    waterbody_profiles,
    waterbody_drivers,
    inverted_blending_matrix,
    entry_layer_matrix,
    entry_layer_offset,
    exit_layer_matrix,
):
    air = air_profile_matrix
    idx = underlying_water_index.T
    small = (
        spreading_numbers.reshape(1, -1),
        eastward_advection_number.reshape(1, -1),
        northward_advection_number.reshape(1, -1),
        idx,
        physics_increments.T,
    )
    big = (entry_layer_matrix, entry_layer_offset.reshape(1, -1), exit_layer_matrix)
    gy = lax.axis_index("gy")
    early = jnp.where(gy < 2, 2, jnp.where(gy < 4, 1, 0)).astype(jnp.int32)
    middle = early + 2

    slab_low, slab_high, low4, high4 = y_slabs(air)
    acc0 = interior(jnp.stack([jnp.int32(0), early]), air, small, big)
    acc0, slab_low, slab_high = lax.optimization_barrier((acc0, slab_low, slab_high))
    ylow = lax.ppermute(slab_high, AXES, neighbours(0, -1))
    yhigh = lax.ppermute(slab_low, AXES, neighbours(0, 1))
    acc1 = interior(jnp.stack([early, middle]), air, small, big)
    acc1, ylow, yhigh = lax.optimization_barrier((acc1, ylow, yhigh))
    pad = jnp.zeros((6, 256), F32)
    send_high = jnp.concatenate(
        [air[62], air[63], ylow[127:128], yhigh[63:64], pad], 0
    )
    send_low = jnp.concatenate([air[0], air[1], ylow[64:65], yhigh[0:1], pad], 0)
    xlow = lax.ppermute(send_high, AXES, neighbours(-1, 0))
    xhigh = lax.ppermute(send_low, AXES, neighbours(1, 0))
    sides = side(
        waterbody_profiles.transpose(0, 2, 3, 1),
        water_indicator.T,
        waterbody_drivers.transpose(0, 2, 1),
        inverted_blending_matrix,
        landmass_warmth.T,
        idx,
    )
    acc2 = interior(jnp.stack([middle, jnp.int32(TILES)]), air, small, big)
    acc2, sides, xlow, xhigh = lax.optimization_barrier((acc2, sides, xlow, xhigh))
    result = edges(air, (low4, high4, ylow, yhigh, xlow, xhigh), small, big, (sides, acc0, acc1, acc2))
    return result.transpose(0, 2, 1)[None]


def solution(mesh):
    in_specs = (
        P("gx", "gy", None),
        P(),
        P(),
        P(),
        P("gx", "gy"),
        P(None, "gy"),
        P("gx", "gy"),
        P("gx", "gy"),
        P(None, None, "gx", "gy"),
        P(None, "gx", "gy"),
        P(),
        P(),
        P(),
        P(),
    )
    out_specs = P("sect", None, "gx", "gy")
    return jax.shard_map(shards, mesh=mesh, in_specs=in_specs, out_specs=out_specs, check_vma=False)
```

time: 131 us -> 41.5 us (0.32)
  the two profiles are of different devices: /device:TPU:0 before, /device:TPU:4 now
where the time goes in v1:
time: 41.5 us; the launch traced here: 41 us
  Pallas kernels  20.1 us (48%)
  local copies, waits for them, and re-layouts  12.5 us (30%)
  starting transfers between devices  5.77 us (14%)
  waiting for transfers between devices  1.63 us (4%)
  other arithmetic  0.81 us (2%)
    pallas_call x3, Pallas kernels, interior(): pl.pallas_call(interior_kernel, out_shape=jax.ShapeDtypeStruct((LANES, 16...  13.1 us
    unnamed x56, local copies, waits for them, and re-layouts  5.41 us
    concatenate x1, local copies, waits for them, and re-layouts, shards(): jnp.concatenate([air[62], air[63], ylow[127:128], yhigh[63:64], pad], 0)  4.05 us
    pallas_call x1, Pallas kernels, edges(): pl.pallas_call(edge_kernel, out_shape=jax.ShapeDtypeStruct((2, 16, 32), F...  3.23 us
    ppermute x1, starting transfers between devices, shards(): xhigh = lax.ppermute(send_low, AXES, neighbours(1, 0))  2.53 us
    pallas_call x1, Pallas kernels, y_slabs(): pl.pallas_call(slab_kernel, out_shape=[jax.ShapeDtypeStruct((LANES, 256),...  2.28 us
    ppermute x1, starting transfers between devices, shards(): ylow = lax.ppermute(slab_high, AXES, neighbours(0, -1))  1.92 us
    concatenate x1, local copies, waits for them, and re-layouts, shards(): jnp.concatenate([air[0], air[1], ylow[64:65], yhigh[0:1], pad], 0)  1.82 us
  transfers between devices with their start and end apart: 4, of which 1 were waited for; matrix products, arithmetic and copies ran while one was open for 13% of the time, Pallas kernels for 23%

profile of v1, /device:TPU:4, one launch (start us, length us, event | category | flops | bytes accessed | tf_op | source)
XLA Modules:
  0.0 41.0 jit_solution(10170417714523422533)
XLA Ops:
  0.0 0.0 copy-start.22
  0.0 0.0 copy-start.23
  0.0 0.0 copy-start.20
  0.0 2.3 %shard_map.136 = (f32[128,256]{1,0:T(8,128)}, f32[128,256]{1,0:T(8,128)}, f32[4,64,256]{2,1,0:T(8,128)}, f32[4,64,256]{2,1,0:T(8,128)}) custom-call(f32[64,32,256]{2,1,0:T(8,128)} %air_ref.9), custom_call_target="tpu_custom_call" | custom-call | tf_op jit(solution)/shard_map/pallas_call | solution.py:214
  2.4 0.1 pad_add_fusion.1.range_ref
  2.4 0.0 copy-done
  2.4 0.0 copy-done.12
  2.4 0.0 copy-done.21
  2.4 0.0 copy-done.22
  2.4 0.0 copy-done.23
  2.5 0.0 copy-done.20
  2.5 0.0 copy-start.2
  2.5 0.9 %copy-done.2 = bf16[256,512]{1,0:T(8,128)(2,1)S(1)} copy-done((bf16[256,512]{1,0:T(8,128)(2,1)S(1)}, bf16[256,512]{1,0:T(8,128)(2,1)}, u32[]{:S(2)}) %copy-start.2) | copy-done | bytes 262168
  3.4 0.9 %copy-done.4 = bf16[512,256]{1,0:T(8,128)(2,1)S(1)} copy-done((bf16[512,256]{1,0:T(8,128)(2,1)S(1)}, bf16[512,256]{1,0:T(8,128)(2,1)}, u32[]{:S(2)}) %copy-start.4) | copy-done | bytes 262168
  4.4 0.8 %copy-done.14 = s32[1024,8]{0,1:T(8,128)S(1)} copy-done((s32[1024,8]{0,1:T(8,128)S(1)}, s32[1024,8]{0,1:T(8,128)}, u32[]{:S(2)}) %copy-start.14) | copy-done | bytes 32792
  5.1 0.0 copy-start.15
  5.1 5.1 %shard_map.138.acc0_ref = f32[128,16]{1,0:T(8,128)S(1)} custom-call(s32[2]{0:T(128)S(1)} %pad_add_fusion.1.range_ref, f32[64,32,256]{2,1,0:T(8,128)S(1)} %copy-done, f32[1,256]{1,0:T(1,128)S(1)} %bitcast.40, f32[1,256]{1,0:T(1,128)S(1)} %bitcast.44, f32[1,256]{1,0:T(1,128)S(1)} %bitcast.48, s32[32,64]{1,0:T(8,128)S(1)} %bitcast.24, s32[8,1024]{1,0:T(8,128)S(1)} %bitcast.29, ...), custom_call_target="tpu_custom_call" | custom-call | flops 1073741824 | bytes 2097152 | tf_op jit(solution)/shard_map/pallas_call | solution.py:176
  10.2 0.6 %copy-done.8 = f32[128,16]{1,0:T(8,128)} copy-done((f32[128,16]{1,0:T(8,128)}, f32[128,16]{1,0:T(8,128)S(1)}, u32[]{:S(2)}) %copy-start.8) | copy-done | bytes 8216
  10.9 1.9 %collective-permute-start = (f32[128,256]{1,0:T(8,128)S(1)}, f32[128,256]{1,0:T(8,128)S(1)}, u32[]{:S(2)}, u32[]{:S(2)}) collective-permute-start(f32[128,256]{1,0:T(8,128)S(1)} %copy-done.27), channel_id=1, source_target_pairs={{7,0},{0,1},{1,2},{2,3},{3,4},{4,5},{5,6},{6,7},{15,8},{8,9},{9,10... | collective-permute-start | bytes 393224 | tf_op jit(solution)/shard_map/ppermute | solution.py:464
  12.8 1.3 %collective-permute-start.1 = (f32[128,256]{1,0:T(8,128)S(1)}, f32[128,256]{1,0:T(8,128)S(1)}, u32[]{:S(2)}, u32[]{:S(2)}) collective-permute-start(f32[128,256]{1,0:T(8,128)S(1)} %copy-done.26), channel_id=1, source_target_pairs={{1,0},{2,1},{3,2},{4,3},{5,4},{6,5},{7,6},{0,7},{9,8},{10,9},{11,1... | collective-permute-start | bytes 393224 | tf_op jit(solution)/shard_map/ppermute | solution.py:465
  14.1 0.0 copy-start.19
  14.1 0.6 %slice_bitcast_fusion = (f32[32,256]{1,0:T(8,128)S(1)}, f32[32,256]{1,0:T(8,128)S(1)}, f32[32,256]{1,0:T(8,128)}, f32[32,256]{1,0:T(8,128)}) fusion(f32[64,32,256]{2,1,0:T(8,128)S(1)} %copy-done), kind=kLoop, calls=%fused_computation | loop fusion | bytes 262144 | tf_op jit(solution)/shard_map/squeeze | solution.py:472
  14.7 0.1 pad_add_fusion.range_ref
  14.8 5.1 %shard_map.137.acc1_ref = f32[128,16]{1,0:T(8,128)S(1)} custom-call(s32[2]{0:T(128)S(1)} %pad_add_fusion.range_ref, f32[64,32,256]{2,1,0:T(8,128)S(1)} %copy-done, f32[1,256]{1,0:T(1,128)S(1)} %bitcast.41, f32[1,256]{1,0:T(1,128)S(1)} %bitcast.45, f32[1,256]{1,0:T(1,128)S(1)} %bitcast.49, s32[32,64]{1,0:T(8,128)S(1)} %bitcast.25, s32[8,1024]{1,0:T(8,128)S(1)} %bitcast.30, ...), custom_call_target="tpu_custom_call" | custom-call | flops 1073741824 | bytes 2097152 | tf_op jit(solution)/shard_map/pallas_call | solution.py:176
  19.9 0.0 copy-start.10
  19.9 0.0 copy-done.1
  19.9 0.0 copy-done.13
  19.9 0.0 copy-done.17
  19.9 0.0 copy-done.18
  20.0 0.0 copy-done.19
  20.0 1.4 %shard_map.140.side_ref = f32[5,16,32]{2,1,0:T(8,128)S(1)} custom-call(f32[2,32,16,80]{3,2,1,0:T(8,128)S(1)} %bitcast.23, s32[16,32]{1,0:T(8,128)S(1)} %bitcast.35, f32[2,16,32]{2,1,0:T(8,128)S(1)} %bitcast.33, f32[80,80]{1,0:T(8,128)S(1)} %copy-done.13, f32[32,64]{1,0:T(8,128)S(1)} %bitcast.34, s32[32,64]{1,0:T(8,128)S(1)} %bitcast.26), custom_call_target="tpu_custom_call" | custom-call | flops 4194304 | bytes 2097152 | tf_op jit(solution)/shard_map/pallas_call | solution.py:353
  21.4 0.7 %pad_add_fusion.2.range_ref = s32[2]{0:T(128)} fusion(s32[1]{0:T(128)} %constant.6.clone.1, s32[1]{0:T(128)} %bitcast.1), kind=kLoop, calls=%fused_computation.6 | loop fusion | flops 2 | bytes 16 | tf_op jit(solution)/shard_map/stack | solution.py:483
  22.1 0.0 collective-permute-done.ylow_ref
  22.1 0.0 collective-permute-done.1.yhigh_ref
  22.1 0.6 %fusion = (f32[1,256]{1,0:T(1,128)S(1)}, f32[1,256]{1,0:T(1,128)}, f32[1,256]{1,0:T(1,128)}, f32[1,256]{1,0:T(1,128)S(1)}) fusion(f32[128,256]{1,0:T(8,128)S(1)} %collective-permute-done.1.yhigh_ref, f32[128,256]{1,0:T(8,128)S(1)} %collective-permute-done.ylow_ref), kind=kLoop, calls=%fused_computation.7 | loop fusion | bytes 8192 | tf_op jit(solution)/shard_map/slice | solution.py:472
  22.7 0.6 %copy-done.25 = f32[6,256]{1,0:T(8,128)} copy-done((f32[6,256]{1,0:T(8,128)}, f32[6,256]{1,0:T(8,128)S(1)}, u32[]{:S(2)}) %copy-start.25) | copy-done | bytes 6168
  23.3 1.8 %concatenate.7 = f32[72,256]{1,0:T(8,128)} concatenate(f32[32,256]{1,0:T(8,128)S(1)} %get-tuple-element.34, f32[32,256]{1,0:T(8,128)S(1)} %get-tuple-element.33, f32[1,256]{1,0:T(1,128)S(1)} %get-tuple-element.42, f32[1,256]{1,0:T(1,128)S(1)} %get-tuple-element.37, f32[6,256]{1,0:T(8,128)S(1)} %broadcast_in_dim.6), dimensions={0} | concatenate | bytes 147456 | tf_op jit(solution)/shard_map/concatenate | solution.py:472
  25.1 2.5 %collective-permute-start.3 = (f32[72,256]{1,0:T(8,128)}, f32[72,256]{1,0:T(8,128)S(1)}, u32[]{:S(2)}, u32[]{:S(2)}) collective-permute-start(f32[72,256]{1,0:T(8,128)} %concatenate.7), channel_id=1, source_target_pairs={{8,0},{9,1},{10,2},{11,3},{12,4},{13,5},{14,6},{15,7},{16,8},{17,9... | collective-permute-start | bytes 221192 | tf_op jit(solution)/shard_map/ppermute | solution.py:474
  27.6 4.1 %concatenate.6 = f32[72,256]{1,0:T(8,128)} concatenate(f32[32,256]{1,0:T(8,128)} %get-tuple-element.36, f32[32,256]{1,0:T(8,128)} %get-tuple-element.35, f32[1,256]{1,0:T(1,128)} %get-tuple-element.41, f32[1,256]{1,0:T(1,128)} %get-tuple-element.38, f32[6,256]{1,0:T(8,128)} %copy-done.25), dimensions={0} | concatenate | bytes 147456 | tf_op jit(solution)/shard_map/concatenate | solution.py:469
  31.7 0.0 collective-permute-start.2
  31.7 0.0 copy-start.16
  31.7 0.8 %copy-done.16 = s32[1024,8]{0,1:T(8,128)S(1)} copy-done((s32[1024,8]{0,1:T(8,128)S(1)}, s32[1024,8]{0,1:T(8,128)}, u32[]{:S(2)}) %copy-start.16) | copy-done | bytes 32792
  32.5 0.7 %copy-done.24 = s32[2]{0:T(128)S(1)} copy-done((s32[2]{0:T(128)S(1)}, s32[2]{0:T(128)}, u32[]{:S(2)}) %copy-start.24) | copy-done | bytes 32
  33.1 3.0 %shard_map.139.acc2_ref = f32[128,16]{1,0:T(8,128)S(1)} custom-call(s32[2]{0:T(128)S(1)} %copy-done.24, f32[64,32,256]{2,1,0:T(8,128)S(1)} %copy-done, f32[1,256]{1,0:T(1,128)S(1)} %bitcast.42, f32[1,256]{1,0:T(1,128)S(1)} %bitcast.46, f32[1,256]{1,0:T(1,128)S(1)} %bitcast.50, s32[32,64]{1,0:T(8,128)S(1)} %bitcast.27, s32[8,1024]{1,0:T(8,128)S(1)} %bitcast.31, ...), custom_call_target="tpu_custom_call" | custom-call | flops 1073741824 | bytes 2097152 | tf_op jit(solution)/shard_map/pallas_call | solution.py:176
  36.1 0.0 collective-permute-done.3.xhigh_ref
  36.1 1.6 %collective-permute-done.2.xlow_ref = f32[72,256]{1,0:T(8,128)S(1)} collective-permute-done((f32[72,256]{1,0:T(8,128)}, f32[72,256]{1,0:T(8,128)S(1)}, u32[]{:S(2)}, u32[]{:S(2)}) %collective-permute-start.2) | collective-permute-done | bytes 73760 | tf_op jit(solution)/shard_map/ppermute | solution.py:473
  37.8 0.0 copy-done.6
  37.8 3.2 %shard_map.141 = f32[2,16,32]{2,1,0:T(8,128)} custom-call(f32[64,32,256]{2,1,0:T(8,128)S(1)} %copy-done, f32[4,64,256]{2,1,0:T(8,128)S(1)} %copy-done.6, f32[4,64,256]{2,1,0:T(8,128)S(1)} %copy-done.7, f32[128,256]{1,0:T(8,128)S(1)} %collective-permute-done.ylow_ref, f32[128,256]{1,0:T(8,128)S(1)} %collective-permute-done.1.yhigh_ref, ...), custom_call_target="tpu_custom_call" | custom-call | flops 268435456 | bytes 2097152 | tf_op jit(solution)/shard_map/pallas_call | solution.py:403
  (30 shorter events, 0.1 us)
Async XLA Ops:
  0.0 2.4 %copy-start = (f32[64,32,256]{2,1,0:T(8,128)S(1)}, f32[64,32,256]{2,1,0:T(8,128)}, u32[]{:S(2)}) copy-start(f32[64,32,256]{2,1,0:T(8,128)} %air_ref.9) | copy-start | bytes 6291460
  0.0 2.4 %copy-start.12 = (s32[64,32]{0,1:T(8,128)S(1)}, s32[64,32]{0,1:T(8,128)}, u32[]{:S(2)}) copy-start(s32[64,32]{0,1:T(8,128)} %param.20) | copy-start | bytes 24580
  0.0 2.4 %copy-start.21 = (f32[256]{0:T(256)S(1)}, f32[256]{0:T(256)}, u32[]{:S(2)}) copy-start(f32[256]{0:T(256)} %param.15) | copy-start | bytes 3076
  0.0 2.4 %copy-start.22 = (f32[256]{0:T(256)S(1)}, f32[256]{0:T(256)}, u32[]{:S(2)}) copy-start(f32[256]{0:T(256)} %param.16) | copy-start | bytes 3076
  0.0 2.4 %copy-start.23 = (f32[256]{0:T(256)S(1)}, f32[256]{0:T(256)}, u32[]{:S(2)}) copy-start(f32[256]{0:T(256)} %param.17) | copy-start | bytes 3076
  0.0 2.4 %copy-start.20 = (f32[512]{0:T(512)S(1)}, f32[512]{0:T(512)}, u32[]{:S(2)}) copy-start(f32[512]{0:T(512)} %param.26) | copy-start | bytes 6148
  2.5 1.0 %copy-start.2 = (bf16[256,512]{1,0:T(8,128)(2,1)S(1)}, bf16[256,512]{1,0:T(8,128)(2,1)}, u32[]{:S(2)}) copy-start(bf16[256,512]{1,0:T(8,128)(2,1)} %w1_ref.7) | copy-start | bytes 786436
  3.4 0.9 %copy-start.4 = (bf16[512,256]{1,0:T(8,128)(2,1)S(1)}, bf16[512,256]{1,0:T(8,128)(2,1)}, u32[]{:S(2)}) copy-start(bf16[512,256]{1,0:T(8,128)(2,1)} %w2_ref.7) | copy-start | bytes 786436
  4.4 0.8 %copy-start.14 = (s32[1024,8]{0,1:T(8,128)S(1)}, s32[1024,8]{0,1:T(8,128)}, u32[]{:S(2)}) copy-start(s32[1024,8]{0,1:T(8,128)} %param.19) | copy-start | bytes 98308
  5.1 5.7 %copy-start.27 = (f32[128,256]{1,0:T(8,128)S(1)}, f32[128,256]{1,0:T(8,128)}, u32[]{:S(2)}) copy-start(f32[128,256]{1,0:T(8,128)} %get-tuple-element.23) | copy-start | bytes 393220
  5.1 7.6 %copy-start.26 = (f32[128,256]{1,0:T(8,128)S(1)}, f32[128,256]{1,0:T(8,128)}, u32[]{:S(2)}) copy-start(f32[128,256]{1,0:T(8,128)} %get-tuple-element.24) | copy-start | bytes 393220
  5.1 9.7 %copy-start.3 = (bf16[256,512]{1,0:T(8,128)(2,1)S(1)}, bf16[256,512]{1,0:T(8,128)(2,1)}, u32[]{:S(2)}) copy-start(bf16[256,512]{1,0:T(8,128)(2,1)} %w1_ref.7) | copy-start | bytes 786436
  5.1 9.7 %copy-start.5 = (bf16[512,256]{1,0:T(8,128)(2,1)S(1)}, bf16[512,256]{1,0:T(8,128)(2,1)}, u32[]{:S(2)}) copy-start(bf16[512,256]{1,0:T(8,128)(2,1)} %w2_ref.7) | copy-start | bytes 786436
  5.1 9.7 %copy-start.15 = (s32[1024,8]{0,1:T(8,128)S(1)}, s32[1024,8]{0,1:T(8,128)}, u32[]{:S(2)}) copy-start(s32[1024,8]{0,1:T(8,128)} %param.19) | copy-start | bytes 98308
  10.2 0.6 %copy-start.8 = (f32[128,16]{1,0:T(8,128)}, f32[128,16]{1,0:T(8,128)S(1)}, u32[]{:S(2)}) copy-start(f32[128,16]{1,0:T(8,128)S(1)} %shard_map.138.acc0_ref) | copy-start | bytes 24580
  10.9 11.2 %collective-permute-start = (f32[128,256]{1,0:T(8,128)S(1)}, f32[128,256]{1,0:T(8,128)S(1)}, u32[]{:S(2)}, u32[]{:S(2)}) collective-permute-start(f32[128,256]{1,0:T(8,128)S(1)} %copy-done.27), channel_id=1, source_target_pairs={{7,0},{0,1},{1,2},{2,3},{3,4},{4,5},{5,6},{6,7},{15,8},{8,9},{9,10... | collective-permute-start | bytes 393224 | tf_op jit(solution)/shard_map/ppermute | solution.py:464
  12.8 9.3 %collective-permute-start.1 = (f32[128,256]{1,0:T(8,128)S(1)}, f32[128,256]{1,0:T(8,128)S(1)}, u32[]{:S(2)}, u32[]{:S(2)}) collective-permute-start(f32[128,256]{1,0:T(8,128)S(1)} %copy-done.26), channel_id=1, source_target_pairs={{1,0},{2,1},{3,2},{4,3},{5,4},{6,5},{7,6},{0,7},{9,8},{10,9},{11,1... | collective-permute-start | bytes 393224 | tf_op jit(solution)/shard_map/ppermute | solution.py:465
  14.1 5.8 %copy-start.1 = (f32[2,80,32,16]{1,3,2,0:T(8,128)S(1)}, f32[2,80,32,16]{1,3,2,0:T(8,128)}, u32[]{:S(2)}) copy-start(f32[2,80,32,16]{1,3,2,0:T(8,128)} %param.22) | copy-start | bytes 983044
  14.1 5.8 %copy-start.13 = (f32[80,80]{1,0:T(8,128)S(1)}, f32[80,80]{1,0:T(8,128)}, u32[]{:S(2)}) copy-start(f32[80,80]{1,0:T(8,128)} %mixing_ref.1) | copy-start | bytes 76804
  14.1 5.8 %copy-start.17 = (f32[2,32,16]{1,2,0:T(8,128)S(1)}, f32[2,32,16]{1,2,0:T(8,128)}, u32[]{:S(2)}) copy-start(f32[2,32,16]{1,2,0:T(8,128)} %param.23) | copy-start | bytes 12292
  14.1 5.8 %copy-start.18 = (f32[64,32]{0,1:T(8,128)S(1)}, f32[64,32]{0,1:T(8,128)}, u32[]{:S(2)}) copy-start(f32[64,32]{0,1:T(8,128)} %param.18) | copy-start | bytes 24580
  14.1 5.9 %copy-start.19 = (s32[32,16]{0,1:T(8,128)S(1)}, s32[32,16]{0,1:T(8,128)}, u32[]{:S(2)}) copy-start(s32[32,16]{0,1:T(8,128)} %param.21) | copy-start | bytes 6148
  19.9 2.2 %copy-start.10 = (f32[128,16]{1,0:T(8,128)}, f32[128,16]{1,0:T(8,128)S(1)}, u32[]{:S(2)}) copy-start(f32[128,16]{1,0:T(8,128)S(1)} %shard_map.137.acc1_ref) | copy-start | bytes 24580
  22.7 0.6 %copy-start.25 = (f32[6,256]{1,0:T(8,128)}, f32[6,256]{1,0:T(8,128)S(1)}, u32[]{:S(2)}) copy-start(f32[6,256]{1,0:T(8,128)S(1)} %broadcast_in_dim.6) | copy-start | bytes 18436
  25.1 12.7 %copy-start.6 = (f32[4,64,256]{2,1,0:T(8,128)S(1)}, f32[4,64,256]{2,1,0:T(8,128)}, u32[]{:S(2)}) copy-start(f32[4,64,256]{2,1,0:T(8,128)} %get-tuple-element.19.low4_ref) | copy-start | bytes 786436
  25.1 12.7 %copy-start.7 = (f32[4,64,256]{2,1,0:T(8,128)S(1)}, f32[4,64,256]{2,1,0:T(8,128)}, u32[]{:S(2)}) copy-start(f32[4,64,256]{2,1,0:T(8,128)} %get-tuple-element.20.high4_ref) | copy-start | bytes 786436
  25.1 11.1 %collective-permute-start.3 = (f32[72,256]{1,0:T(8,128)}, f32[72,256]{1,0:T(8,128)S(1)}, u32[]{:S(2)}, u32[]{:S(2)}) collective-permute-start(f32[72,256]{1,0:T(8,128)} %concatenate.7), channel_id=1, source_target_pairs={{8,0},{9,1},{10,2},{11,3},{12,4},{13,5},{14,6},{15,7},{16,8},{17,9... | collective-permute-start | bytes 221192 | tf_op jit(solution)/shard_map/ppermute | solution.py:474
  31.7 6.1 %copy-start.9 = (f32[128,16]{1,0:T(8,128)S(1)}, f32[128,16]{1,0:T(8,128)}, u32[]{:S(2)}) copy-start(f32[128,16]{1,0:T(8,128)} %copy-done.8) | copy-start | bytes 24580
  31.7 6.1 %copy-start.11 = (f32[128,16]{1,0:T(8,128)S(1)}, f32[128,16]{1,0:T(8,128)}, u32[]{:S(2)}) copy-start(f32[128,16]{1,0:T(8,128)} %copy-done.10) | copy-start | bytes 24580
  31.7 6.1 %collective-permute-start.2 = (f32[72,256]{1,0:T(8,128)}, f32[72,256]{1,0:T(8,128)S(1)}, u32[]{:S(2)}, u32[]{:S(2)}) collective-permute-start(f32[72,256]{1,0:T(8,128)} %concatenate.6), channel_id=1, source_target_pairs={{120,0},{121,1},{122,2},{123,3},{124,4},{125,5},{126,6},{127,7},{0... | collective-permute-start | bytes 221192 | tf_op jit(solution)/shard_map/ppermute | solution.py:473
  31.7 0.8 %copy-start.16 = (s32[1024,8]{0,1:T(8,128)S(1)}, s32[1024,8]{0,1:T(8,128)}, u32[]{:S(2)}) copy-start(s32[1024,8]{0,1:T(8,128)} %param.19) | copy-start | bytes 98308
  32.5 0.7 %copy-start.24 = (s32[2]{0:T(128)S(1)}, s32[2]{0:T(128)}, u32[]{:S(2)}) copy-start(s32[2]{0:T(128)} %pad_add_fusion.2.range_ref) | copy-start | bytes 28

commit v2 on v0

v2 whole, which is shorter than its diff:
```python
import jax
import jax.numpy as jnp
from jax import lax
from jax.experimental import pallas as pl
from jax.experimental.pallas import tpu as pltpu
from jax.sharding import PartitionSpec as P

BS = 4
PAIRS = 6
THERMAL_FACTOR = 0.8
WETNESS_FACTOR = 0.6
OCEAN_STEP = 0.1
TANH_SCALE = 0.7978845608028654
TANH_CUBE = 0.044715

GROUPS = 5
TILES = 3
LANES = 128
NT = (((1,), (1,)), ((), ()))
F32 = jnp.float32
BF16 = jnp.bfloat16
AXES = ("sect", "gx", "gy")


def iota(shape, dim):
    return lax.broadcasted_iota(jnp.int32, shape, dim)


def combine(coefs, centre, plus_x, minus_x, plus_y, minus_y):
    c0, cxp, cxm, cyp, cym = coefs
    return c0 * centre + cxp * plus_x + cxm * minus_x + cyp * plus_y + cym * minus_y


def advance(block, coefs):
    centre = block[1:-1]
    size = centre.shape[1]
    plus_y = pltpu.roll(centre, size - 1, 1)
    minus_y = pltpu.roll(centre, 1, 1)
    return combine(coefs, centre, block[2:], block[:-2], plus_y, minus_y)


def lanes_of(half):
    return pl.ds(half * LANES, LANES)


def coefs_of(coef_ref, half):
    return [coef_ref[i : i + 1, lanes_of(half)] for i in range(5)]


def hidden_of(state, w1, bias):
    inputs = jnp.concatenate([part.astype(BF16) for part in state], 1)
    half = jnp.dot(inputs, w1, preferred_element_type=F32) + bias
    inner = half * (half * half * (8.0 * TANH_SCALE * TANH_CUBE) + 2.0 * TANH_SCALE)
    return (half * jnp.tanh(inner) + half).astype(BF16)


def physics(state, counts, matrices):
    w1, bias, w2, w2_last = matrices
    for index in range(3):
        delta = jnp.dot(hidden_of(state, w1, bias), w2, preferred_element_type=F32)
        parts = [delta[:, :LANES], delta[:, LANES:]]
        if index:
            needed = counts > float(index)
            parts = [jnp.where(needed, part, 0.0) for part in parts]
        state = [old + part for old, part in zip(state, parts)]
    delta = jnp.dot(hidden_of(state, w1, bias), w2_last, preferred_element_type=F32)
    lane = iota((1, LANES), 1)
    kept = jnp.where(lane == 0, state[0], pltpu.roll(state[1], 1, 1))
    return kept + jnp.where(counts > 3.0, delta, 0.0)


def expand_counts(row):
    square = (LANES, LANES)
    diagonal = jnp.where(iota(square, 0) == iota(square, 1), row, 0.0).astype(BF16)
    return jnp.dot(diagonal, jnp.ones(square, BF16), preferred_element_type=F32)


def split(row):
    high = row.astype(BF16).astype(F32)
    return high, row - high


def one_hots(cells):
    n = cells.shape[1]
    first = iota((32, n), 0) == jnp.right_shift(cells, 4)
    second = (iota((16, n), 0) == jnp.bitwise_and(cells, 15)) & (cells >= 0)
    return first, second.astype(F32).astype(BF16)


def scatter(values, first, second):
    rows = []
    for value in values:
        for part in split(value):
            rows.append(jnp.where(first, part, 0.0))
    stacked = jnp.concatenate(rows, 0).astype(BF16)
    return lax.dot_general(stacked, second, NT, preferred_element_type=F32)


def scatter_columns(kept, cells):
    n = kept.shape[0]
    rows = [jnp.transpose(kept[i : i + LANES])[:2] for i in range(0, n, LANES)]
    flat = jnp.concatenate(rows, 1)
    first, second = one_hots(cells)
    return scatter([flat[0:1], flat[1:2]], first, second)


def column_codes(idx_ref, inc_ref):
    gx = lax.axis_index("gx")
    start = pl.multiple_of((gx // 2) * LANES, LANES)
    block = inc_ref[:, pl.ds(start, LANES)].astype(F32)
    block = jnp.where(gx % 2 == 1, pltpu.roll(block, 64, 1), block)
    spread = (iota((32, 8), 0) // BS == iota((32, 8), 1)).astype(F32)
    counts = jnp.dot(spread.astype(BF16), block.astype(BF16), preferred_element_type=F32)
    cells = idx_ref[...].astype(F32)
    return jnp.concatenate([cells, jnp.zeros_like(cells)], 1) * 8.0 + counts


def group_rows(idx_ref, inc_ref, turned, cell_ref, count_ref):
    code = column_codes(idx_ref, inc_ref)
    turned[...] = jnp.transpose(jnp.concatenate([code, jnp.zeros((96, LANES), F32)], 0))
    count = GROUPS * TILES
    parts = [turned[pl.ds(2 + j, count, stride=4), :][:, :32] for j in range(4)]
    inner = jnp.concatenate(parts, 1)
    along_y = jnp.concatenate([turned[i : i + 1, :][:, :32] for i in (0, 1, 62, 63)], 1)
    along_x = [
        jnp.concatenate([code[i : i + 1, :64], code[i + 1 : i + 2, :64]], 1) for i in (0, 30)
    ]
    y = jnp.bitwise_and(iota((1, LANES), 1), 31)
    keep = (y >= 2) & (y < 30)
    whole = jnp.concatenate([inner, along_y] + along_x, 0).astype(jnp.int32)
    cells = jnp.right_shift(whole, 3)
    masked = (iota(whole.shape, 0) < count + 1) & ((y < 2) | (y >= 30))
    cell_ref[pl.ds(0, count + 3), :] = jnp.where(masked, -1, cells)
    count_ref[pl.ds(0, count + 3), :] = jnp.bitwise_and(whole, 7).astype(F32)


def row_at(ref, index):
    return ref[pl.ds(index, 1), :]


def matrices_of(w1_ref, bias_ref, w2_ref, last_ref):
    return w1_ref[...], bias_ref[...], w2_ref[...], last_ref[...]


def tile_state(air_ref, coef_ref, tile):
    state = []
    for half in range(2):
        block = air_ref[half, pl.ds(tile * (4 * GROUPS), 4 * GROUPS + 4)]
        coefs = coefs_of(coef_ref, half)
        state.append(advance(advance(block, coefs), coefs).reshape(GROUPS * LANES, LANES))
    return state


def finish(state, groups, matrices, cell_ref, count_ref):
    needs = [expand_counts(row_at(count_ref, g)) for g in groups]
    kept = physics(state, jnp.concatenate(needs, 0), matrices)
    cells = jnp.concatenate([row_at(cell_ref, g) for g in groups], 1)
    return scatter_columns(kept, cells)


def tiles(lo, hi, air_ref, coef_ref, matrix_refs, cell_ref, count_ref, acc_ref):
    @pl.loop(lo, hi)
    def _(tile):
        state = tile_state(air_ref, coef_ref, tile)
        groups = [tile * GROUPS + g for g in range(GROUPS)]
        acc_ref[...] += finish(state, groups, matrices_of(*matrix_refs), cell_ref, count_ref)


def early_tiles():
    gy = lax.axis_index("gy")
    return jnp.where(gy < 3, 1, 0).astype(jnp.int32)


def is_even(axis):
    return lax.axis_index(axis) % 2 == 0


def load_kernel(
    air_in, spread_in, east_in, north_in, land_in, inc_in, idx_in, water_in, ocean_in, driver_in,
    mixing_in, w1_in, bias_in, w2_in,
    send1_ref, send2_ref, air_ref, coef_ref, w1_ref, bias_ref, w2_ref, last_ref,
    cell_ref, count_ref, acc_ref, land_ref, idx_ref, water_ref, ocean_ref, driver_ref, mixing_ref,
    inc_ref, numbers, raw_bias, raw_w1, turned, sem,
):
    used = []

    def fetch(source, target):
        copy = pltpu.make_async_copy(source, target, sem.at[len(used)])
        copy.start()
        used.append(copy)
        return copy

    def rows(lo, size):
        return [
            fetch(
                air_in.at[:, pl.ds(lo, size), lanes_of(half)],
                air_ref.at[half, :, pl.ds(lo, size), :],
            )
            for half in range(2)
        ]

    prep = [fetch(inc_in, inc_ref), fetch(idx_in, idx_ref)]
    low = rows(0, 8)
    high = rows(24, 8)
    rest = rows(8, 16)
    rest += [
        fetch(w1_in, raw_w1),
        fetch(w2_in, w2_ref),
        fetch(bias_in, raw_bias),
        fetch(spread_in, numbers.at[pl.ds(0, 1)]),
        fetch(east_in, numbers.at[pl.ds(1, 1)]),
        fetch(north_in, numbers.at[pl.ds(2, 1)]),
        fetch(land_in, land_ref),
        fetch(water_in, water_ref),
        fetch(driver_in, driver_ref),
        fetch(mixing_in, mixing_ref),
        fetch(ocean_in, ocean_ref),
    ]
    for copy in prep:
        copy.wait()
    group_rows(idx_ref, inc_ref, turned, cell_ref, count_ref)
    acc_ref[...] = jnp.zeros_like(acc_ref)
    for copy in low + high:
        copy.wait()
    upper = jnp.where(is_even("gy"), 30, 0)
    for send, first in ((send1_ref, upper), (send2_ref, 30 - upper)):
        for half in range(2):
            flat = air_ref.at[half].reshape(64 * 32, LANES)
            for k in range(2):
                send[pl.ds(k * 64, 64), lanes_of(half)] = flat[pl.ds(first + k, 64, stride=32), :]
    for copy in rest:
        copy.wait()
    w1_ref[...] = raw_w1[...] * jnp.asarray(0.5, BF16)
    bias_ref[...] = raw_bias[...] * 0.5
    spread, east, north = (numbers[i : i + 1] for i in range(3))
    coef_ref[0:1] = 1.0 - 4.0 * spread
    coef_ref[1:2] = spread - 0.5 * east
    coef_ref[2:3] = spread + 0.5 * east
    coef_ref[3:4] = spread - 0.5 * north
    coef_ref[4:5] = spread + 0.5 * north
    lane = iota((1, LANES), 1)
    first = w2_ref[:, :LANES].astype(F32)
    second = pltpu.roll(w2_ref[:, LANES:].astype(F32), 1, 1)
    last_ref[...] = jnp.where(lane == 0, first, jnp.where(lane == 1, second, 0.0)).astype(BF16)
    matrix_refs = (w1_ref, bias_ref, w2_ref, last_ref)
    tiles(
        jnp.int32(0), early_tiles(), air_ref, coef_ref, matrix_refs, cell_ref, count_ref, acc_ref
    )


VMEM = pl.BlockSpec(memory_space=pltpu.VMEM)


def params(size):
    return pltpu.CompilerParams(vmem_limit_bytes=size << 20)


def cost(flops):
    return pl.CostEstimate(flops=flops, bytes_accessed=1 << 20, transcendentals=1 << 10)


def load(arrays):
    shapes = [
        ((LANES, 256), F32),
        ((LANES, 256), F32),
        ((2, 64, 32, LANES), F32),
        ((8, 256), F32),
        ((256, 512), BF16),
        ((1, 512), F32),
        ((512, 256), BF16),
        ((512, LANES), BF16),
        ((24, LANES), jnp.int32),
        ((24, LANES), F32),
        ((LANES, 16), F32),
        ((32, 64), F32),
        ((32, 64), jnp.int32),
        ((16, 32), jnp.int32),
        ((2, 32, 16, 80), F32),
        ((2, 16, 32), F32),
        ((80, 80), F32),
    ]
    return pl.pallas_call(
        load_kernel,
        out_shape=[jax.ShapeDtypeStruct(*shape) for shape in shapes],
        in_specs=[pl.BlockSpec(memory_space=pl.ANY)] * 14,
        out_specs=[VMEM] * len(shapes),
        scratch_shapes=[
            pltpu.VMEM((8, 1024), jnp.int32),
            pltpu.VMEM((8, 256), F32),
            pltpu.VMEM((1, 512), F32),
            pltpu.VMEM((256, 512), BF16),
            pltpu.VMEM((LANES, LANES), F32),
            pltpu.SemaphoreType.DMA((24,)),
        ],
        compiler_params=params(24),
        cost_estimate=cost(1 << 20),
    )(*[pltpu.with_memory_space_constraint(array, pltpu.HBM) for array in arrays])


def ocean_fields(water, driver_ref, ocean_ref, mixing_ref):
    levels = mixing_ref.shape[0]
    wide = jnp.concatenate([mixing_ref[...], jnp.zeros((levels, LANES - levels), F32)], 1)
    tall = jnp.concatenate([wide, jnp.zeros((LANES - levels, LANES), F32)], 0)
    turned = jnp.transpose(tall)
    column = (iota((LANES, 1), 0) == 0).astype(F32)
    total = jnp.zeros((1, 1), F32)

    def pair(_, carry):
        column, total = carry
        row = jnp.sum(column * tall, axis=0, keepdims=True)
        total = total + row[:, 0:1]
        column = jnp.sum(turned * row, axis=1, keepdims=True)
        return column, total + column[0:1]

    column, total = lax.fori_loop(0, PAIRS, pair, (column, total))
    row = jnp.transpose(jnp.broadcast_to(column, (LANES, LANES)))[0:1, :levels]
    fields = []
    for field in range(2):
        block = ocean_ref[field]
        mixed = jnp.transpose(jnp.sum(block * row, axis=2))
        mixed = mixed + (OCEAN_STEP * total) * driver_ref[field]
        fields.append(jnp.where(water == 1, mixed, jnp.transpose(block[:, :, 0])))
    return fields


def land_sums(land, cells):
    lands = jnp.concatenate([land[y : y + 1] for y in range(32)], 1)
    places = jnp.concatenate([cells[y : y + 1] for y in range(32)], 1)
    first, second = one_hots(places)
    sums = scatter([lands, jnp.tanh(lands)], first, second)
    ones = first.astype(F32).astype(BF16)
    return sums, lax.dot_general(ones, second, NT, preferred_element_type=F32)


def middle_kernel(
    air_ref, coef_ref, w1_ref, bias_ref, w2_ref, last_ref, cell_ref, count_ref, land_ref, idx_ref,
    water_ref, ocean_ref, driver_ref, mixing_ref, acc_ref, side_ref,
):
    water = water_ref[...]
    fields = ocean_fields(water, driver_ref, ocean_ref, mixing_ref)
    sums, count = land_sums(land_ref[...], idx_ref[...])
    land = jnp.transpose(sums[0:32] + sums[32:64])
    warm = jnp.transpose(sums[64:96] + sums[96:128])
    count = jnp.transpose(count)
    side_ref[0] = fields[0]
    side_ref[1] = fields[1]
    side_ref[2] = jnp.where(water == 1, count * fields[0], land)
    side_ref[3] = jnp.where(water == 1, count * jnp.tanh(fields[0]), warm)
    side_ref[4] = jnp.maximum(count, 1.0)
    acc_ref[...] = jnp.zeros_like(acc_ref)
    early = early_tiles()
    matrix_refs = (w1_ref, bias_ref, w2_ref, last_ref)
    tiles(
        early, early + 1, air_ref, coef_ref, matrix_refs, cell_ref, count_ref, acc_ref
    )


def middle(core, others):
    return pl.pallas_call(
        middle_kernel,
        out_shape=[
            jax.ShapeDtypeStruct((LANES, 16), F32),
            jax.ShapeDtypeStruct((5, 16, 32), F32),
        ],
        in_specs=[VMEM] * 14,
        out_specs=[VMEM] * 2,
        compiler_params=params(24),
        cost_estimate=cost(1 << 30),
    )(*core, *others)


def by_side(axis, first, second):
    even = is_even(axis)
    return jnp.where(even, second, first), jnp.where(even, first, second)


def slab_kernel(air_ref, recv1_ref, recv2_ref, pair_ref, cross_ref):
    even = is_even("gx")
    ylow, yhigh = by_side("gy", recv1_ref[...], recv2_ref[...])
    for half in range(2):
        lanes = lanes_of(half)
        low = air_ref[half, 0:2].reshape(64, LANES)
        high = air_ref[half, 62:64].reshape(64, LANES)
        pair_ref[0:64, lanes] = jnp.where(even, high, low)
        cross_ref[0:64, lanes] = jnp.where(even, low, high)
    low = jnp.concatenate([ylow[64:65], yhigh[0:1], jnp.zeros((6, 256), F32)], 0)
    high = jnp.concatenate([ylow[127:128], yhigh[63:64], jnp.zeros((6, 256), F32)], 0)
    pair_ref[64:72] = jnp.where(even, high, low)
    cross_ref[64:72] = jnp.where(even, low, high)


def x_slabs(air, recv1, recv2):
    return pl.pallas_call(
        slab_kernel,
        out_shape=[jax.ShapeDtypeStruct((72, 256), F32)] * 2,
        in_specs=[VMEM] * 3,
        out_specs=[VMEM] * 2,
        compiler_params=params(16),
        cost_estimate=cost(1 << 10),
    )(air, recv1, recv2)


def late_kernel(
    air_ref, coef_ref, w1_ref, bias_ref, w2_ref, last_ref, cell_ref, count_ref, acc_ref
):
    acc_ref[...] = jnp.zeros_like(acc_ref)
    matrix_refs = (w1_ref, bias_ref, w2_ref, last_ref)
    tiles(
        early_tiles() + 1, jnp.int32(TILES), air_ref, coef_ref, matrix_refs, cell_ref, count_ref,
        acc_ref,
    )


def late(core):
    return pl.pallas_call(
        late_kernel,
        out_shape=jax.ShapeDtypeStruct((LANES, 16), F32),
        in_specs=[VMEM] * 8,
        out_specs=VMEM,
        compiler_params=params(24),
        cost_estimate=cost(1 << 30),
    )(*core)


def shift_down(block, edge):
    return jnp.where(iota(block.shape, 1) == 0, edge, pltpu.roll(block, 1, 1))


def shift_up(block, edge):
    size = block.shape[1]
    return jnp.where(iota(block.shape, 1) == size - 1, edge, pltpu.roll(block, size - 1, 1))


def y_edge_state(half, air_ref, coefs, ylow, yhigh, before, after, low_corner, high_corner):
    flat = air_ref.at[half].reshape(64 * 32, LANES)

    def column(halo, corner, inner, at, low_side):
        far, near = (0, 1) if low_side else (1, 0)
        minus_y = corner[0:1] if at == 0 else halo[near, at - 1 : at]
        plus_y = corner[1:2] if at == 31 else halo[near, at + 1 : at + 2]
        centre = halo[near, at : at + 1]
        outer = halo[far, at : at + 1]
        plus_x, minus_x = (inner, outer) if low_side else (outer, inner)
        return combine(coefs, centre, plus_x, minus_x, plus_y, minus_y)

    def step(block, left, right):
        centre = block[1:-1]
        plus_x = shift_up(centre, jnp.stack(right, 0))
        minus_x = shift_down(centre, jnp.stack(left, 0))
        return combine(coefs, centre, plus_x, minus_x, block[2:], block[:-2])

    states = []
    for low in (True, False):
        ys = range(4) if low else range(28, 32)
        own = jnp.stack([flat[pl.ds(y, 64, stride=32), :] for y in ys], 0)
        if low:
            block = jnp.concatenate([ylow, own], 0)
            left = [low_corner[0:1]] + [before[1, y : y + 1] for y in (0, 1, 2)]
            right = [high_corner[0:1]] + [after[0, y : y + 1] for y in (0, 1, 2)]
            targets = (0, 1)
        else:
            block = jnp.concatenate([own, yhigh], 0)
            left = [before[1, y : y + 1] for y in (29, 30, 31)] + [low_corner[1:2]]
            right = [after[0, y : y + 1] for y in (29, 30, 31)] + [high_corner[1:2]]
            targets = (30, 31)
        block = step(block, left, right)
        left = [column(before, low_corner, air_ref[half, 0, y : y + 1, :], y, True) for y in targets]
        right = [
            column(after, high_corner, air_ref[half, 63, y : y + 1, :], y, False) for y in targets
        ]
        states.append(step(block, left, right).reshape(LANES, LANES))
    return jnp.concatenate(states, 0)


def x_edge_state(half, air_ref, coefs, before, after):
    low = jnp.concatenate([before, air_ref[half, 0:4]], 0)
    high = jnp.concatenate([air_ref[half, 60:64], after], 0)
    ends = [advance(advance(block, coefs), coefs).reshape(64, LANES) for block in (low, high)]
    return jnp.concatenate(ends, 0)


def edge_kernel(
    air_ref, coef_ref, w1_ref, bias_ref, w2_ref, last_ref, cell_ref, count_ref, recv1_ref,
    recv2_ref, pair_ref, cross_ref, side_ref, acc0_ref, acc1_ref, acc2_ref, out_ref,
):
    state = []
    for half in range(2):
        lanes = lanes_of(half)
        coefs = coefs_of(coef_ref, half)
        ylow, yhigh = by_side("gy", recv1_ref[:, lanes], recv2_ref[:, lanes])
        xlow, xhigh = by_side("gx", pair_ref[:, lanes], cross_ref[:, lanes])
        before = xlow[:64].reshape(2, 32, LANES)
        after = xhigh[:64].reshape(2, 32, LANES)
        by_x = y_edge_state(
            half,
            air_ref,
            coefs,
            ylow.reshape(2, 64, LANES),
            yhigh.reshape(2, 64, LANES),
            before,
            after,
            xlow[64:66],
            xhigh[64:66],
        )
        by_y = x_edge_state(half, air_ref, coefs, before, after)
        state.append(jnp.concatenate([by_y, by_x], 0))
    groups = [GROUPS * TILES + g for g in range(3)]
    matrices = matrices_of(w1_ref, bias_ref, w2_ref, last_ref)
    acc = finish(state, groups, matrices, cell_ref, count_ref)
    acc = acc + (acc0_ref[...] + acc1_ref[...] + acc2_ref[...])
    heat = jnp.transpose(acc[0:32] + acc[32:64])
    vapour = jnp.transpose(acc[64:96] + acc[96:128])
    below = side_ref[4]
    ocean = lax.axis_index("sect") == 1
    flux = THERMAL_FACTOR * (side_ref[2] - heat) / below
    out_ref[0] = jnp.where(ocean, side_ref[0], flux)
    flux = WETNESS_FACTOR * (side_ref[3] - vapour) / below
    out_ref[1] = jnp.where(ocean, side_ref[1], flux)


def edges(core, halos, others):
    return pl.pallas_call(
        edge_kernel,
        out_shape=jax.ShapeDtypeStruct((2, 16, 32), F32),
        in_specs=[VMEM] * 16,
        out_specs=VMEM,
        compiler_params=params(24),
        cost_estimate=cost(1 << 28),
    )(*core, *halos, *others)


def exchanges(axis, first):
    sizes = [lax.axis_size(name) for name in AXES]
    size = lax.axis_size(axis)
    pairs = []
    for device in range(sizes[0] * sizes[1] * sizes[2]):
        at = [device // (sizes[1] * sizes[2]), device // sizes[2] % sizes[1], device % sizes[2]]
        dim = AXES.index(axis)
        step = 1 if (at[dim] - first) % 2 == 0 else -1
        at[dim] = (at[dim] + step) % size
        pairs.append((device, (at[0] * sizes[1] + at[1]) * sizes[2] + at[2]))
    return pairs


def shards(
    air_profile_matrix,
    spreading_numbers,
    eastward_advection_number,
    northward_advection_number,
    landmass_warmth,
    physics_increments,
    underlying_water_index,
    water_indicator,
    waterbody_profiles,
    waterbody_drivers,
    inverted_blending_matrix,
    entry_layer_matrix,
    entry_layer_offset,
    exit_layer_matrix,
):
    loaded = load(
        (
            air_profile_matrix,
            spreading_numbers.reshape(1, -1),
            eastward_advection_number.reshape(1, -1),
            northward_advection_number.reshape(1, -1),
            landmass_warmth.T,
            physics_increments.T,
            underlying_water_index.T,
            water_indicator.T,
            waterbody_profiles.transpose(0, 2, 3, 1),
            waterbody_drivers.transpose(0, 2, 1),
            inverted_blending_matrix,
            entry_layer_matrix,
            entry_layer_offset.reshape(1, -1),
            exit_layer_matrix,
        )
    )
    send1, send2 = loaded[:2]
    core = loaded[2:10]
    acc0 = loaded[10]
    recv1 = lax.ppermute(send1, AXES, exchanges("gy", 0))
    recv2 = lax.ppermute(send2, AXES, exchanges("gy", 1))
    acc1, sides = middle(core, loaded[11:])
    acc1, recv1, recv2 = lax.optimization_barrier((acc1, recv1, recv2))
    send_pair, send_cross = x_slabs(core[0], recv1, recv2)
    cross = lax.ppermute(send_cross, AXES, exchanges("gx", 1))
    pair = lax.ppermute(send_pair, AXES, exchanges("gx", 0))
    acc2 = late(core)
    acc2, pair, cross = lax.optimization_barrier((acc2, pair, cross))
    result = edges(core, (recv1, recv2, pair, cross), (sides, acc0, acc1, acc2))
    return result.transpose(0, 2, 1)[None]


def solution(mesh):
    in_specs = (
        P("gx", "gy", None),
        P(),
        P(),
        P(),
        P("gx", "gy"),
        P(None, "gy"),
        P("gx", "gy"),
        P("gx", "gy"),
        P(None, None, "gx", "gy"),
        P(None, "gx", "gy"),
        P(),
        P(),
        P(),
        P(),
    )
    out_specs = P("sect", None, "gx", "gy")
    return jax.shard_map(shards, mesh=mesh, in_specs=in_specs, out_specs=out_specs, check_vma=False)
```

time: 131 us -> 24.5 us (0.19)
  the two profiles are of different devices: /device:TPU:0 before, /device:TPU:96 now
where the time goes in v2:
time: 24.5 us; the launch traced here: 24.4 us
  Pallas kernels  15 us (61%)
  starting transfers between devices  8.37 us (34%)
  waiting for transfers between devices  0.97 us (4%)
    pallas_call x1, Pallas kernels, late(): pl.pallas_call(late_kernel, out_shape=jax.ShapeDtypeStruct((LANES, 16), F...  5.56 us
    ppermute x1, starting transfers between devices, shards(): cross = lax.ppermute(send_cross, AXES, exchanges('gx', 1))  4.04 us
    pallas_call x1, Pallas kernels, middle(): pl.pallas_call(middle_kernel, out_shape=[jax.ShapeDtypeStruct((LANES, 16)...  3.96 us
    pallas_call x1, Pallas kernels, edges(): pl.pallas_call(edge_kernel, out_shape=jax.ShapeDtypeStruct((2, 16, 32), F...  3.16 us
    ppermute x1, starting transfers between devices, shards(): recv1 = lax.ppermute(send1, AXES, exchanges('gy', 0))  2.98 us
    pallas_call x1, Pallas kernels, load(): pl.pallas_call(load_kernel, out_shape=[jax.ShapeDtypeStruct(*shape) for s...  2.28 us
    ppermute x1, starting transfers between devices, shards(): recv2 = lax.ppermute(send2, AXES, exchanges('gy', 1))  1.26 us
    ppermute x1, waiting for transfers between devices, shards(): recv2 = lax.ppermute(send2, AXES, exchanges('gy', 1))  0.96 us
  transfers between devices with their start and end apart: 4, of which 1 were waited for; matrix products, arithmetic and copies ran while one was open for 0% of the time, Pallas kernels for 39%

profile of v2, /device:TPU:96, one launch (start us, length us, event | category | flops | bytes accessed | tf_op | source)
XLA Modules:
  0.0 24.4 jit_solution(6241908595009159399)
XLA Ops:
  0.0 2.3 %shard_map.136 = (f32[128,256]{1,0:T(8,128)S(1)}, f32[128,256]{1,0:T(8,128)S(1)}, f32[2,64,32,128]{3,2,1,0:T(8,128)S(1)}, f32[8,256]{1,0:T(8,128)S(1)}, bf16[256...) custom-call(f32[64,32,256]{2,1,0:T(8,128)} %air_in.1, ...), custom_call_target="tpu_custom_call" | custom-call | flops 1048576 | bytes 1048576 | tf_op jit(solution)/shard_map/pallas_call | solution.py:282
  2.3 3.0 %collective-permute-start = (f32[128,256]{1,0:T(8,128)S(1)}, f32[128,256]{1,0:T(8,128)S(1)}, u32[]{:S(2)}, u32[]{:S(2)}) collective-permute-start(f32[128,256]{1,0:T(8,128)S(1)} %get-tuple-element.47), channel_id=1, source_target_pairs={{0,1},{1,0},{2,3},{3,2},{4,5},{5,4},{6,7},{7,6},{8,9},{9,8},{10,11... | collective-permute-start | bytes 393224 | tf_op jit(solution)/shard_map/ppermute | solution.py:582
  5.3 1.3 %collective-permute-start.1 = (f32[128,256]{1,0:T(8,128)S(1)}, f32[128,256]{1,0:T(8,128)S(1)}, u32[]{:S(2)}, u32[]{:S(2)}) collective-permute-start(f32[128,256]{1,0:T(8,128)S(1)} %get-tuple-element.48), channel_id=1, source_target_pairs={{0,7},{1,2},{2,1},{3,4},{4,3},{5,6},{6,5},{7,0},{8,15},{9,10},{10,... | collective-permute-start | bytes 393224 | tf_op jit(solution)/shard_map/ppermute | solution.py:583
  6.5 4.0 %shard_map.137 = (f32[128,16]{1,0:T(8,128)S(1)}, f32[5,16,32]{2,1,0:T(8,128)S(1)}) custom-call(f32[2,64,32,128]{3,2,1,0:T(8,128)S(1)} %get-tuple-element.32.air_ref, f32[8,256]{1,0:T(8,128)S(1)} %get-tuple-element.33.coef_ref, bf16[256,512]{1,0:T(8,128)(2,1)S(1)} %get-tuple-element.34.w1_ref, f32[1,512]{1,0:T(1,128)S(1)} %get-tuple-element.35.bias_ref, ...), custom_call_target="tpu_custom_call" | custom-call | flops 1073741824 | bytes 1048576 | tf_op jit(solution)/shard_map/pallas_call | solution.py:359
  10.5 0.0 collective-permute-done.recv1_ref
  10.5 1.0 %collective-permute-done.1.recv2_ref = f32[128,256]{1,0:T(8,128)S(1)} collective-permute-done((f32[128,256]{1,0:T(8,128)S(1)}, f32[128,256]{1,0:T(8,128)S(1)}, u32[]{:S(2)}, u32[]{:S(2)}) %collective-permute-start.1) | collective-permute-done | bytes 131104 | tf_op jit(solution)/shard_map/ppermute | solution.py:583
  11.5 0.1 collective-permute-start.2
  11.6 4.0 %collective-permute-start.3 = (f32[72,256]{1,0:T(8,128)S(1)}, f32[72,256]{1,0:T(8,128)S(1)}, u32[]{:S(2)}, u32[]{:S(2)}) collective-permute-start(f32[72,256]{1,0:T(8,128)S(1)} %get-tuple-element.52), channel_id=1, source_target_pairs={{0,120},{1,121},{2,122},{3,123},{4,124},{5,125},{6,126},{7,127},{8... | collective-permute-start | bytes 221192 | tf_op jit(solution)/shard_map/ppermute | solution.py:587
  15.6 5.6 %shard_map.138.acc2_ref = f32[128,16]{1,0:T(8,128)S(1)} custom-call(f32[2,64,32,128]{3,2,1,0:T(8,128)S(1)} %get-tuple-element.32.air_ref, f32[8,256]{1,0:T(8,128)S(1)} %get-tuple-element.33.coef_ref, bf16[256,512]{1,0:T(8,128)(2,1)S(1)} %get-tuple-element.34.w1_ref, f32[1,512]{1,0:T(1,128)S(1)} %get-tuple-element.35.bias_ref, ...), custom_call_target="tpu_custom_call" | custom-call | flops 1073741824 | bytes 1048576 | tf_op jit(solution)/shard_map/pallas_call | solution.py:415
  21.2 0.0 collective-permute-done.2.pair_ref
  21.2 0.0 collective-permute-done.3.cross_ref
  21.2 3.2 %shard_map.140 = f32[2,16,32]{2,1,0:T(8,128)} custom-call(f32[2,64,32,128]{3,2,1,0:T(8,128)S(1)} %get-tuple-element.32.air_ref, f32[8,256]{1,0:T(8,128)S(1)} %get-tuple-element.33.coef_ref, bf16[256,512]{1,0:T(8,128)(2,1)S(1)} %get-tuple-element.34.w1_ref, f32[1,512]{1,0:T(1,128)S(1)} %get-tuple-element.35.bias_ref, ...), custom_call_target="tpu_custom_call" | custom-call | flops 268435456 | bytes 1048576 | tf_op jit(solution)/shard_map/pallas_call | solution.py:522
  (1 shorter events, 0.0 us)
Async XLA Ops:
  2.3 8.2 %collective-permute-start = (f32[128,256]{1,0:T(8,128)S(1)}, f32[128,256]{1,0:T(8,128)S(1)}, u32[]{:S(2)}, u32[]{:S(2)}) collective-permute-start(f32[128,256]{1,0:T(8,128)S(1)} %get-tuple-element.47), channel_id=1, source_target_pairs={{0,1},{1,0},{2,3},{3,2},{4,5},{5,4},{6,7},{7,6},{8,9},{9,8},{10,11... | collective-permute-start | bytes 393224 | tf_op jit(solution)/shard_map/ppermute | solution.py:582
  5.3 6.2 %collective-permute-start.1 = (f32[128,256]{1,0:T(8,128)S(1)}, f32[128,256]{1,0:T(8,128)S(1)}, u32[]{:S(2)}, u32[]{:S(2)}) collective-permute-start(f32[128,256]{1,0:T(8,128)S(1)} %get-tuple-element.48), channel_id=1, source_target_pairs={{0,7},{1,2},{2,1},{3,4},{4,3},{5,6},{6,5},{7,0},{8,15},{9,10},{10,... | collective-permute-start | bytes 393224 | tf_op jit(solution)/shard_map/ppermute | solution.py:583
  11.5 9.7 %collective-permute-start.2 = (f32[72,256]{1,0:T(8,128)S(1)}, f32[72,256]{1,0:T(8,128)S(1)}, u32[]{:S(2)}, u32[]{:S(2)}) collective-permute-start(f32[72,256]{1,0:T(8,128)S(1)} %get-tuple-element.51), channel_id=1, source_target_pairs={{0,8},{1,9},{2,10},{3,11},{4,12},{5,13},{6,14},{7,15},{8,0},{9,1},... | collective-permute-start | bytes 221192 | tf_op jit(solution)/shard_map/ppermute | solution.py:588
  11.6 9.6 %collective-permute-start.3 = (f32[72,256]{1,0:T(8,128)S(1)}, f32[72,256]{1,0:T(8,128)S(1)}, u32[]{:S(2)}, u32[]{:S(2)}) collective-permute-start(f32[72,256]{1,0:T(8,128)S(1)} %get-tuple-element.52), channel_id=1, source_target_pairs={{0,120},{1,121},{2,122},{3,123},{4,124},{5,125},{6,126},{7,127},{8... | collective-permute-start | bytes 221192 | tf_op jit(solution)/shard_map/ppermute | solution.py:587

commit v3 on v2

--- a/solution.py
+++ b/solution.py
@@ -15,6 +15,8 @@
 
 GROUPS = 5
 TILES = 3
+TILE_CHUNKS = (320, 320)
+EDGE_CHUNKS = (384,)
 LANES = 128
 NT = (((1,), (1,)), ((), ()))
 F32 = jnp.float32
@@ -54,19 +56,28 @@
     return (half * jnp.tanh(inner) + half).astype(BF16)
 
 
-def physics(state, counts, matrices):
+def physics(state, counts, matrices, sizes):
     w1, bias, w2, w2_last = matrices
+    places = [sum(sizes[:i]) for i in range(len(sizes))]
+    states = [[part[at : at + n] for part in state] for at, n in zip(places, sizes)]
+    counts = [counts[at : at + n] for at, n in zip(places, sizes)]
+    lane = iota((1, LANES), 1)
     for index in range(3):
-        delta = jnp.dot(hidden_of(state, w1, bias), w2, preferred_element_type=F32)
-        parts = [delta[:, :LANES], delta[:, LANES:]]
-        if index:
-            needed = counts > float(index)
-            parts = [jnp.where(needed, part, 0.0) for part in parts]
-        state = [old + part for old, part in zip(state, parts)]
-    delta = jnp.dot(hidden_of(state, w1, bias), w2_last, preferred_element_type=F32)
-    lane = iota((1, LANES), 1)
-    kept = jnp.where(lane == 0, state[0], pltpu.roll(state[1], 1, 1))
-    return kept + jnp.where(counts > 3.0, delta, 0.0)
+        for chunk, needs in enumerate(counts):
+            hidden = hidden_of(states[chunk], w1, bias)
+            delta = jnp.dot(hidden, w2, preferred_element_type=F32)
+            parts = [delta[:, :LANES], delta[:, LANES:]]
+            if index:
+                needed = needs > float(index)
+                parts = [jnp.where(needed, part, 0.0) for part in parts]
+            states[chunk] = [old + part for old, part in zip(states[chunk], parts)]
+    kept = []
+    for (first, second), needs in zip(states, counts):
+        hidden = hidden_of([first, second], w1, bias)
+        delta = jnp.dot(hidden, w2_last, preferred_element_type=F32)
+        both = jnp.where(lane == 0, first, pltpu.roll(second, 1, 1))
+        kept.append(both + jnp.where(needs > 3.0, delta, 0.0))
+    return jnp.concatenate(kept, 0)
 
 
 def expand_counts(row):
@@ -125,11 +136,12 @@
     along_x = [
         jnp.concatenate([code[i : i + 1, :64], code[i + 1 : i + 2, :64]], 1) for i in (0, 30)
     ]
-    y = jnp.bitwise_and(iota((1, LANES), 1), 31)
-    keep = (y >= 2) & (y < 30)
-    whole = jnp.concatenate([inner, along_y] + along_x, 0).astype(jnp.int32)
+    whole = jnp.concatenate([inner] + along_x + [along_y], 0).astype(jnp.int32)
     cells = jnp.right_shift(whole, 3)
-    masked = (iota(whole.shape, 0) < count + 1) & ((y < 2) | (y >= 30))
+    row = iota(whole.shape, 0)
+    place = jnp.bitwise_and(iota(whole.shape, 1), jnp.where(row < count, 31, 63))
+    masked = (place < 2) | (place >= jnp.where(row < count, 30, 62))
+    masked = masked & (row < count + 2)
     cell_ref[pl.ds(0, count + 3), :] = jnp.where(masked, -1, cells)
     count_ref[pl.ds(0, count + 3), :] = jnp.bitwise_and(whole, 7).astype(F32)
 
@@ -151,9 +163,9 @@
     return state
 
 
-def finish(state, groups, matrices, cell_ref, count_ref):
+def finish(state, groups, matrices, cell_ref, count_ref, sizes):
     needs = [expand_counts(row_at(count_ref, g)) for g in groups]
-    kept = physics(state, jnp.concatenate(needs, 0), matrices)
+    kept = physics(state, jnp.concatenate(needs, 0), matrices, sizes)
     cells = jnp.concatenate([row_at(cell_ref, g) for g in groups], 1)
     return scatter_columns(kept, cells)
 
@@ -163,24 +175,35 @@
     def _(tile):
         state = tile_state(air_ref, coef_ref, tile)
         groups = [tile * GROUPS + g for g in range(GROUPS)]
-        acc_ref[...] += finish(state, groups, matrices_of(*matrix_refs), cell_ref, count_ref)
+        matrices = matrices_of(*matrix_refs)
+        acc_ref[...] += finish(state, groups, matrices, cell_ref, count_ref, TILE_CHUNKS)
 
 
 def early_tiles():
     gy = lax.axis_index("gy")
-    return jnp.where(gy < 3, 1, 0).astype(jnp.int32)
+    return jnp.where(gy < 4, 1, 0).astype(jnp.int32)
+
+
+def middle_tiles():
+    late = lax.axis_index("gy") >= 4
+    return jnp.where(late & (lax.axis_index("gx") % 8 == 1), 2, 1).astype(jnp.int32)
 
 
 def is_even(axis):
     return lax.axis_index(axis) % 2 == 0
+
+
+def side_turn():
+    gy = lax.axis_index("gy")
+    return jnp.where(gy == 0, 0, 1)
 
 
 def load_kernel(
     air_in, spread_in, east_in, north_in, land_in, inc_in, idx_in, water_in, ocean_in, driver_in,
     mixing_in, w1_in, bias_in, w2_in,
     send1_ref, send2_ref, air_ref, coef_ref, w1_ref, bias_ref, w2_ref, last_ref,
-    cell_ref, count_ref, acc_ref, land_ref, idx_ref, water_ref, ocean_ref, driver_ref, mixing_ref,
-    inc_ref, numbers, raw_bias, raw_w1, turned, sem,
+    cell_ref, count_ref, acc_ref, side_ref, land_ref, idx_ref, water_ref, ocean_ref, driver_ref,
+    mixing_ref, inc_ref, numbers, raw_bias, raw_w1, turned, sem,
 ):
     used = []
 
@@ -202,24 +225,26 @@
     prep = [fetch(inc_in, inc_ref), fetch(idx_in, idx_ref)]
     low = rows(0, 8)
     high = rows(24, 8)
-    rest = rows(8, 16)
-    rest += [
+    layers = [
         fetch(w1_in, raw_w1),
         fetch(w2_in, w2_ref),
         fetch(bias_in, raw_bias),
         fetch(spread_in, numbers.at[pl.ds(0, 1)]),
         fetch(east_in, numbers.at[pl.ds(1, 1)]),
         fetch(north_in, numbers.at[pl.ds(2, 1)]),
+    ]
+    rest = rows(8, 16)
+    rest += [
         fetch(land_in, land_ref),
         fetch(water_in, water_ref),
         fetch(driver_in, driver_ref),
         fetch(mixing_in, mixing_ref),
         fetch(ocean_in, ocean_ref),
     ]
+    acc_ref[...] = jnp.zeros_like(acc_ref)
     for copy in prep:
         copy.wait()
     group_rows(idx_ref, inc_ref, turned, cell_ref, count_ref)
-    acc_ref[...] = jnp.zeros_like(acc_ref)
     for copy in low + high:
         copy.wait()
     upper = jnp.where(is_even("gy"), 30, 0)
@@ -228,7 +253,7 @@
             flat = air_ref.at[half].reshape(64 * 32, LANES)
             for k in range(2):
                 send[pl.ds(k * 64, 64), lanes_of(half)] = flat[pl.ds(first + k, 64, stride=32), :]
-    for copy in rest:
+    for copy in layers:
         copy.wait()
     w1_ref[...] = raw_w1[...] * jnp.asarray(0.5, BF16)
     bias_ref[...] = raw_bias[...] * 0.5
@@ -242,6 +267,10 @@
     first = w2_ref[:, :LANES].astype(F32)
     second = pltpu.roll(w2_ref[:, LANES:].astype(F32), 1, 1)
     last_ref[...] = jnp.where(lane == 0, first, jnp.where(lane == 1, second, 0.0)).astype(BF16)
+    for copy in rest:
+        copy.wait()
+    side_refs = (land_ref, idx_ref, water_ref, ocean_ref, driver_ref, mixing_ref)
+    side_parts(0, side_refs, side_ref)
     matrix_refs = (w1_ref, bias_ref, w2_ref, last_ref)
     tiles(
         jnp.int32(0), early_tiles(), air_ref, coef_ref, matrix_refs, cell_ref, count_ref, acc_ref
@@ -272,6 +301,7 @@
         ((24, LANES), jnp.int32),
         ((24, LANES), F32),
         ((LANES, 16), F32),
+        ((5, 16, 32), F32),
         ((32, 64), F32),
         ((32, 64), jnp.int32),
         ((16, 32), jnp.int32),
@@ -332,27 +362,34 @@
     return sums, lax.dot_general(ones, second, NT, preferred_element_type=F32)
 
 
+def side_parts(turn, refs, side_ref):
+    land_ref, idx_ref, water_ref, ocean_ref, driver_ref, mixing_ref = refs
+
+    @pl.when(side_turn() == turn)
+    def _():
+        water = water_ref[...]
+        fields = ocean_fields(water, driver_ref, ocean_ref, mixing_ref)
+        sums, count = land_sums(land_ref[...], idx_ref[...])
+        land = jnp.transpose(sums[0:32] + sums[32:64])
+        warm = jnp.transpose(sums[64:96] + sums[96:128])
+        count = jnp.transpose(count)
+        side_ref[0] = fields[0]
+        side_ref[1] = fields[1]
+        side_ref[2] = jnp.where(water == 1, count * fields[0], land)
+        side_ref[3] = jnp.where(water == 1, count * jnp.tanh(fields[0]), warm)
+        side_ref[4] = jnp.maximum(count, 1.0)
+
+
 def middle_kernel(
     air_ref, coef_ref, w1_ref, bias_ref, w2_ref, last_ref, cell_ref, count_ref, land_ref, idx_ref,
     water_ref, ocean_ref, driver_ref, mixing_ref, acc_ref, side_ref,
 ):
-    water = water_ref[...]
-    fields = ocean_fields(water, driver_ref, ocean_ref, mixing_ref)
-    sums, count = land_sums(land_ref[...], idx_ref[...])
-    land = jnp.transpose(sums[0:32] + sums[32:64])
-    warm = jnp.transpose(sums[64:96] + sums[96:128])
-    count = jnp.transpose(count)
-    side_ref[0] = fields[0]
-    side_ref[1] = fields[1]
-    side_ref[2] = jnp.where(water == 1, count * fields[0], land)
-    side_ref[3] = jnp.where(water == 1, count * jnp.tanh(fields[0]), warm)
-    side_ref[4] = jnp.maximum(count, 1.0)
+    side_refs = (land_ref, idx_ref, water_ref, ocean_ref, driver_ref, mixing_ref)
+    side_parts(1, side_refs, side_ref)
     acc_ref[...] = jnp.zeros_like(acc_ref)
     early = early_tiles()
     matrix_refs = (w1_ref, bias_ref, w2_ref, last_ref)
-    tiles(
-        early, early + 1, air_ref, coef_ref, matrix_refs, cell_ref, count_ref, acc_ref
-    )
+    tiles(early, early + middle_tiles(), air_ref, coef_ref, matrix_refs, cell_ref, count_ref, acc_ref)
 
 
 def middle(core, others):
@@ -405,10 +442,8 @@
 ):
     acc_ref[...] = jnp.zeros_like(acc_ref)
     matrix_refs = (w1_ref, bias_ref, w2_ref, last_ref)
-    tiles(
-        early_tiles() + 1, jnp.int32(TILES), air_ref, coef_ref, matrix_refs, cell_ref, count_ref,
-        acc_ref,
-    )
+    first = early_tiles() + middle_tiles()
+    tiles(first, jnp.int32(TILES), air_ref, coef_ref, matrix_refs, cell_ref, count_ref, acc_ref)
 
 
 def late(core):
@@ -422,107 +457,110 @@
     )(*core)
 
 
-def shift_down(block, edge):
-    return jnp.where(iota(block.shape, 1) == 0, edge, pltpu.roll(block, 1, 1))
-
-
-def shift_up(block, edge):
-    size = block.shape[1]
-    return jnp.where(iota(block.shape, 1) == size - 1, edge, pltpu.roll(block, size - 1, 1))
-
-
-def y_edge_state(half, air_ref, coefs, ylow, yhigh, before, after, low_corner, high_corner):
+def y_edge_state(half, air_ref, coefs, ylow, yhigh):
     flat = air_ref.at[half].reshape(64 * 32, LANES)
 
-    def column(halo, corner, inner, at, low_side):
-        far, near = (0, 1) if low_side else (1, 0)
-        minus_y = corner[0:1] if at == 0 else halo[near, at - 1 : at]
-        plus_y = corner[1:2] if at == 31 else halo[near, at + 1 : at + 2]
-        centre = halo[near, at : at + 1]
-        outer = halo[far, at : at + 1]
-        plus_x, minus_x = (inner, outer) if low_side else (outer, inner)
-        return combine(coefs, centre, plus_x, minus_x, plus_y, minus_y)
-
-    def step(block, left, right):
+    def step(block):
         centre = block[1:-1]
-        plus_x = shift_up(centre, jnp.stack(right, 0))
-        minus_x = shift_down(centre, jnp.stack(left, 0))
+        plus_x = pltpu.roll(centre, 63, 1)
+        minus_x = pltpu.roll(centre, 1, 1)
         return combine(coefs, centre, plus_x, minus_x, block[2:], block[:-2])
 
     states = []
     for low in (True, False):
         ys = range(4) if low else range(28, 32)
         own = jnp.stack([flat[pl.ds(y, 64, stride=32), :] for y in ys], 0)
-        if low:
-            block = jnp.concatenate([ylow, own], 0)
-            left = [low_corner[0:1]] + [before[1, y : y + 1] for y in (0, 1, 2)]
-            right = [high_corner[0:1]] + [after[0, y : y + 1] for y in (0, 1, 2)]
-            targets = (0, 1)
-        else:
-            block = jnp.concatenate([own, yhigh], 0)
-            left = [before[1, y : y + 1] for y in (29, 30, 31)] + [low_corner[1:2]]
-            right = [after[0, y : y + 1] for y in (29, 30, 31)] + [high_corner[1:2]]
-            targets = (30, 31)
-        block = step(block, left, right)
-        left = [column(before, low_corner, air_ref[half, 0, y : y + 1, :], y, True) for y in targets]
-        right = [
-            column(after, high_corner, air_ref[half, 63, y : y + 1, :], y, False) for y in targets
-        ]
-        states.append(step(block, left, right).reshape(LANES, LANES))
-    return jnp.concatenate(states, 0)
-
-
-def x_edge_state(half, air_ref, coefs, before, after):
-    low = jnp.concatenate([before, air_ref[half, 0:4]], 0)
-    high = jnp.concatenate([air_ref[half, 60:64], after], 0)
-    ends = [advance(advance(block, coefs), coefs).reshape(64, LANES) for block in (low, high)]
-    return jnp.concatenate(ends, 0)
+        halo = (ylow if low else yhigh).reshape(2, 64, LANES)
+        block = jnp.concatenate([halo, own] if low else [own, halo], 0)
+        states.append(step(step(block)).reshape(LANES, LANES))
+    return states
+
+
+def x_edge_state(half, air_ref, coefs, ylow, yhigh, xlow, xhigh):
+    def with_ends(row, first, last):
+        at = iota(row.shape, 0)
+        size = row.shape[0]
+        plus_y = jnp.where(at == size - 1, last, pltpu.roll(row, size - 1, 0))
+        minus_y = jnp.where(at == 0, first, pltpu.roll(row, 1, 0))
+        return plus_y, minus_y
+
+    def own(x):
+        return air_ref[half, x]
+
+    def beyond(x, y):
+        slab = ylow if y < 0 else yhigh
+        at = (y + 2 if y < 0 else y - 32) * 64 + x
+        return slab[at : at + 1]
+
+    done = []
+    for low in (True, False):
+        halo = xlow if low else xhigh
+        near, far = (halo[32:64], halo[0:32]) if low else (halo[0:32], halo[32:64])
+        xs = [0, 1, 2, 3] if low else [63, 62, 61, 60]
+        rows = [far, near] + [own(x) for x in xs]
+        ends = [None, (halo[64:65], halo[65:66])] + [(beyond(x, -1), beyond(x, 32)) for x in xs]
+        outer = [None, None] + [(beyond(x, -2), beyond(x, 33)) for x in xs]
+
+        def apply(centre, outward, inward, plus_y, minus_y):
+            plus_x, minus_x = (inward, outward) if low else (outward, inward)
+            return combine(coefs, centre, plus_x, minus_x, plus_y, minus_y)
+
+        once = {}
+        for i in range(1, 5):
+            plus_y, minus_y = with_ends(rows[i], *ends[i])
+            once[i] = apply(rows[i], rows[i - 1], rows[i + 1], plus_y, minus_y)
+        twice = []
+        for i in (2, 3):
+            first = apply(
+                ends[i][0], ends[i - 1][0], ends[i + 1][0], rows[i][0:1], outer[i][0]
+            )
+            last = apply(
+                ends[i][1], ends[i - 1][1], ends[i + 1][1], outer[i][1], rows[i][31:32]
+            )
+            plus_y, minus_y = with_ends(once[i], first, last)
+            twice.append(apply(once[i], once[i - 1], once[i + 1], plus_y, minus_y))
+        done += twice if low else twice[::-1]
+    return jnp.concatenate(done, 0)
 
 
 def edge_kernel(
     air_ref, coef_ref, w1_ref, bias_ref, w2_ref, last_ref, cell_ref, count_ref, recv1_ref,
-    recv2_ref, pair_ref, cross_ref, side_ref, acc0_ref, acc1_ref, acc2_ref, out_ref,
+    recv2_ref, pair_ref, cross_ref, acc0_ref, acc1_ref, acc2_ref, side0_ref, side1_ref,
+    out_ref,
 ):
     state = []
     for half in range(2):
         lanes = lanes_of(half)
-        coefs = coefs_of(coef_ref, half)
         ylow, yhigh = by_side("gy", recv1_ref[:, lanes], recv2_ref[:, lanes])
         xlow, xhigh = by_side("gx", pair_ref[:, lanes], cross_ref[:, lanes])
-        before = xlow[:64].reshape(2, 32, LANES)
-        after = xhigh[:64].reshape(2, 32, LANES)
-        by_x = y_edge_state(
-            half,
-            air_ref,
-            coefs,
-            ylow.reshape(2, 64, LANES),
-            yhigh.reshape(2, 64, LANES),
-            before,
-            after,
-            xlow[64:66],
-            xhigh[64:66],
-        )
-        by_y = x_edge_state(half, air_ref, coefs, before, after)
-        state.append(jnp.concatenate([by_y, by_x], 0))
+        coefs = coefs_of(coef_ref, half)
+        along_x = y_edge_state(half, air_ref, coefs, ylow, yhigh)
+        along_y = x_edge_state(half, air_ref, coefs, ylow, yhigh, xlow, xhigh)
+        state.append(jnp.concatenate(along_x + [along_y], 0))
+    matrices = matrices_of(w1_ref, bias_ref, w2_ref, last_ref)
     groups = [GROUPS * TILES + g for g in range(3)]
-    matrices = matrices_of(w1_ref, bias_ref, w2_ref, last_ref)
-    acc = finish(state, groups, matrices, cell_ref, count_ref)
+    acc = finish(state, groups, matrices, cell_ref, count_ref, EDGE_CHUNKS)
     acc = acc + (acc0_ref[...] + acc1_ref[...] + acc2_ref[...])
     heat = jnp.transpose(acc[0:32] + acc[32:64])
     vapour = jnp.transpose(acc[64:96] + acc[96:128])
-    below = side_ref[4]
+    turn = side_turn()
+
+    def side(index):
+        return jnp.where(turn == 0, side0_ref[index], side1_ref[index])
+
+    below = side(4)
     ocean = lax.axis_index("sect") == 1
-    flux = THERMAL_FACTOR * (side_ref[2] - heat) / below
-    out_ref[0] = jnp.where(ocean, side_ref[0], flux)
-    flux = WETNESS_FACTOR * (side_ref[3] - vapour) / below
-    out_ref[1] = jnp.where(ocean, side_ref[1], flux)
+    flux = THERMAL_FACTOR * (side(2) - heat) / below
+    out_ref[0] = jnp.where(ocean, side(0), flux)
+    flux = WETNESS_FACTOR * (side(3) - vapour) / below
+    out_ref[1] = jnp.where(ocean, side(1), flux)
 
 
 def edges(core, halos, others):
     return pl.pallas_call(
         edge_kernel,
         out_shape=jax.ShapeDtypeStruct((2, 16, 32), F32),
-        in_specs=[VMEM] * 16,
+        in_specs=[VMEM] * 17,
         out_specs=VMEM,
         compiler_params=params(24),
         cost_estimate=cost(1 << 28),
@@ -578,17 +616,19 @@
     )
     send1, send2 = loaded[:2]
     core = loaded[2:10]
-    acc0 = loaded[10]
+    acc0, side0 = loaded[10:12]
     recv1 = lax.ppermute(send1, AXES, exchanges("gy", 0))
     recv2 = lax.ppermute(send2, AXES, exchanges("gy", 1))
-    acc1, sides = middle(core, loaded[11:])
+    acc1, side1 = middle(core, loaded[12:])
     acc1, recv1, recv2 = lax.optimization_barrier((acc1, recv1, recv2))
     send_pair, send_cross = x_slabs(core[0], recv1, recv2)
     cross = lax.ppermute(send_cross, AXES, exchanges("gx", 1))
     pair = lax.ppermute(send_pair, AXES, exchanges("gx", 0))
     acc2 = late(core)
-    acc2, pair, cross = lax.optimization_barrier((acc2, pair, cross))
-    result = edges(core, (recv1, recv2, pair, cross), (sides, acc0, acc1, acc2))
+    acc2, cross, pair = lax.optimization_barrier((acc2, cross, pair))
+    result = edges(
+        core, (recv1, recv2, pair, cross), (acc0, acc1, acc2, side0, side1)
+    )
     return result.transpose(0, 2, 1)[None]
 
 

time: 24.5 us -> 22.6 us (0.922)
  the two profiles are of different devices: /device:TPU:96 before, /device:TPU:4 now
where the time goes in v3:
time: 22.6 us; the launch traced here: 22.2 us
  Pallas kernels  14.9 us (66%)
  starting transfers between devices  4.58 us (20%)
  waiting for transfers between devices  2.69 us (12%)
    pallas_call x1, Pallas kernels, load(): pl.pallas_call(load_kernel, out_shape=[jax.ShapeDtypeStruct(*shape) for s...  6.3 us
    pallas_call x1, Pallas kernels, edges(): pl.pallas_call(edge_kernel, out_shape=jax.ShapeDtypeStruct((2, 16, 32), F...  3.15 us
    pallas_call x1, Pallas kernels, late(): pl.pallas_call(late_kernel, out_shape=jax.ShapeDtypeStruct((LANES, 16), F...  2.71 us
    pallas_call x1, Pallas kernels, middle(): pl.pallas_call(middle_kernel, out_shape=[jax.ShapeDtypeStruct((LANES, 16)...  2.71 us
    ppermute x1, starting transfers between devices, shards(): recv2 = lax.ppermute(send2, AXES, exchanges('gy', 1))  2.24 us
    ppermute x1, starting transfers between devices, shards(): cross = lax.ppermute(send_cross, AXES, exchanges('gx', 1))  1.74 us
    ppermute x1, waiting for transfers between devices, shards(): cross = lax.ppermute(send_cross, AXES, exchanges('gx', 1))  1.47 us
    ppermute x1, waiting for transfers between devices, shards(): recv2 = lax.ppermute(send2, AXES, exchanges('gy', 1))  1.21 us
  transfers between devices with their start and end apart: 4, of which 2 were waited for; matrix products, arithmetic and copies ran while one was open for 0% of the time, Pallas kernels for 24%

profile of v3, /device:TPU:4, one launch (start us, length us, event | category | flops | bytes accessed | tf_op | source)
XLA Modules:
  0.0 22.2 jit_solution(14871684434565001711)
XLA Ops:
  0.0 6.3 %shard_map.136 = (f32[128,256]{1,0:T(8,128)S(1)}, f32[128,256]{1,0:T(8,128)S(1)}, f32[2,64,32,128]{3,2,1,0:T(8,128)S(1)}, f32[8,256]{1,0:T(8,128)S(1)}, bf16[256...) custom-call(f32[64,32,256]{2,1,0:T(8,128)} %air_in.1, ...), custom_call_target="tpu_custom_call" | custom-call | flops 1048576 | bytes 1048576 | tf_op jit(solution)/shard_map/pallas_call | solution.py:312
  6.3 0.6 %collective-permute-start = (f32[128,256]{1,0:T(8,128)S(1)}, f32[128,256]{1,0:T(8,128)S(1)}, u32[]{:S(2)}, u32[]{:S(2)}) collective-permute-start(f32[128,256]{1,0:T(8,128)S(1)} %get-tuple-element.48), channel_id=1, source_target_pairs={{0,1},{1,0},{2,3},{3,2},{4,5},{5,4},{6,7},{7,6},{8,9},{9,8},{10,11... | collective-permute-start | bytes 393224 | tf_op jit(solution)/shard_map/ppermute | solution.py:620
  6.9 2.2 %collective-permute-start.1 = (f32[128,256]{1,0:T(8,128)S(1)}, f32[128,256]{1,0:T(8,128)S(1)}, u32[]{:S(2)}, u32[]{:S(2)}) collective-permute-start(f32[128,256]{1,0:T(8,128)S(1)} %get-tuple-element.49), channel_id=1, source_target_pairs={{0,7},{1,2},{2,1},{3,4},{4,3},{5,6},{6,5},{7,0},{8,15},{9,10},{10,... | collective-permute-start | bytes 393224 | tf_op jit(solution)/shard_map/ppermute | solution.py:621
  9.1 2.7 %shard_map.137 = (f32[128,16]{1,0:T(8,128)S(1)}, f32[5,16,32]{2,1,0:T(8,128)S(1)}) custom-call(f32[2,64,32,128]{3,2,1,0:T(8,128)S(1)} %get-tuple-element.33.air_ref, f32[8,256]{1,0:T(8,128)S(1)} %get-tuple-element.34.coef_ref, bf16[256,512]{1,0:T(8,128)(2,1)S(1)} %get-tuple-element.35.w1_ref, f32[1,512]{1,0:T(1,128)S(1)} %get-tuple-element.36.bias_ref, ...), custom_call_target="tpu_custom_call" | custom-call | flops 1073741824 | bytes 1048576 | tf_op jit(solution)/shard_map/pallas_call | solution.py:396
  11.8 0.0 collective-permute-done.recv1_ref
  11.8 1.2 %collective-permute-done.1.recv2_ref = f32[128,256]{1,0:T(8,128)S(1)} collective-permute-done((f32[128,256]{1,0:T(8,128)S(1)}, f32[128,256]{1,0:T(8,128)S(1)}, u32[]{:S(2)}, u32[]{:S(2)}) %collective-permute-start.1) | collective-permute-done | bytes 131104 | tf_op jit(solution)/shard_map/ppermute | solution.py:621
  13.1 1.7 %collective-permute-start.2 = (f32[72,256]{1,0:T(8,128)S(1)}, f32[72,256]{1,0:T(8,128)S(1)}, u32[]{:S(2)}, u32[]{:S(2)}) collective-permute-start(f32[72,256]{1,0:T(8,128)S(1)} %get-tuple-element.52), channel_id=1, source_target_pairs={{0,120},{1,121},{2,122},{3,123},{4,124},{5,125},{6,126},{7,127},{8... | collective-permute-start | bytes 221192 | tf_op jit(solution)/shard_map/ppermute | solution.py:625
  14.8 0.0 collective-permute-start.3
  14.9 2.7 %shard_map.138.acc2_ref = f32[128,16]{1,0:T(8,128)S(1)} custom-call(f32[2,64,32,128]{3,2,1,0:T(8,128)S(1)} %get-tuple-element.33.air_ref, f32[8,256]{1,0:T(8,128)S(1)} %get-tuple-element.34.coef_ref, bf16[256,512]{1,0:T(8,128)(2,1)S(1)} %get-tuple-element.35.w1_ref, f32[1,512]{1,0:T(1,128)S(1)} %get-tuple-element.36.bias_ref, ...), custom_call_target="tpu_custom_call" | custom-call | flops 1073741824 | bytes 1048576 | tf_op jit(solution)/shard_map/pallas_call | solution.py:450
  17.6 1.5 %collective-permute-done.2.cross_ref = f32[72,256]{1,0:T(8,128)S(1)} collective-permute-done((f32[72,256]{1,0:T(8,128)S(1)}, f32[72,256]{1,0:T(8,128)S(1)}, u32[]{:S(2)}, u32[]{:S(2)}) %collective-permute-start.2) | collective-permute-done | bytes 73760 | tf_op jit(solution)/shard_map/ppermute | solution.py:625
  19.1 0.0 collective-permute-done.3.pair_ref
  19.1 3.2 %shard_map.140 = f32[2,16,32]{2,1,0:T(8,128)} custom-call(f32[2,64,32,128]{3,2,1,0:T(8,128)S(1)} %get-tuple-element.33.air_ref, f32[8,256]{1,0:T(8,128)S(1)} %get-tuple-element.34.coef_ref, bf16[256,512]{1,0:T(8,128)(2,1)S(1)} %get-tuple-element.35.w1_ref, f32[1,512]{1,0:T(1,128)S(1)} %get-tuple-element.36.bias_ref, ...), custom_call_target="tpu_custom_call" | custom-call | flops 268435456 | bytes 1048576 | tf_op jit(solution)/shard_map/pallas_call | solution.py:560
  (1 shorter events, 0.0 us)
Async XLA Ops:
  6.3 5.5 %collective-permute-start = (f32[128,256]{1,0:T(8,128)S(1)}, f32[128,256]{1,0:T(8,128)S(1)}, u32[]{:S(2)}, u32[]{:S(2)}) collective-permute-start(f32[128,256]{1,0:T(8,128)S(1)} %get-tuple-element.48), channel_id=1, source_target_pairs={{0,1},{1,0},{2,3},{3,2},{4,5},{5,4},{6,7},{7,6},{8,9},{9,8},{10,11... | collective-permute-start | bytes 393224 | tf_op jit(solution)/shard_map/ppermute | solution.py:620
  6.9 6.2 %collective-permute-start.1 = (f32[128,256]{1,0:T(8,128)S(1)}, f32[128,256]{1,0:T(8,128)S(1)}, u32[]{:S(2)}, u32[]{:S(2)}) collective-permute-start(f32[128,256]{1,0:T(8,128)S(1)} %get-tuple-element.49), channel_id=1, source_target_pairs={{0,7},{1,2},{2,1},{3,4},{4,3},{5,6},{6,5},{7,0},{8,15},{9,10},{10,... | collective-permute-start | bytes 393224 | tf_op jit(solution)/shard_map/ppermute | solution.py:621
  13.1 6.0 %collective-permute-start.2 = (f32[72,256]{1,0:T(8,128)S(1)}, f32[72,256]{1,0:T(8,128)S(1)}, u32[]{:S(2)}, u32[]{:S(2)}) collective-permute-start(f32[72,256]{1,0:T(8,128)S(1)} %get-tuple-element.52), channel_id=1, source_target_pairs={{0,120},{1,121},{2,122},{3,123},{4,124},{5,125},{6,126},{7,127},{8... | collective-permute-start | bytes 221192 | tf_op jit(solution)/shard_map/ppermute | solution.py:625
  14.8 4.2 %collective-permute-start.3 = (f32[72,256]{1,0:T(8,128)S(1)}, f32[72,256]{1,0:T(8,128)S(1)}, u32[]{:S(2)}, u32[]{:S(2)}) collective-permute-start(f32[72,256]{1,0:T(8,128)S(1)} %get-tuple-element.53), channel_id=1, source_target_pairs={{0,8},{1,9},{2,10},{3,11},{4,12},{5,13},{6,14},{7,15},{8,0},{9,1},... | collective-permute-start | bytes 221192 | tf_op jit(solution)/shard_map/ppermute | solution.py:626

commit v4 on v3

--- a/solution.py
+++ b/solution.py
@@ -181,12 +181,15 @@
 
 def early_tiles():
     gy = lax.axis_index("gy")
-    return jnp.where(gy < 4, 1, 0).astype(jnp.int32)
+    return jnp.where(gy < 3, 1, 0).astype(jnp.int32)
+
+
+def loads_all():
+    return lax.axis_index("gy") < 4
 
 
 def middle_tiles():
-    late = lax.axis_index("gy") >= 4
-    return jnp.where(late & (lax.axis_index("gx") % 8 == 1), 2, 1).astype(jnp.int32)
+    return jnp.where(lax.axis_index("gx") % 8 == 1, 2, 1).astype(jnp.int32)
 
 
 def is_even(axis):
@@ -195,66 +198,50 @@
 
 def side_turn():
     gy = lax.axis_index("gy")
-    return jnp.where(gy == 0, 0, 1)
-
-
-def load_kernel(
-    air_in, spread_in, east_in, north_in, land_in, inc_in, idx_in, water_in, ocean_in, driver_in,
-    mixing_in, w1_in, bias_in, w2_in,
-    send1_ref, send2_ref, air_ref, coef_ref, w1_ref, bias_ref, w2_ref, last_ref,
-    cell_ref, count_ref, acc_ref, side_ref, land_ref, idx_ref, water_ref, ocean_ref, driver_ref,
-    mixing_ref, inc_ref, numbers, raw_bias, raw_w1, turned, sem,
-):
-    used = []
-
-    def fetch(source, target):
-        copy = pltpu.make_async_copy(source, target, sem.at[len(used)])
-        copy.start()
-        used.append(copy)
-        return copy
-
-    def rows(lo, size):
-        return [
-            fetch(
-                air_in.at[:, pl.ds(lo, size), lanes_of(half)],
-                air_ref.at[half, :, pl.ds(lo, size), :],
+    return jnp.where((gy == 0) | (gy == 3), 0, 1)
+
+
+class Copies:
+    def __init__(self, sem, first):
+        self.sem = sem
+        self.next = first
+        self.started = []
+
+    def copy(self, place):
+        index, ends = self.started[place]
+        return pltpu.make_async_copy(*ends(), self.sem.at[index])
+
+    def fetch(self, ends):
+        self.started.append((self.next, ends))
+        self.next += 1
+        self.copy(len(self.started) - 1).start()
+
+    def rows(self, air_in, air_ref, lo, size):
+        for half in range(2):
+            self.fetch(
+                lambda half=half: (
+                    air_in.at[:, pl.ds(lo, size), lanes_of(half)],
+                    air_ref.at[half, :, pl.ds(lo, size), :],
+                )
             )
-            for half in range(2)
-        ]
-
-    prep = [fetch(inc_in, inc_ref), fetch(idx_in, idx_ref)]
-    low = rows(0, 8)
-    high = rows(24, 8)
-    layers = [
-        fetch(w1_in, raw_w1),
-        fetch(w2_in, w2_ref),
-        fetch(bias_in, raw_bias),
-        fetch(spread_in, numbers.at[pl.ds(0, 1)]),
-        fetch(east_in, numbers.at[pl.ds(1, 1)]),
-        fetch(north_in, numbers.at[pl.ds(2, 1)]),
-    ]
-    rest = rows(8, 16)
-    rest += [
-        fetch(land_in, land_ref),
-        fetch(water_in, water_ref),
-        fetch(driver_in, driver_ref),
-        fetch(mixing_in, mixing_ref),
-        fetch(ocean_in, ocean_ref),
-    ]
-    acc_ref[...] = jnp.zeros_like(acc_ref)
-    for copy in prep:
-        copy.wait()
-    group_rows(idx_ref, inc_ref, turned, cell_ref, count_ref)
-    for copy in low + high:
-        copy.wait()
-    upper = jnp.where(is_even("gy"), 30, 0)
-    for send, first in ((send1_ref, upper), (send2_ref, 30 - upper)):
-        for half in range(2):
-            flat = air_ref.at[half].reshape(64 * 32, LANES)
-            for k in range(2):
-                send[pl.ds(k * 64, 64), lanes_of(half)] = flat[pl.ds(first + k, 64, stride=32), :]
-    for copy in layers:
-        copy.wait()
+
+    def wait(self):
+        for place in range(len(self.started)):
+            self.copy(place).wait()
+
+
+def fetch_layers(copies, sources, raw, w2_ref):
+    spread_in, east_in, north_in, w1_in, bias_in, w2_in = sources
+    raw_w1, raw_bias, numbers = raw
+    copies.fetch(lambda: (w1_in, raw_w1))
+    copies.fetch(lambda: (w2_in, w2_ref))
+    copies.fetch(lambda: (bias_in, raw_bias))
+    for row, source in enumerate((spread_in, east_in, north_in)):
+        copies.fetch(lambda row=row, source=source: (source, numbers.at[pl.ds(row, 1)]))
+
+
+def prepare_layers(raw, coef_ref, w1_ref, bias_ref, w2_ref, last_ref):
+    raw_w1, raw_bias, numbers = raw
     w1_ref[...] = raw_w1[...] * jnp.asarray(0.5, BF16)
     bias_ref[...] = raw_bias[...] * 0.5
     spread, east, north = (numbers[i : i + 1] for i in range(3))
@@ -267,14 +254,63 @@
     first = w2_ref[:, :LANES].astype(F32)
     second = pltpu.roll(w2_ref[:, LANES:].astype(F32), 1, 1)
     last_ref[...] = jnp.where(lane == 0, first, jnp.where(lane == 1, second, 0.0)).astype(BF16)
-    for copy in rest:
-        copy.wait()
-    side_refs = (land_ref, idx_ref, water_ref, ocean_ref, driver_ref, mixing_ref)
-    side_parts(0, side_refs, side_ref)
-    matrix_refs = (w1_ref, bias_ref, w2_ref, last_ref)
-    tiles(
-        jnp.int32(0), early_tiles(), air_ref, coef_ref, matrix_refs, cell_ref, count_ref, acc_ref
-    )
+
+
+def load_kernel(
+    air_in, land_in, inc_in, idx_in, water_in, ocean_in, driver_in, mixing_in, spread_in, east_in,
+    north_in, w1_in, bias_in, w2_in,
+    send1_ref, send2_ref, air_ref, coef_ref, w1_ref, bias_ref, w2_ref, last_ref,
+    cell_ref, count_ref, acc_ref, side_ref, idx_ref, land_ref, water_ref, ocean_ref, driver_ref,
+    mixing_ref, inc_ref, numbers, raw_bias, raw_w1, turned, sem,
+):
+    early = loads_all()
+    ours = side_turn() == 0
+    raw = (raw_w1, raw_bias, numbers)
+    columns = Copies(sem, 0)
+    columns.fetch(lambda: (inc_in, inc_ref))
+    columns.fetch(lambda: (idx_in, idx_ref))
+    slabs = Copies(sem, columns.next)
+    slabs.rows(air_in, air_ref, 0, 8)
+    slabs.rows(air_in, air_ref, 24, 8)
+    layers = Copies(sem, slabs.next)
+
+    @pl.when(early)
+    def _():
+        fetch_layers(layers, (spread_in, east_in, north_in, w1_in, bias_in, w2_in), raw, w2_ref)
+        layers.rows(air_in, air_ref, 8, 16)
+
+    others = Copies(sem, layers.next)
+    sides = (land_in, water_in, ocean_in, driver_in, mixing_in)
+    side_refs = (land_ref, water_ref, ocean_ref, driver_ref, mixing_ref)
+
+    for source, target in zip(sides, side_refs):
+        others.fetch(lambda source=source, target=target: (source, target))
+    acc_ref[...] = jnp.zeros_like(acc_ref)
+    columns.wait()
+    group_rows(idx_ref, inc_ref, turned, cell_ref, count_ref)
+    slabs.wait()
+    upper = jnp.where(is_even("gy"), 30, 0)
+    for send, first in ((send1_ref, upper), (send2_ref, 30 - upper)):
+        for half in range(2):
+            flat = air_ref.at[half].reshape(64 * 32, LANES)
+            for k in range(2):
+                send[pl.ds(k * 64, 64), lanes_of(half)] = flat[pl.ds(first + k, 64, stride=32), :]
+
+    others.wait()
+
+    @pl.when(ours)
+    def _():
+        side_parts(idx_ref, side_refs, side_ref)
+
+    @pl.when(early)
+    def _():
+        layers.wait()
+        prepare_layers(raw, coef_ref, w1_ref, bias_ref, w2_ref, last_ref)
+        matrix_refs = (w1_ref, bias_ref, w2_ref, last_ref)
+        tiles(
+            jnp.int32(0), early_tiles(), air_ref, coef_ref, matrix_refs, cell_ref, count_ref,
+            acc_ref,
+        )
 
 
 VMEM = pl.BlockSpec(memory_space=pltpu.VMEM)
@@ -288,62 +324,71 @@
     return pl.CostEstimate(flops=flops, bytes_accessed=1 << 20, transcendentals=1 << 10)
 
 
+SIDE = [
+    ((32, 64), F32),
+    ((16, 32), jnp.int32),
+    ((2, 32, 16, 80), F32),
+    ((2, 16, 32), F32),
+    ((80, 80), F32),
+]
+LAYER_SCRATCH = [
+    pltpu.VMEM((8, 256), F32),
+    pltpu.VMEM((1, 512), F32),
+    pltpu.VMEM((256, 512), BF16),
+]
+CORE = [
+    ((2, 64, 32, LANES), F32),
+    ((8, 256), F32),
+    ((256, 512), BF16),
+    ((1, 512), F32),
+    ((512, 256), BF16),
+    ((512, LANES), BF16),
+]
+
+
+def shapes_of(shapes):
+    return [jax.ShapeDtypeStruct(*shape) for shape in shapes]
+
+
 def load(arrays):
-    shapes = [
-        ((LANES, 256), F32),
-        ((LANES, 256), F32),
-        ((2, 64, 32, LANES), F32),
-        ((8, 256), F32),
-        ((256, 512), BF16),
-        ((1, 512), F32),
-        ((512, 256), BF16),
-        ((512, LANES), BF16),
+    shapes = [((LANES, 256), F32)] * 2 + CORE
+    shapes += [
         ((24, LANES), jnp.int32),
         ((24, LANES), F32),
         ((LANES, 16), F32),
         ((5, 16, 32), F32),
-        ((32, 64), F32),
         ((32, 64), jnp.int32),
-        ((16, 32), jnp.int32),
-        ((2, 32, 16, 80), F32),
-        ((2, 16, 32), F32),
-        ((80, 80), F32),
-    ]
+    ] + SIDE
     return pl.pallas_call(
         load_kernel,
-        out_shape=[jax.ShapeDtypeStruct(*shape) for shape in shapes],
+        out_shape=shapes_of(shapes),
         in_specs=[pl.BlockSpec(memory_space=pl.ANY)] * 14,
         out_specs=[VMEM] * len(shapes),
-        scratch_shapes=[
-            pltpu.VMEM((8, 1024), jnp.int32),
-            pltpu.VMEM((8, 256), F32),
-            pltpu.VMEM((1, 512), F32),
-            pltpu.VMEM((256, 512), BF16),
-            pltpu.VMEM((LANES, LANES), F32),
-            pltpu.SemaphoreType.DMA((24,)),
-        ],
+        scratch_shapes=[pltpu.VMEM((8, 1024), jnp.int32)]
+        + LAYER_SCRATCH
+        + [pltpu.VMEM((LANES, LANES), F32), pltpu.SemaphoreType.DMA((24,))],
         compiler_params=params(24),
         cost_estimate=cost(1 << 20),
-    )(*[pltpu.with_memory_space_constraint(array, pltpu.HBM) for array in arrays])
+    )(*arrays)
 
 
 def ocean_fields(water, driver_ref, ocean_ref, mixing_ref):
     levels = mixing_ref.shape[0]
-    wide = jnp.concatenate([mixing_ref[...], jnp.zeros((levels, LANES - levels), F32)], 1)
+    matrix = mixing_ref[...]
+    wide = jnp.concatenate([matrix, jnp.zeros((levels, LANES - levels), F32)], 1)
     tall = jnp.concatenate([wide, jnp.zeros((LANES - levels, LANES), F32)], 0)
-    turned = jnp.transpose(tall)
-    column = (iota((LANES, 1), 0) == 0).astype(F32)
+    turned = jnp.transpose(tall)[:levels]
+    column = (iota((levels, 1), 0) == 0).astype(F32)
     total = jnp.zeros((1, 1), F32)
-
-    def pair(_, carry):
-        column, total = carry
-        row = jnp.sum(column * tall, axis=0, keepdims=True)
+    for _ in range(PAIRS):
+        row = jnp.sum(column * wide, axis=0, keepdims=True)
         total = total + row[:, 0:1]
         column = jnp.sum(turned * row, axis=1, keepdims=True)
-        return column, total + column[0:1]
-
-    column, total = lax.fori_loop(0, PAIRS, pair, (column, total))
-    row = jnp.transpose(jnp.broadcast_to(column, (LANES, LANES)))[0:1, :levels]
+        total = total + column[0:1]
+    spread = jnp.concatenate(
+        [jnp.broadcast_to(column, (levels, LANES)), jnp.zeros((LANES - levels, LANES), F32)], 0
+    )
+    row = jnp.transpose(spread)[0:1, :levels]
     fields = []
     for field in range(2):
         block = ocean_ref[field]
@@ -362,48 +407,66 @@
     return sums, lax.dot_general(ones, second, NT, preferred_element_type=F32)
 
 
-def side_parts(turn, refs, side_ref):
-    land_ref, idx_ref, water_ref, ocean_ref, driver_ref, mixing_ref = refs
-
-    @pl.when(side_turn() == turn)
+def side_parts(idx_ref, refs, side_ref):
+    land_ref, water_ref, ocean_ref, driver_ref, mixing_ref = refs
+    water = water_ref[...]
+    fields = ocean_fields(water, driver_ref, ocean_ref, mixing_ref)
+    sums, count = land_sums(land_ref[...], idx_ref[...])
+    land = jnp.transpose(sums[0:32] + sums[32:64])
+    warm = jnp.transpose(sums[64:96] + sums[96:128])
+    count = jnp.transpose(count)
+    side_ref[0] = fields[0]
+    side_ref[1] = fields[1]
+    side_ref[2] = jnp.where(water == 1, count * fields[0], land)
+    side_ref[3] = jnp.where(water == 1, count * jnp.tanh(fields[0]), warm)
+    side_ref[4] = jnp.maximum(count, 1.0)
+
+
+def middle_kernel(
+    air_old, coef_old, w1_old, bias_old, w2_old, last_old, cell_ref, count_ref, idx_ref, land_ref,
+    water_ref, ocean_ref, driver_ref, mixing_ref, air_in, spread_in, east_in, north_in, w1_in,
+    bias_in, w2_in,
+    air_ref, coef_ref, w1_ref, bias_ref, w2_ref, last_ref, acc_ref, side_ref,
+    numbers, raw_bias, raw_w1, sem,
+):
+    early = early_tiles()
+    raw = (raw_w1, raw_bias, numbers)
+    layers = Copies(sem, 0)
+
+    @pl.when(jnp.logical_not(loads_all()))
     def _():
-        water = water_ref[...]
-        fields = ocean_fields(water, driver_ref, ocean_ref, mixing_ref)
-        sums, count = land_sums(land_ref[...], idx_ref[...])
-        land = jnp.transpose(sums[0:32] + sums[32:64])
-        warm = jnp.transpose(sums[64:96] + sums[96:128])
-        count = jnp.transpose(count)
-        side_ref[0] = fields[0]
-        side_ref[1] = fields[1]
-        side_ref[2] = jnp.where(water == 1, count * fields[0], land)
-        side_ref[3] = jnp.where(water == 1, count * jnp.tanh(fields[0]), warm)
-        side_ref[4] = jnp.maximum(count, 1.0)
-
-
-def middle_kernel(
-    air_ref, coef_ref, w1_ref, bias_ref, w2_ref, last_ref, cell_ref, count_ref, land_ref, idx_ref,
-    water_ref, ocean_ref, driver_ref, mixing_ref, acc_ref, side_ref,
-):
-    side_refs = (land_ref, idx_ref, water_ref, ocean_ref, driver_ref, mixing_ref)
-    side_parts(1, side_refs, side_ref)
+        fetch_layers(layers, (spread_in, east_in, north_in, w1_in, bias_in, w2_in), raw, w2_ref)
+        layers.rows(air_in, air_ref, 8, 16)
+
+    @pl.when(side_turn() == 1)
+    def _():
+        side_refs = (land_ref, water_ref, ocean_ref, driver_ref, mixing_ref)
+        side_parts(idx_ref, side_refs, side_ref)
+
+    @pl.when(jnp.logical_not(loads_all()))
+    def _():
+        layers.wait()
+        prepare_layers(raw, coef_ref, w1_ref, bias_ref, w2_ref, last_ref)
+
     acc_ref[...] = jnp.zeros_like(acc_ref)
-    early = early_tiles()
     matrix_refs = (w1_ref, bias_ref, w2_ref, last_ref)
-    tiles(early, early + middle_tiles(), air_ref, coef_ref, matrix_refs, cell_ref, count_ref, acc_ref)
-
-
-def middle(core, others):
+    tiles(
+        early, early + middle_tiles(), air_ref, coef_ref, matrix_refs, cell_ref, count_ref, acc_ref
+    )
+
+
+def middle(core, sides, sources):
+    shapes = CORE + [((LANES, 16), F32), ((5, 16, 32), F32)]
     return pl.pallas_call(
         middle_kernel,
-        out_shape=[
-            jax.ShapeDtypeStruct((LANES, 16), F32),
-            jax.ShapeDtypeStruct((5, 16, 32), F32),
-        ],
-        in_specs=[VMEM] * 14,
-        out_specs=[VMEM] * 2,
+        out_shape=shapes_of(shapes),
+        in_specs=[VMEM] * 14 + [pl.BlockSpec(memory_space=pl.ANY)] * 7,
+        out_specs=[VMEM] * len(shapes),
+        input_output_aliases={i: i for i in range(len(CORE))},
+        scratch_shapes=LAYER_SCRATCH + [pltpu.SemaphoreType.DMA((24,))],
         compiler_params=params(24),
         cost_estimate=cost(1 << 30),
-    )(*core, *others)
+    )(*core, *sides, *sources)
 
 
 def by_side(axis, first, second):
@@ -438,26 +501,36 @@
 
 
 def late_kernel(
-    air_ref, coef_ref, w1_ref, bias_ref, w2_ref, last_ref, cell_ref, count_ref, acc_ref
+    air_ref, coef_ref, w1_ref, bias_ref, w2_ref, last_ref, cell_ref, count_ref, recv1_ref,
+    recv2_ref, send1_ref, send2_ref, acc_ref, edge_ref,
 ):
     acc_ref[...] = jnp.zeros_like(acc_ref)
+    for half in range(2):
+        lanes = lanes_of(half)
+        ylow, yhigh = by_side("gy", recv1_ref[:, lanes], recv2_ref[:, lanes])
+        first, last = by_side("gy", send1_ref[:, lanes], send2_ref[:, lanes])
+        along_x = y_edge_state(half, air_ref, coefs_of(coef_ref, half), ylow, yhigh, first, last)
+        edge_ref[half] = jnp.concatenate(along_x, 0)
     matrix_refs = (w1_ref, bias_ref, w2_ref, last_ref)
     first = early_tiles() + middle_tiles()
     tiles(first, jnp.int32(TILES), air_ref, coef_ref, matrix_refs, cell_ref, count_ref, acc_ref)
 
 
-def late(core):
+def late(core, halos):
     return pl.pallas_call(
         late_kernel,
-        out_shape=jax.ShapeDtypeStruct((LANES, 16), F32),
-        in_specs=[VMEM] * 8,
-        out_specs=VMEM,
+        out_shape=[
+            jax.ShapeDtypeStruct((LANES, 16), F32),
+            jax.ShapeDtypeStruct((2, 2 * LANES, LANES), F32),
+        ],
+        in_specs=[VMEM] * 12,
+        out_specs=[VMEM] * 2,
         compiler_params=params(24),
         cost_estimate=cost(1 << 30),
-    )(*core)
-
-
-def y_edge_state(half, air_ref, coefs, ylow, yhigh):
+    )(*core, *halos)
+
+
+def y_edge_state(half, air_ref, coefs, ylow, yhigh, first, last):
     flat = air_ref.at[half].reshape(64 * 32, LANES)
 
     def step(block):
@@ -468,10 +541,11 @@
 
     states = []
     for low in (True, False):
-        ys = range(4) if low else range(28, 32)
-        own = jnp.stack([flat[pl.ds(y, 64, stride=32), :] for y in ys], 0)
+        ys = (2, 3) if low else (28, 29)
+        inner = jnp.stack([flat[pl.ds(y, 64, stride=32), :] for y in ys], 0)
+        outer = (first if low else last).reshape(2, 64, LANES)
         halo = (ylow if low else yhigh).reshape(2, 64, LANES)
-        block = jnp.concatenate([halo, own] if low else [own, halo], 0)
+        block = jnp.concatenate([halo, outer, inner] if low else [inner, outer, halo], 0)
         states.append(step(step(block)).reshape(LANES, LANES))
     return states
 
@@ -525,7 +599,7 @@
 
 def edge_kernel(
     air_ref, coef_ref, w1_ref, bias_ref, w2_ref, last_ref, cell_ref, count_ref, recv1_ref,
-    recv2_ref, pair_ref, cross_ref, acc0_ref, acc1_ref, acc2_ref, side0_ref, side1_ref,
+    recv2_ref, pair_ref, cross_ref, edge_ref, acc0_ref, acc1_ref, acc2_ref, side0_ref, side1_ref,
     out_ref,
 ):
     state = []
@@ -534,9 +608,8 @@
         ylow, yhigh = by_side("gy", recv1_ref[:, lanes], recv2_ref[:, lanes])
         xlow, xhigh = by_side("gx", pair_ref[:, lanes], cross_ref[:, lanes])
         coefs = coefs_of(coef_ref, half)
-        along_x = y_edge_state(half, air_ref, coefs, ylow, yhigh)
         along_y = x_edge_state(half, air_ref, coefs, ylow, yhigh, xlow, xhigh)
-        state.append(jnp.concatenate(along_x + [along_y], 0))
+        state.append(jnp.concatenate([edge_ref[half], along_y], 0))
     matrices = matrices_of(w1_ref, bias_ref, w2_ref, last_ref)
     groups = [GROUPS * TILES + g for g in range(3)]
     acc = finish(state, groups, matrices, cell_ref, count_ref, EDGE_CHUNKS)
@@ -560,7 +633,7 @@
     return pl.pallas_call(
         edge_kernel,
         out_shape=jax.ShapeDtypeStruct((2, 16, 32), F32),
-        in_specs=[VMEM] * 17,
+        in_specs=[VMEM] * 18,
         out_specs=VMEM,
         compiler_params=params(24),
         cost_estimate=cost(1 << 28),
@@ -596,38 +669,42 @@
     entry_layer_offset,
     exit_layer_matrix,
 ):
-    loaded = load(
-        (
-            air_profile_matrix,
-            spreading_numbers.reshape(1, -1),
-            eastward_advection_number.reshape(1, -1),
-            northward_advection_number.reshape(1, -1),
-            landmass_warmth.T,
-            physics_increments.T,
-            underlying_water_index.T,
-            water_indicator.T,
-            waterbody_profiles.transpose(0, 2, 3, 1),
-            waterbody_drivers.transpose(0, 2, 1),
-            inverted_blending_matrix,
-            entry_layer_matrix,
-            entry_layer_offset.reshape(1, -1),
-            exit_layer_matrix,
-        )
+    air = air_profile_matrix
+    sides = (
+        landmass_warmth.T,
+        water_indicator.T,
+        waterbody_profiles.transpose(0, 2, 3, 1),
+        waterbody_drivers.transpose(0, 2, 1),
+        inverted_blending_matrix,
     )
+    layers = (
+        spreading_numbers.reshape(1, -1),
+        eastward_advection_number.reshape(1, -1),
+        northward_advection_number.reshape(1, -1),
+        entry_layer_matrix,
+        entry_layer_offset.reshape(1, -1),
+        exit_layer_matrix,
+    )
+    columns = (physics_increments.T, underlying_water_index.T)
+    air, sides, layers, columns = jax.tree.map(
+        lambda array: pltpu.with_memory_space_constraint(array, pltpu.HBM),
+        (air, sides, layers, columns),
+    )
+    loaded = load((air, sides[0], *columns, *sides[1:], *layers))
     send1, send2 = loaded[:2]
-    core = loaded[2:10]
     acc0, side0 = loaded[10:12]
+    recv2 = lax.ppermute(send2, AXES, exchanges("gy", 1))
     recv1 = lax.ppermute(send1, AXES, exchanges("gy", 0))
-    recv2 = lax.ppermute(send2, AXES, exchanges("gy", 1))
-    acc1, side1 = middle(core, loaded[12:])
-    acc1, recv1, recv2 = lax.optimization_barrier((acc1, recv1, recv2))
+    *core, acc1, side1 = middle(loaded[2:10], loaded[12:], (air, *layers))
+    core += loaded[8:10]
+    acc1, recv2, recv1 = lax.optimization_barrier((acc1, recv2, recv1))
     send_pair, send_cross = x_slabs(core[0], recv1, recv2)
     cross = lax.ppermute(send_cross, AXES, exchanges("gx", 1))
     pair = lax.ppermute(send_pair, AXES, exchanges("gx", 0))
-    acc2 = late(core)
+    acc2, edge = late(core, (recv1, recv2, send1, send2))
     acc2, cross, pair = lax.optimization_barrier((acc2, cross, pair))
     result = edges(
-        core, (recv1, recv2, pair, cross), (acc0, acc1, acc2, side0, side1)
+        core, (recv1, recv2, pair, cross), (edge, acc0, acc1, acc2, side0, side1)
     )
     return result.transpose(0, 2, 1)[None]
 

time: 22.6 us -> 21.5 us (0.951)
  waiting for transfers between devices: 2.69 us -> 1.17 us
  starting transfers between devices: 4.58 us -> 5.07 us
    ppermute x1, waiting for transfers between devices: 1.47 us -> 0.33 us  [shards(): cross = lax.ppermute(send_cross, AXES, exchanges('gx', 1))]
    ppermute x1, starting transfers between devices: 2.24 us -> 1.48 us  [shards(): recv2 = lax.ppermute(send2, AXES, exchanges('gy', 1))]
    ppermute x1, starting transfers between devices: 0.56 us -> 1.29 us  [shards(): recv1 = lax.ppermute(send1, AXES, exchanges('gy', 0))]
    pallas_call x3, Pallas kernels: 11.7 us -> 12.4 us  [the longest x1 6.13 us: load(): pl.pallas_call(load_kernel, out_shape=shapes_of(shapes), in_specs=[pl.Blo...]
    ppermute x1, starting transfers between devices: 1.74 us -> 2.3 us  [shards(): cross = lax.ppermute(send_cross, AXES, exchanges('gx', 1))]
    pallas_call x1, Pallas kernels: 3.15 us -> 2.6 us  [edges(): pl.pallas_call(edge_kernel, out_shape=jax.ShapeDtypeStruct((2, 16, 32), F...]
    ppermute x1, waiting for transfers between devices: 1.21 us -> 0.83 us  [shards(): recv2 = lax.ppermute(send2, AXES, exchanges('gy', 1))]
  transfers between devices with their start and end apart: 4 -> 4, of which waited for: 2 -> 2; matrix products, arithmetic and copies ran while one was open for 0% -> 0% of each run, Pallas kernels for 24% -> 29%
where the time goes in v4:
time: 21.5 us; the launch traced here: 21.3 us
  Pallas kernels  15 us (70%)
  starting transfers between devices  5.07 us (24%)
  waiting for transfers between devices  1.17 us (5%)
    pallas_call x1, Pallas kernels, load(): pl.pallas_call(load_kernel, out_shape=shapes_of(shapes), in_specs=[pl.Blo...  6.13 us
    pallas_call x1, Pallas kernels, late(): pl.pallas_call(late_kernel, out_shape=[jax.ShapeDtypeStruct((LANES, 16),...  3.33 us
    pallas_call x1, Pallas kernels, middle(): pl.pallas_call(middle_kernel, out_shape=shapes_of(shapes), in_specs=[VMEM...  2.92 us
    pallas_call x1, Pallas kernels, edges(): pl.pallas_call(edge_kernel, out_shape=jax.ShapeDtypeStruct((2, 16, 32), F...  2.6 us
    ppermute x1, starting transfers between devices, shards(): cross = lax.ppermute(send_cross, AXES, exchanges('gx', 1))  2.3 us
    ppermute x1, starting transfers between devices, shards(): recv2 = lax.ppermute(send2, AXES, exchanges('gy', 1))  1.48 us
    ppermute x1, starting transfers between devices, shards(): recv1 = lax.ppermute(send1, AXES, exchanges('gy', 0))  1.29 us
    ppermute x1, waiting for transfers between devices, shards(): recv2 = lax.ppermute(send2, AXES, exchanges('gy', 1))  0.83 us
  transfers between devices with their start and end apart: 4, of which 2 were waited for; matrix products, arithmetic and copies ran while one was open for 0% of the time, Pallas kernels for 29%

profile of v4, /device:TPU:4, one launch (start us, length us, event | category | flops | bytes accessed | tf_op | source)
XLA Modules:
  0.0 21.3 jit_solution(9970500652887048970)
XLA Ops:
  0.0 6.1 %shard_map.136 = (f32[128,256]{1,0:T(8,128)S(1)}, f32[128,256]{1,0:T(8,128)S(1)}, f32[2,64,32,128]{3,2,1,0:T(8,128)S(1)}, f32[8,256]{1,0:T(8,128)S(1)}, bf16[256...) custom-call(f32[64,32,256]{2,1,0:T(8,128)} %air_in.3, ...), custom_call_target="tpu_custom_call" | custom-call | flops 1048576 | bytes 1048576 | tf_op jit(solution)/shard_map/pallas_call | solution.py:362
  6.1 1.5 %collective-permute-start = (f32[128,256]{1,0:T(8,128)S(1)}, f32[128,256]{1,0:T(8,128)S(1)}, u32[]{:S(2)}, u32[]{:S(2)}) collective-permute-start(f32[128,256]{1,0:T(8,128)S(1)} %get-tuple-element.62.send2_ref), channel_id=1, source_target_pairs={{0,7},{1,2},{2,1},{3,4},{4,3},{5,6},{6,5},{7,0},{8,15},{9,10},{10,... | collective-permute-start | bytes 393224 | tf_op jit(solution)/shard_map/ppermute | solution.py:696
  7.6 1.3 %collective-permute-start.1 = (f32[128,256]{1,0:T(8,128)S(1)}, f32[128,256]{1,0:T(8,128)S(1)}, u32[]{:S(2)}, u32[]{:S(2)}) collective-permute-start(f32[128,256]{1,0:T(8,128)S(1)} %get-tuple-element.63.send1_ref), channel_id=1, source_target_pairs={{0,1},{1,0},{2,3},{3,2},{4,5},{5,4},{6,7},{7,6},{8,9},{9,8},{10,11... | collective-permute-start | bytes 393224 | tf_op jit(solution)/shard_map/ppermute | solution.py:697
  8.9 2.9 %shard_map.137 = (f32[2,64,32,128]{3,2,1,0:T(8,128)S(1)}, f32[8,256]{1,0:T(8,128)S(1)}, bf16[256,512]{1,0:T(8,128)(2,1)S(1)}, f32[1,512]{1,0:T(1,128)S(1)}, bf16...) custom-call(f32[2,64,32,128]{3,2,1,0:T(8,128)S(1)} %get-tuple-elemen, ...), custom_call_target="tpu_custom_call", output_to_operand_aliasing={{0}: (0, {}), {1}: (1, {}), {2}: (2, {}), {3}: (3, {}), {4}... | custom-call | flops 1073741824 | bytes 1048576 | tf_op jit(solution)/shard_map/pallas_call | solution.py:460
  11.8 0.8 %collective-permute-done.recv2_ref = f32[128,256]{1,0:T(8,128)S(1)} collective-permute-done((f32[128,256]{1,0:T(8,128)S(1)}, f32[128,256]{1,0:T(8,128)S(1)}, u32[]{:S(2)}, u32[]{:S(2)}) %collective-permute-start) | collective-permute-done | bytes 131104 | tf_op jit(solution)/shard_map/ppermute | solution.py:696
  12.7 0.0 collective-permute-done.1.recv1_ref
  12.7 2.3 %collective-permute-start.2 = (f32[72,256]{1,0:T(8,128)S(1)}, f32[72,256]{1,0:T(8,128)S(1)}, u32[]{:S(2)}, u32[]{:S(2)}) collective-permute-start(f32[72,256]{1,0:T(8,128)S(1)} %get-tuple-element.67), channel_id=1, source_target_pairs={{0,120},{1,121},{2,122},{3,123},{4,124},{5,125},{6,126},{7,127},{8... | collective-permute-start | bytes 221192 | tf_op jit(solution)/shard_map/ppermute | solution.py:702
  15.0 0.0 collective-permute-start.3
  15.0 3.3 %shard_map.138 = (f32[128,16]{1,0:T(8,128)S(1)}, f32[2,256,128]{2,1,0:T(8,128)S(1)}) custom-call(f32[2,64,32,128]{3,2,1,0:T(8,128)S(1)} %get-tuple-element.55.air_ref, f32[8,256]{1,0:T(8,128)S(1)} %get-tuple-element.56.coef_ref, bf16[256,512]{1,0:T(8,128)(2,1)S(1)} %get-tuple-element.57.w1_ref, f32[1,512]{1,0:T(1,128)S(1)} %get-tuple-element.58.bias_ref, ...), custom_call_target="tpu_custom_call" | custom-call | flops 1073741824 | bytes 1048576 | tf_op jit(solution)/shard_map/pallas_call | solution.py:520
  18.4 0.3 %collective-permute-done.2.cross_ref = f32[72,256]{1,0:T(8,128)S(1)} collective-permute-done((f32[72,256]{1,0:T(8,128)S(1)}, f32[72,256]{1,0:T(8,128)S(1)}, u32[]{:S(2)}, u32[]{:S(2)}) %collective-permute-start.2) | collective-permute-done | bytes 73760 | tf_op jit(solution)/shard_map/ppermute | solution.py:702
  18.7 0.0 collective-permute-done.3.pair_ref
  18.7 2.6 %shard_map.140 = f32[2,16,32]{2,1,0:T(8,128)} custom-call(f32[2,64,32,128]{3,2,1,0:T(8,128)S(1)} %get-tuple-element.55.air_ref, f32[8,256]{1,0:T(8,128)S(1)} %get-tuple-element.56.coef_ref, bf16[256,512]{1,0:T(8,128)(2,1)S(1)} %get-tuple-element.57.w1_ref, f32[1,512]{1,0:T(1,128)S(1)} %get-tuple-element.58.bias_ref, ...), custom_call_target="tpu_custom_call" | custom-call | flops 268435456 | bytes 1048576 | tf_op jit(solution)/shard_map/pallas_call | solution.py:633
  (1 shorter events, 0.0 us)
Async XLA Ops:
  6.1 6.5 %collective-permute-start = (f32[128,256]{1,0:T(8,128)S(1)}, f32[128,256]{1,0:T(8,128)S(1)}, u32[]{:S(2)}, u32[]{:S(2)}) collective-permute-start(f32[128,256]{1,0:T(8,128)S(1)} %get-tuple-element.62.send2_ref), channel_id=1, source_target_pairs={{0,7},{1,2},{2,1},{3,4},{4,3},{5,6},{6,5},{7,0},{8,15},{9,10},{10,... | collective-permute-start | bytes 393224 | tf_op jit(solution)/shard_map/ppermute | solution.py:696
  7.6 5.1 %collective-permute-start.1 = (f32[128,256]{1,0:T(8,128)S(1)}, f32[128,256]{1,0:T(8,128)S(1)}, u32[]{:S(2)}, u32[]{:S(2)}) collective-permute-start(f32[128,256]{1,0:T(8,128)S(1)} %get-tuple-element.63.send1_ref), channel_id=1, source_target_pairs={{0,1},{1,0},{2,3},{3,2},{4,5},{5,4},{6,7},{7,6},{8,9},{9,8},{10,11... | collective-permute-start | bytes 393224 | tf_op jit(solution)/shard_map/ppermute | solution.py:697
  12.7 6.0 %collective-permute-start.2 = (f32[72,256]{1,0:T(8,128)S(1)}, f32[72,256]{1,0:T(8,128)S(1)}, u32[]{:S(2)}, u32[]{:S(2)}) collective-permute-start(f32[72,256]{1,0:T(8,128)S(1)} %get-tuple-element.67), channel_id=1, source_target_pairs={{0,120},{1,121},{2,122},{3,123},{4,124},{5,125},{6,126},{7,127},{8... | collective-permute-start | bytes 221192 | tf_op jit(solution)/shard_map/ppermute | solution.py:702
  15.0 3.7 %collective-permute-start.3 = (f32[72,256]{1,0:T(8,128)S(1)}, f32[72,256]{1,0:T(8,128)S(1)}, u32[]{:S(2)}, u32[]{:S(2)}) collective-permute-start(f32[72,256]{1,0:T(8,128)S(1)} %get-tuple-element.68), channel_id=1, source_target_pairs={{0,8},{1,9},{2,10},{3,11},{4,12},{5,13},{6,14},{7,15},{8,0},{9,1},... | collective-permute-start | bytes 221192 | tf_op jit(solution)/shard_map/ppermute | solution.py:703

commit v5 on v4

--- a/solution.py
+++ b/solution.py
@@ -170,18 +170,23 @@
     return scatter_columns(kept, cells)
 
 
-def tiles(lo, hi, air_ref, coef_ref, matrix_refs, cell_ref, count_ref, acc_ref):
+def add_tile(tile, refs):
+    air_ref, coef_ref, matrix_refs, cell_ref, count_ref, acc_ref = refs
+    state = tile_state(air_ref, coef_ref, tile)
+    groups = [tile * GROUPS + g for g in range(GROUPS)]
+    matrices = matrices_of(*matrix_refs)
+    acc_ref[...] += finish(state, groups, matrices, cell_ref, count_ref, TILE_CHUNKS)
+
+
+def tiles(lo, hi, *refs):
     @pl.loop(lo, hi)
     def _(tile):
-        state = tile_state(air_ref, coef_ref, tile)
-        groups = [tile * GROUPS + g for g in range(GROUPS)]
-        matrices = matrices_of(*matrix_refs)
-        acc_ref[...] += finish(state, groups, matrices, cell_ref, count_ref, TILE_CHUNKS)
+        add_tile(tile, refs)
 
 
 def early_tiles():
     gy = lax.axis_index("gy")
-    return jnp.where(gy < 3, 1, 0).astype(jnp.int32)
+    return jnp.where(gy < 2, 1, 0).astype(jnp.int32)
 
 
 def loads_all():
@@ -198,7 +203,7 @@
 
 def side_turn():
     gy = lax.axis_index("gy")
-    return jnp.where((gy == 0) | (gy == 3), 0, 1)
+    return jnp.where((gy < 4) & (gy != 1), 0, 1)
 
 
 class Copies:
@@ -221,7 +226,7 @@
             self.fetch(
                 lambda half=half: (
                     air_in.at[:, pl.ds(lo, size), lanes_of(half)],
-                    air_ref.at[half, :, pl.ds(lo, size), :],
+                    air_ref.at[half, pl.ds(0, 64), pl.ds(lo, size), :],
                 )
             )
 
@@ -292,25 +297,33 @@
     upper = jnp.where(is_even("gy"), 30, 0)
     for send, first in ((send1_ref, upper), (send2_ref, 30 - upper)):
         for half in range(2):
-            flat = air_ref.at[half].reshape(64 * 32, LANES)
+            flat = air_ref.at[half].reshape(65 * 32, LANES)
             for k in range(2):
                 send[pl.ds(k * 64, 64), lanes_of(half)] = flat[pl.ds(first + k, 64, stride=32), :]
 
     others.wait()
 
-    @pl.when(ours)
-    def _():
-        side_parts(idx_ref, side_refs, side_ref)
-
     @pl.when(early)
     def _():
         layers.wait()
         prepare_layers(raw, coef_ref, w1_ref, bias_ref, w2_ref, last_ref)
-        matrix_refs = (w1_ref, bias_ref, w2_ref, last_ref)
-        tiles(
-            jnp.int32(0), early_tiles(), air_ref, coef_ref, matrix_refs, cell_ref, count_ref,
-            acc_ref,
-        )
+
+    matrix_refs = (w1_ref, bias_ref, w2_ref, last_ref)
+    tile_refs = (air_ref, coef_ref, matrix_refs, cell_ref, count_ref, acc_ref)
+    some = early_tiles() > 0
+
+    @pl.when(ours & jnp.logical_not(some))
+    def _():
+        side_parts(idx_ref, side_refs, side_ref)
+
+    @pl.when(ours & some)
+    def _():
+        side_parts(idx_ref, side_refs, side_ref)
+        add_tile(jnp.int32(0), tile_refs)
+
+    @pl.when(jnp.logical_not(ours) & some)
+    def _():
+        add_tile(jnp.int32(0), tile_refs)
 
 
 VMEM = pl.BlockSpec(memory_space=pltpu.VMEM)
@@ -337,7 +350,7 @@
     pltpu.VMEM((256, 512), BF16),
 ]
 CORE = [
-    ((2, 64, 32, LANES), F32),
+    ((2, 65, 32, LANES), F32),
     ((8, 256), F32),
     ((256, 512), BF16),
     ((1, 512), F32),
@@ -438,9 +451,15 @@
         fetch_layers(layers, (spread_in, east_in, north_in, w1_in, bias_in, w2_in), raw, w2_ref)
         layers.rows(air_in, air_ref, 8, 16)
 
-    @pl.when(side_turn() == 1)
-    def _():
-        side_refs = (land_ref, water_ref, ocean_ref, driver_ref, mixing_ref)
+    ours = side_turn() == 1
+    side_refs = (land_ref, water_ref, ocean_ref, driver_ref, mixing_ref)
+    matrix_refs = (w1_ref, bias_ref, w2_ref, last_ref)
+    tile_refs = (air_ref, coef_ref, matrix_refs, cell_ref, count_ref, acc_ref)
+    acc_ref[...] = jnp.zeros_like(acc_ref)
+    both = ours & loads_all()
+
+    @pl.when(ours & jnp.logical_not(both))
+    def _():
         side_parts(idx_ref, side_refs, side_ref)
 
     @pl.when(jnp.logical_not(loads_all()))
@@ -448,11 +467,12 @@
         layers.wait()
         prepare_layers(raw, coef_ref, w1_ref, bias_ref, w2_ref, last_ref)
 
-    acc_ref[...] = jnp.zeros_like(acc_ref)
-    matrix_refs = (w1_ref, bias_ref, w2_ref, last_ref)
-    tiles(
-        early, early + middle_tiles(), air_ref, coef_ref, matrix_refs, cell_ref, count_ref, acc_ref
-    )
+    @pl.when(both)
+    def _():
+        side_parts(idx_ref, side_refs, side_ref)
+        add_tile(early, tile_refs)
+
+    tiles(early + both.astype(jnp.int32), early + middle_tiles(), *tile_refs)
 
 
 def middle(core, sides, sources):
@@ -531,7 +551,7 @@
 
 
 def y_edge_state(half, air_ref, coefs, ylow, yhigh, first, last):
-    flat = air_ref.at[half].reshape(64 * 32, LANES)
+    flat = air_ref.at[half].reshape(65 * 32, LANES)
 
     def step(block):
         centre = block[1:-1]

time: 21.5 us -> 21.4 us (level)
  waiting for transfers between devices: 1.17 us -> 2.59 us
  starting transfers between devices: 5.07 us -> 4.27 us
  Pallas kernels: 15 us -> 14.3 us
    ppermute x1, starting transfers between devices: 1.29 us -> 0.01 us  [shards(): recv1 = lax.ppermute(send1, AXES, exchanges('gy', 0))]
    ppermute x1, starting transfers between devices: 1.48 us -> 2.23 us  [shards(): recv2 = lax.ppermute(send2, AXES, exchanges('gy', 1))]
    pallas_call x1, Pallas kernels: 6.13 us -> 5.39 us  [load(): pl.pallas_call(load_kernel, out_shape=shapes_of(shapes), in_specs=[pl.Blo...]
    ppermute x1, waiting for transfers between devices: 0.01 us -> 0.66 us  [shards(): recv1 = lax.ppermute(send1, AXES, exchanges('gy', 0))]
    ppermute x1, waiting for transfers between devices: 0.33 us -> 0.76 us  [shards(): cross = lax.ppermute(send_cross, AXES, exchanges('gx', 1))]
    ppermute x1, waiting for transfers between devices: 0.83 us -> 1.17 us  [shards(): recv2 = lax.ppermute(send2, AXES, exchanges('gy', 1))]
    ppermute x1, starting transfers between devices: 2.3 us -> 2.04 us  [shards(): cross = lax.ppermute(send_cross, AXES, exchanges('gx', 1))]
  transfers between devices with their start and end apart: 4 -> 4, of which waited for: 2 -> 3; matrix products, arithmetic and copies ran while one was open for 0% -> 0% of each run, Pallas kernels for 29% -> 30%
where the time goes in v5:
time: 21.4 us; the launch traced here: 21.2 us
  Pallas kernels  14.3 us (67%)
  starting transfers between devices  4.27 us (20%)
  waiting for transfers between devices  2.59 us (12%)
    pallas_call x1, Pallas kernels, load(): pl.pallas_call(load_kernel, out_shape=shapes_of(shapes), in_specs=[pl.Blo...  5.39 us
    pallas_call x1, Pallas kernels, late(): pl.pallas_call(late_kernel, out_shape=[jax.ShapeDtypeStruct((LANES, 16),...  3.16 us
    pallas_call x1, Pallas kernels, middle(): pl.pallas_call(middle_kernel, out_shape=shapes_of(shapes), in_specs=[VMEM...  3.12 us
    pallas_call x1, Pallas kernels, edges(): pl.pallas_call(edge_kernel, out_shape=jax.ShapeDtypeStruct((2, 16, 32), F...  2.6 us
    ppermute x1, starting transfers between devices, shards(): recv2 = lax.ppermute(send2, AXES, exchanges('gy', 1))  2.23 us
    ppermute x1, starting transfers between devices, shards(): cross = lax.ppermute(send_cross, AXES, exchanges('gx', 1))  2.04 us
    ppermute x1, waiting for transfers between devices, shards(): recv2 = lax.ppermute(send2, AXES, exchanges('gy', 1))  1.17 us
    ppermute x1, waiting for transfers between devices, shards(): cross = lax.ppermute(send_cross, AXES, exchanges('gx', 1))  0.76 us
  transfers between devices with their start and end apart: 4, of which 3 were waited for; matrix products, arithmetic and copies ran while one was open for 0% of the time, Pallas kernels for 30%

profile of v5, /device:TPU:4, one launch (start us, length us, event | category | flops | bytes accessed | tf_op | source)
XLA Modules:
  0.0 21.2 jit_solution(3750119058369441831)
XLA Ops:
  0.0 5.4 %shard_map.136 = (f32[128,256]{1,0:T(8,128)S(1)}, f32[128,256]{1,0:T(8,128)S(1)}, f32[2,65,32,128]{3,2,1,0:T(8,128)S(1)}, f32[8,256]{1,0:T(8,128)S(1)}, bf16[256...) custom-call(f32[64,32,256]{2,1,0:T(8,128)} %air_in.3, ...), custom_call_target="tpu_custom_call" | custom-call | flops 1048576 | bytes 1048576 | tf_op jit(solution)/shard_map/pallas_call | solution.py:375
  5.4 2.2 %collective-permute-start = (f32[128,256]{1,0:T(8,128)S(1)}, f32[128,256]{1,0:T(8,128)S(1)}, u32[]{:S(2)}, u32[]{:S(2)}) collective-permute-start(f32[128,256]{1,0:T(8,128)S(1)} %get-tuple-element.62.send2_ref), channel_id=1, source_target_pairs={{0,7},{1,2},{2,1},{3,4},{4,3},{5,6},{6,5},{7,0},{8,15},{9,10},{10,... | collective-permute-start | bytes 393224 | tf_op jit(solution)/shard_map/ppermute | solution.py:716
  7.6 0.0 collective-permute-start.1
  7.6 3.1 %shard_map.137 = (f32[2,65,32,128]{3,2,1,0:T(8,128)S(1)}, f32[8,256]{1,0:T(8,128)S(1)}, bf16[256,512]{1,0:T(8,128)(2,1)S(1)}, f32[1,512]{1,0:T(1,128)S(1)}, bf16...) custom-call(f32[2,65,32,128]{3,2,1,0:T(8,128)S(1)} %get-tuple-elemen, ...), custom_call_target="tpu_custom_call", output_to_operand_aliasing={{0}: (0, {}), {1}: (1, {}), {2}: (2, {}), {3}: (3, {}), {4}... | custom-call | flops 1073741824 | bytes 1048576 | tf_op jit(solution)/shard_map/pallas_call | solution.py:480
  10.8 1.2 %collective-permute-done.recv2_ref = f32[128,256]{1,0:T(8,128)S(1)} collective-permute-done((f32[128,256]{1,0:T(8,128)S(1)}, f32[128,256]{1,0:T(8,128)S(1)}, u32[]{:S(2)}, u32[]{:S(2)}) %collective-permute-start) | collective-permute-done | bytes 131104 | tf_op jit(solution)/shard_map/ppermute | solution.py:716
  11.9 0.7 %collective-permute-done.1.recv1_ref = f32[128,256]{1,0:T(8,128)S(1)} collective-permute-done((f32[128,256]{1,0:T(8,128)S(1)}, f32[128,256]{1,0:T(8,128)S(1)}, u32[]{:S(2)}, u32[]{:S(2)}) %collective-permute-start.1) | collective-permute-done | bytes 131104 | tf_op jit(solution)/shard_map/ppermute | solution.py:717
  12.6 2.0 %collective-permute-start.2 = (f32[72,256]{1,0:T(8,128)S(1)}, f32[72,256]{1,0:T(8,128)S(1)}, u32[]{:S(2)}, u32[]{:S(2)}) collective-permute-start(f32[72,256]{1,0:T(8,128)S(1)} %get-tuple-element.67), channel_id=1, source_target_pairs={{0,120},{1,121},{2,122},{3,123},{4,124},{5,125},{6,126},{7,127},{8... | collective-permute-start | bytes 221192 | tf_op jit(solution)/shard_map/ppermute | solution.py:722
  14.7 0.0 collective-permute-start.3
  14.7 3.2 %shard_map.138 = (f32[128,16]{1,0:T(8,128)S(1)}, f32[2,256,128]{2,1,0:T(8,128)S(1)}) custom-call(f32[2,65,32,128]{3,2,1,0:T(8,128)S(1)} %get-tuple-element.55.air_ref, f32[8,256]{1,0:T(8,128)S(1)} %get-tuple-element.56.coef_ref, bf16[256,512]{1,0:T(8,128)(2,1)S(1)} %get-tuple-element.57.w1_ref, f32[1,512]{1,0:T(1,128)S(1)} %get-tuple-element.58.bias_ref, ...), custom_call_target="tpu_custom_call" | custom-call | flops 1073741824 | bytes 1048576 | tf_op jit(solution)/shard_map/pallas_call | solution.py:540
  17.8 0.8 %collective-permute-done.2.cross_ref = f32[72,256]{1,0:T(8,128)S(1)} collective-permute-done((f32[72,256]{1,0:T(8,128)S(1)}, f32[72,256]{1,0:T(8,128)S(1)}, u32[]{:S(2)}, u32[]{:S(2)}) %collective-permute-start.2) | collective-permute-done | bytes 73760 | tf_op jit(solution)/shard_map/ppermute | solution.py:722
  18.6 0.0 collective-permute-done.3.pair_ref
  18.6 2.6 %shard_map.140 = f32[2,16,32]{2,1,0:T(8,128)} custom-call(f32[2,65,32,128]{3,2,1,0:T(8,128)S(1)} %get-tuple-element.55.air_ref, f32[8,256]{1,0:T(8,128)S(1)} %get-tuple-element.56.coef_ref, bf16[256,512]{1,0:T(8,128)(2,1)S(1)} %get-tuple-element.57.w1_ref, f32[1,512]{1,0:T(1,128)S(1)} %get-tuple-element.58.bias_ref, ...), custom_call_target="tpu_custom_call" | custom-call | flops 268435456 | bytes 1048576 | tf_op jit(solution)/shard_map/pallas_call | solution.py:653
  (1 shorter events, 0.0 us)
Async XLA Ops:
  5.4 6.5 %collective-permute-start = (f32[128,256]{1,0:T(8,128)S(1)}, f32[128,256]{1,0:T(8,128)S(1)}, u32[]{:S(2)}, u32[]{:S(2)}) collective-permute-start(f32[128,256]{1,0:T(8,128)S(1)} %get-tuple-element.62.send2_ref), channel_id=1, source_target_pairs={{0,7},{1,2},{2,1},{3,4},{4,3},{5,6},{6,5},{7,0},{8,15},{9,10},{10,... | collective-permute-start | bytes 393224 | tf_op jit(solution)/shard_map/ppermute | solution.py:716
  7.6 5.0 %collective-permute-start.1 = (f32[128,256]{1,0:T(8,128)S(1)}, f32[128,256]{1,0:T(8,128)S(1)}, u32[]{:S(2)}, u32[]{:S(2)}) collective-permute-start(f32[128,256]{1,0:T(8,128)S(1)} %get-tuple-element.63.send1_ref), channel_id=1, source_target_pairs={{0,1},{1,0},{2,3},{3,2},{4,5},{5,4},{6,7},{7,6},{8,9},{9,8},{10,11... | collective-permute-start | bytes 393224 | tf_op jit(solution)/shard_map/ppermute | solution.py:717
  12.6 6.0 %collective-permute-start.2 = (f32[72,256]{1,0:T(8,128)S(1)}, f32[72,256]{1,0:T(8,128)S(1)}, u32[]{:S(2)}, u32[]{:S(2)}) collective-permute-start(f32[72,256]{1,0:T(8,128)S(1)} %get-tuple-element.67), channel_id=1, source_target_pairs={{0,120},{1,121},{2,122},{3,123},{4,124},{5,125},{6,126},{7,127},{8... | collective-permute-start | bytes 221192 | tf_op jit(solution)/shard_map/ppermute | solution.py:722
  14.7 3.9 %collective-permute-start.3 = (f32[72,256]{1,0:T(8,128)S(1)}, f32[72,256]{1,0:T(8,128)S(1)}, u32[]{:S(2)}, u32[]{:S(2)}) collective-permute-start(f32[72,256]{1,0:T(8,128)S(1)} %get-tuple-element.68), channel_id=1, source_target_pairs={{0,8},{1,9},{2,10},{3,11},{4,12},{5,13},{6,14},{7,15},{8,0},{9,1},... | collective-permute-start | bytes 221192 | tf_op jit(solution)/shard_map/ppermute | solution.py:723

commit v6 on v5

--- a/solution.py
+++ b/solution.py
@@ -194,7 +194,9 @@
 
 
 def middle_tiles():
-    return jnp.where(lax.axis_index("gx") % 8 == 1, 2, 1).astype(jnp.int32)
+    place = lax.axis_index("gx") % 8
+    waiting = (place == 1) | ((place == 3) & (lax.axis_index("gy") >= 2))
+    return jnp.where(waiting, 2, 1).astype(jnp.int32)
 
 
 def is_even(axis):

time: 21.4 us -> 21.4 us (level)
  no operation moved by 1% of the time
where the time goes in v6:
time: 21.4 us; the launch traced here: 21.2 us
  Pallas kernels  14.3 us (67%)
  starting transfers between devices  4.27 us (20%)
  waiting for transfers between devices  2.59 us (12%)
    pallas_call x1, Pallas kernels, load(): pl.pallas_call(load_kernel, out_shape=shapes_of(shapes), in_specs=[pl.Blo...  5.39 us
    pallas_call x1, Pallas kernels, late(): pl.pallas_call(late_kernel, out_shape=[jax.ShapeDtypeStruct((LANES, 16),...  3.16 us
    pallas_call x1, Pallas kernels, middle(): pl.pallas_call(middle_kernel, out_shape=shapes_of(shapes), in_specs=[VMEM...  3.13 us
    pallas_call x1, Pallas kernels, edges(): pl.pallas_call(edge_kernel, out_shape=jax.ShapeDtypeStruct((2, 16, 32), F...  2.6 us
    ppermute x1, starting transfers between devices, shards(): recv2 = lax.ppermute(send2, AXES, exchanges('gy', 1))  2.23 us
    ppermute x1, starting transfers between devices, shards(): cross = lax.ppermute(send_cross, AXES, exchanges('gx', 1))  2.04 us
    ppermute x1, waiting for transfers between devices, shards(): recv2 = lax.ppermute(send2, AXES, exchanges('gy', 1))  1.17 us
    ppermute x1, waiting for transfers between devices, shards(): cross = lax.ppermute(send_cross, AXES, exchanges('gx', 1))  0.76 us
  transfers between devices with their start and end apart: 4, of which 3 were waited for; matrix products, arithmetic and copies ran while one was open for 0% of the time, Pallas kernels for 30%

profile of v6, /device:TPU:4, one launch (start us, length us, event | category | flops | bytes accessed | tf_op | source)
XLA Modules:
  0.0 21.2 jit_solution(404712242650684768)
XLA Ops:
  0.0 5.4 %shard_map.136 = (f32[128,256]{1,0:T(8,128)S(1)}, f32[128,256]{1,0:T(8,128)S(1)}, f32[2,65,32,128]{3,2,1,0:T(8,128)S(1)}, f32[8,256]{1,0:T(8,128)S(1)}, bf16[256...) custom-call(f32[64,32,256]{2,1,0:T(8,128)} %air_in.3, ...), custom_call_target="tpu_custom_call" | custom-call | flops 1048576 | bytes 1048576 | tf_op jit(solution)/shard_map/pallas_call | solution.py:377
  5.4 2.2 %collective-permute-start = (f32[128,256]{1,0:T(8,128)S(1)}, f32[128,256]{1,0:T(8,128)S(1)}, u32[]{:S(2)}, u32[]{:S(2)}) collective-permute-start(f32[128,256]{1,0:T(8,128)S(1)} %get-tuple-element.62.send2_ref), channel_id=1, source_target_pairs={{0,7},{1,2},{2,1},{3,4},{4,3},{5,6},{6,5},{7,0},{8,15},{9,10},{10,... | collective-permute-start | bytes 393224 | tf_op jit(solution)/shard_map/ppermute | solution.py:718
  7.6 0.0 collective-permute-start.1
  7.6 3.1 %shard_map.137 = (f32[2,65,32,128]{3,2,1,0:T(8,128)S(1)}, f32[8,256]{1,0:T(8,128)S(1)}, bf16[256,512]{1,0:T(8,128)(2,1)S(1)}, f32[1,512]{1,0:T(1,128)S(1)}, bf16...) custom-call(f32[2,65,32,128]{3,2,1,0:T(8,128)S(1)} %get-tuple-elemen, ...), custom_call_target="tpu_custom_call", output_to_operand_aliasing={{0}: (0, {}), {1}: (1, {}), {2}: (2, {}), {3}: (3, {}), {4}... | custom-call | flops 1073741824 | bytes 1048576 | tf_op jit(solution)/shard_map/pallas_call | solution.py:482
  10.8 1.2 %collective-permute-done.recv2_ref = f32[128,256]{1,0:T(8,128)S(1)} collective-permute-done((f32[128,256]{1,0:T(8,128)S(1)}, f32[128,256]{1,0:T(8,128)S(1)}, u32[]{:S(2)}, u32[]{:S(2)}) %collective-permute-start) | collective-permute-done | bytes 131104 | tf_op jit(solution)/shard_map/ppermute | solution.py:718
  11.9 0.7 %collective-permute-done.1.recv1_ref = f32[128,256]{1,0:T(8,128)S(1)} collective-permute-done((f32[128,256]{1,0:T(8,128)S(1)}, f32[128,256]{1,0:T(8,128)S(1)}, u32[]{:S(2)}, u32[]{:S(2)}) %collective-permute-start.1) | collective-permute-done | bytes 131104 | tf_op jit(solution)/shard_map/ppermute | solution.py:719
  12.6 2.0 %collective-permute-start.2 = (f32[72,256]{1,0:T(8,128)S(1)}, f32[72,256]{1,0:T(8,128)S(1)}, u32[]{:S(2)}, u32[]{:S(2)}) collective-permute-start(f32[72,256]{1,0:T(8,128)S(1)} %get-tuple-element.67), channel_id=1, source_target_pairs={{0,120},{1,121},{2,122},{3,123},{4,124},{5,125},{6,126},{7,127},{8... | collective-permute-start | bytes 221192 | tf_op jit(solution)/shard_map/ppermute | solution.py:724
  14.7 0.0 collective-permute-start.3
  14.7 3.2 %shard_map.138 = (f32[128,16]{1,0:T(8,128)S(1)}, f32[2,256,128]{2,1,0:T(8,128)S(1)}) custom-call(f32[2,65,32,128]{3,2,1,0:T(8,128)S(1)} %get-tuple-element.55.air_ref, f32[8,256]{1,0:T(8,128)S(1)} %get-tuple-element.56.coef_ref, bf16[256,512]{1,0:T(8,128)(2,1)S(1)} %get-tuple-element.57.w1_ref, f32[1,512]{1,0:T(1,128)S(1)} %get-tuple-element.58.bias_ref, ...), custom_call_target="tpu_custom_call" | custom-call | flops 1073741824 | bytes 1048576 | tf_op jit(solution)/shard_map/pallas_call | solution.py:542
  17.8 0.8 %collective-permute-done.2.cross_ref = f32[72,256]{1,0:T(8,128)S(1)} collective-permute-done((f32[72,256]{1,0:T(8,128)S(1)}, f32[72,256]{1,0:T(8,128)S(1)}, u32[]{:S(2)}, u32[]{:S(2)}) %collective-permute-start.2) | collective-permute-done | bytes 73760 | tf_op jit(solution)/shard_map/ppermute | solution.py:724
  18.6 0.0 collective-permute-done.3.pair_ref
  18.6 2.6 %shard_map.140 = f32[2,16,32]{2,1,0:T(8,128)} custom-call(f32[2,65,32,128]{3,2,1,0:T(8,128)S(1)} %get-tuple-element.55.air_ref, f32[8,256]{1,0:T(8,128)S(1)} %get-tuple-element.56.coef_ref, bf16[256,512]{1,0:T(8,128)(2,1)S(1)} %get-tuple-element.57.w1_ref, f32[1,512]{1,0:T(1,128)S(1)} %get-tuple-element.58.bias_ref, ...), custom_call_target="tpu_custom_call" | custom-call | flops 268435456 | bytes 1048576 | tf_op jit(solution)/shard_map/pallas_call | solution.py:655
  (1 shorter events, 0.0 us)
Async XLA Ops:
  5.4 6.5 %collective-permute-start = (f32[128,256]{1,0:T(8,128)S(1)}, f32[128,256]{1,0:T(8,128)S(1)}, u32[]{:S(2)}, u32[]{:S(2)}) collective-permute-start(f32[128,256]{1,0:T(8,128)S(1)} %get-tuple-element.62.send2_ref), channel_id=1, source_target_pairs={{0,7},{1,2},{2,1},{3,4},{4,3},{5,6},{6,5},{7,0},{8,15},{9,10},{10,... | collective-permute-start | bytes 393224 | tf_op jit(solution)/shard_map/ppermute | solution.py:718
  7.6 5.0 %collective-permute-start.1 = (f32[128,256]{1,0:T(8,128)S(1)}, f32[128,256]{1,0:T(8,128)S(1)}, u32[]{:S(2)}, u32[]{:S(2)}) collective-permute-start(f32[128,256]{1,0:T(8,128)S(1)} %get-tuple-element.63.send1_ref), channel_id=1, source_target_pairs={{0,1},{1,0},{2,3},{3,2},{4,5},{5,4},{6,7},{7,6},{8,9},{9,8},{10,11... | collective-permute-start | bytes 393224 | tf_op jit(solution)/shard_map/ppermute | solution.py:719
  12.6 6.0 %collective-permute-start.2 = (f32[72,256]{1,0:T(8,128)S(1)}, f32[72,256]{1,0:T(8,128)S(1)}, u32[]{:S(2)}, u32[]{:S(2)}) collective-permute-start(f32[72,256]{1,0:T(8,128)S(1)} %get-tuple-element.67), channel_id=1, source_target_pairs={{0,120},{1,121},{2,122},{3,123},{4,124},{5,125},{6,126},{7,127},{8... | collective-permute-start | bytes 221192 | tf_op jit(solution)/shard_map/ppermute | solution.py:724
  14.7 3.9 %collective-permute-start.3 = (f32[72,256]{1,0:T(8,128)S(1)}, f32[72,256]{1,0:T(8,128)S(1)}, u32[]{:S(2)}, u32[]{:S(2)}) collective-permute-start(f32[72,256]{1,0:T(8,128)S(1)} %get-tuple-element.68), channel_id=1, source_target_pairs={{0,8},{1,9},{2,10},{3,11},{4,12},{5,13},{6,14},{7,15},{8,0},{9,1},... | collective-permute-start | bytes 221192 | tf_op jit(solution)/shard_map/ppermute | solution.py:725

commit v7 on v6

--- a/solution.py
+++ b/solution.py
@@ -295,13 +295,23 @@
     acc_ref[...] = jnp.zeros_like(acc_ref)
     columns.wait()
     group_rows(idx_ref, inc_ref, turned, cell_ref, count_ref)
-    slabs.wait()
-    upper = jnp.where(is_even("gy"), 30, 0)
-    for send, first in ((send1_ref, upper), (send2_ref, 30 - upper)):
-        for half in range(2):
-            flat = air_ref.at[half].reshape(65 * 32, LANES)
-            for k in range(2):
-                send[pl.ds(k * 64, 64), lanes_of(half)] = flat[pl.ds(first + k, 64, stride=32), :]
+
+    def extract(low_send, high_send):
+        for place, (send, first) in enumerate(((low_send, 0), (high_send, 30))):
+            for half in range(2):
+                slabs.copy(2 * place + half).wait()
+                flat = air_ref.at[half].reshape(65 * 32, LANES)
+                for k in range(2):
+                    rows = flat[pl.ds(first + k, 64, stride=32), :]
+                    send[pl.ds(k * 64, 64), lanes_of(half)] = rows
+
+    @pl.when(is_even("gy"))
+    def _():
+        extract(send2_ref, send1_ref)
+
+    @pl.when(jnp.logical_not(is_even("gy")))
+    def _():
+        extract(send1_ref, send2_ref)
 
     others.wait()
 

time: 21.4 us -> 21.3 us (level)
  no operation moved by 1% of the time
where the time goes in v7:
time: 21.3 us; the launch traced here: 21.2 us
  Pallas kernels  14.3 us (67%)
  starting transfers between devices  4.25 us (20%)
  waiting for transfers between devices  2.59 us (12%)
    pallas_call x1, Pallas kernels, load(): pl.pallas_call(load_kernel, out_shape=shapes_of(shapes), in_specs=[pl.Blo...  5.39 us
    pallas_call x1, Pallas kernels, late(): pl.pallas_call(late_kernel, out_shape=[jax.ShapeDtypeStruct((LANES, 16),...  3.16 us
    pallas_call x1, Pallas kernels, middle(): pl.pallas_call(middle_kernel, out_shape=shapes_of(shapes), in_specs=[VMEM...  3.13 us
    pallas_call x1, Pallas kernels, edges(): pl.pallas_call(edge_kernel, out_shape=jax.ShapeDtypeStruct((2, 16, 32), F...  2.6 us
    ppermute x1, starting transfers between devices, shards(): recv2 = lax.ppermute(send2, AXES, exchanges('gy', 1))  2.2 us
    ppermute x1, starting transfers between devices, shards(): cross = lax.ppermute(send_cross, AXES, exchanges('gx', 1))  2.04 us
    ppermute x1, waiting for transfers between devices, shards(): recv2 = lax.ppermute(send2, AXES, exchanges('gy', 1))  1.19 us
    ppermute x1, waiting for transfers between devices, shards(): cross = lax.ppermute(send_cross, AXES, exchanges('gx', 1))  0.76 us
  transfers between devices with their start and end apart: 4, of which 3 were waited for; matrix products, arithmetic and copies ran while one was open for 0% of the time, Pallas kernels for 30%

profile of v7, /device:TPU:4, one launch (start us, length us, event | category | flops | bytes accessed | tf_op | source)
XLA Modules:
  0.0 21.2 jit_solution(2591726134783785194)
XLA Ops:
  0.0 5.4 %shard_map.136 = (f32[128,256]{1,0:T(8,128)S(1)}, f32[128,256]{1,0:T(8,128)S(1)}, f32[2,65,32,128]{3,2,1,0:T(8,128)S(1)}, f32[8,256]{1,0:T(8,128)S(1)}, bf16[256...) custom-call(f32[64,32,256]{2,1,0:T(8,128)} %air_in.3, ...), custom_call_target="tpu_custom_call" | custom-call | flops 1048576 | bytes 1048576 | tf_op jit(solution)/shard_map/pallas_call | solution.py:387
  5.4 2.2 %collective-permute-start = (f32[128,256]{1,0:T(8,128)S(1)}, f32[128,256]{1,0:T(8,128)S(1)}, u32[]{:S(2)}, u32[]{:S(2)}) collective-permute-start(f32[128,256]{1,0:T(8,128)S(1)} %get-tuple-element.62.send2_ref), channel_id=1, source_target_pairs={{0,7},{1,2},{2,1},{3,4},{4,3},{5,6},{6,5},{7,0},{8,15},{9,10},{10,... | collective-permute-start | bytes 393224 | tf_op jit(solution)/shard_map/ppermute | solution.py:728
  7.6 0.0 collective-permute-start.1
  7.6 3.1 %shard_map.137 = (f32[2,65,32,128]{3,2,1,0:T(8,128)S(1)}, f32[8,256]{1,0:T(8,128)S(1)}, bf16[256,512]{1,0:T(8,128)(2,1)S(1)}, f32[1,512]{1,0:T(1,128)S(1)}, bf16...) custom-call(f32[2,65,32,128]{3,2,1,0:T(8,128)S(1)} %get-tuple-elemen, ...), custom_call_target="tpu_custom_call", output_to_operand_aliasing={{0}: (0, {}), {1}: (1, {}), {2}: (2, {}), {3}: (3, {}), {4}... | custom-call | flops 1073741824 | bytes 1048576 | tf_op jit(solution)/shard_map/pallas_call | solution.py:492
  10.7 1.2 %collective-permute-done.recv2_ref = f32[128,256]{1,0:T(8,128)S(1)} collective-permute-done((f32[128,256]{1,0:T(8,128)S(1)}, f32[128,256]{1,0:T(8,128)S(1)}, u32[]{:S(2)}, u32[]{:S(2)}) %collective-permute-start) | collective-permute-done | bytes 131104 | tf_op jit(solution)/shard_map/ppermute | solution.py:728
  11.9 0.6 %collective-permute-done.1.recv1_ref = f32[128,256]{1,0:T(8,128)S(1)} collective-permute-done((f32[128,256]{1,0:T(8,128)S(1)}, f32[128,256]{1,0:T(8,128)S(1)}, u32[]{:S(2)}, u32[]{:S(2)}) %collective-permute-start.1) | collective-permute-done | bytes 131104 | tf_op jit(solution)/shard_map/ppermute | solution.py:729
  12.6 2.0 %collective-permute-start.2 = (f32[72,256]{1,0:T(8,128)S(1)}, f32[72,256]{1,0:T(8,128)S(1)}, u32[]{:S(2)}, u32[]{:S(2)}) collective-permute-start(f32[72,256]{1,0:T(8,128)S(1)} %get-tuple-element.67), channel_id=1, source_target_pairs={{0,120},{1,121},{2,122},{3,123},{4,124},{5,125},{6,126},{7,127},{8... | collective-permute-start | bytes 221192 | tf_op jit(solution)/shard_map/ppermute | solution.py:734
  14.6 0.0 collective-permute-start.3
  14.7 3.2 %shard_map.138 = (f32[128,16]{1,0:T(8,128)S(1)}, f32[2,256,128]{2,1,0:T(8,128)S(1)}) custom-call(f32[2,65,32,128]{3,2,1,0:T(8,128)S(1)} %get-tuple-element.55.air_ref, f32[8,256]{1,0:T(8,128)S(1)} %get-tuple-element.56.coef_ref, bf16[256,512]{1,0:T(8,128)(2,1)S(1)} %get-tuple-element.57.w1_ref, f32[1,512]{1,0:T(1,128)S(1)} %get-tuple-element.58.bias_ref, ...), custom_call_target="tpu_custom_call" | custom-call | flops 1073741824 | bytes 1048576 | tf_op jit(solution)/shard_map/pallas_call | solution.py:552
  17.8 0.8 %collective-permute-done.2.cross_ref = f32[72,256]{1,0:T(8,128)S(1)} collective-permute-done((f32[72,256]{1,0:T(8,128)S(1)}, f32[72,256]{1,0:T(8,128)S(1)}, u32[]{:S(2)}, u32[]{:S(2)}) %collective-permute-start.2) | collective-permute-done | bytes 73760 | tf_op jit(solution)/shard_map/ppermute | solution.py:734
  18.6 0.0 collective-permute-done.3.pair_ref
  18.6 2.6 %shard_map.140 = f32[2,16,32]{2,1,0:T(8,128)} custom-call(f32[2,65,32,128]{3,2,1,0:T(8,128)S(1)} %get-tuple-element.55.air_ref, f32[8,256]{1,0:T(8,128)S(1)} %get-tuple-element.56.coef_ref, bf16[256,512]{1,0:T(8,128)(2,1)S(1)} %get-tuple-element.57.w1_ref, f32[1,512]{1,0:T(1,128)S(1)} %get-tuple-element.58.bias_ref, ...), custom_call_target="tpu_custom_call" | custom-call | flops 268435456 | bytes 1048576 | tf_op jit(solution)/shard_map/pallas_call | solution.py:665
  (1 shorter events, 0.0 us)
Async XLA Ops:
  5.4 6.5 %collective-permute-start = (f32[128,256]{1,0:T(8,128)S(1)}, f32[128,256]{1,0:T(8,128)S(1)}, u32[]{:S(2)}, u32[]{:S(2)}) collective-permute-start(f32[128,256]{1,0:T(8,128)S(1)} %get-tuple-element.62.send2_ref), channel_id=1, source_target_pairs={{0,7},{1,2},{2,1},{3,4},{4,3},{5,6},{6,5},{7,0},{8,15},{9,10},{10,... | collective-permute-start | bytes 393224 | tf_op jit(solution)/shard_map/ppermute | solution.py:728
  7.6 5.0 %collective-permute-start.1 = (f32[128,256]{1,0:T(8,128)S(1)}, f32[128,256]{1,0:T(8,128)S(1)}, u32[]{:S(2)}, u32[]{:S(2)}) collective-permute-start(f32[128,256]{1,0:T(8,128)S(1)} %get-tuple-element.63.send1_ref), channel_id=1, source_target_pairs={{0,1},{1,0},{2,3},{3,2},{4,5},{5,4},{6,7},{7,6},{8,9},{9,8},{10,11... | collective-permute-start | bytes 393224 | tf_op jit(solution)/shard_map/ppermute | solution.py:729
  12.6 6.0 %collective-permute-start.2 = (f32[72,256]{1,0:T(8,128)S(1)}, f32[72,256]{1,0:T(8,128)S(1)}, u32[]{:S(2)}, u32[]{:S(2)}) collective-permute-start(f32[72,256]{1,0:T(8,128)S(1)} %get-tuple-element.67), channel_id=1, source_target_pairs={{0,120},{1,121},{2,122},{3,123},{4,124},{5,125},{6,126},{7,127},{8... | collective-permute-start | bytes 221192 | tf_op jit(solution)/shard_map/ppermute | solution.py:734
  14.6 3.9 %collective-permute-start.3 = (f32[72,256]{1,0:T(8,128)S(1)}, f32[72,256]{1,0:T(8,128)S(1)}, u32[]{:S(2)}, u32[]{:S(2)}) collective-permute-start(f32[72,256]{1,0:T(8,128)S(1)} %get-tuple-element.68), channel_id=1, source_target_pairs={{0,8},{1,9},{2,10},{3,11},{4,12},{5,13},{6,14},{7,15},{8,0},{9,1},... | collective-permute-start | bytes 221192 | tf_op jit(solution)/shard_map/ppermute | solution.py:735
